TPU v7x, 32 devices: a whole 2x2x4 slice. The times are simulated.
32 devices in a mesh: space: 16 (over z, y, core), cuts: 2 (over x).
Axes of the slice: x: 2, y: 2, z: 4, core: 2. Of those that a mesh axis runs over, the one named last changes fastest.
Arguments:
- vectors: float32 [2, 2, 512, 4096], P('cuts', None, None, 'space'), may hold values from -1.25 to 1.25
- momenta: int32 [3, 3], replicated, may hold values from -3 to 3, as said below
- diagrams: int32 [64, 5], replicated, may hold values from 0 to 3, as said below
Outputs:
- meson: float32 [2, 1536, 1024], P('cuts', 'space')
- diagram_values: float32 [64, 2], replicated
Inputs may be any that keep to these rules, and one draw needn't show every extreme that they name: `momenta`: first component of each momentum is nonzero. `diagrams`: column 0 is a tile id below (2)**2, columns 1 and 2 are time slices, column 3 a phase, column 4 the owner index along cuts; no owner is named more than 32 times and one owner exactly 32 times.
All inputs are finite; a program needn't handle non-finite values.
Results may differ from a plain program's by a relative error of at most 0.0003.
Values sent between devices are 32-bit elements; how exact they have to be, the bound alone decides.
No kernel may reach another device: no remote copies, remote signals or barrier semaphores. Data moves between devices by JAX's collectives and lax.ppermute only.
A program may use at most 64 MiB of HBM per device.

v0:
```python
import math

import jax
import jax.numpy as jnp
from jax import lax
from jax.sharding import PartitionSpec as P

MODES = 512
TILE = 256
PHASES = 3
EXTENT = 96


full_turn = 2.0 * math.pi


def angles_for(moment_rows, site_ids):
    coord_x = site_ids % EXTENT
    coord_y = site_ids // EXTENT % EXTENT
    coord_z = site_ids // (EXTENT * EXTENT)
    dotted = (
        moment_rows[:, 0:1] * coord_x[None, :]
        + moment_rows[:, 1:2] * coord_y[None, :]
        + moment_rows[:, 2:3] * coord_z[None, :]
    )
    return jnp.mod(dotted, EXTENT).astype(jnp.float32) * (full_turn / EXTENT)


def phased_rows(real_vec, imag_vec, moment_rows, site_ids):
    angle = angles_for(moment_rows, site_ids)
    cosine = jnp.cos(angle)
    sine = jnp.sin(angle)
    left_real = real_vec * cosine + imag_vec * sine
    left_imag = real_vec * sine - imag_vec * cosine
    return jnp.concatenate([left_real, left_imag], axis=1)


def right_block(real_vec, imag_vec):
    upper = jnp.concatenate([real_vec, -imag_vec], axis=1)
    lower = jnp.concatenate([imag_vec, real_vec], axis=1)
    return jnp.concatenate([upper, lower], axis=0)


def contract(left, right):
    return lax.dot_general(
        left,
        right,
        (((1,), (1,)), ((), ())),
        precision=lax.Precision.HIGHEST,
        preferred_element_type=jnp.float32,
    )


def tile_columns(rows, column_start):
    real_cols = lax.dynamic_slice_in_dim(rows, column_start, TILE, 1)
    imag_cols = lax.dynamic_slice_in_dim(rows, column_start + MODES, TILE, 1)
    return (real_cols, imag_cols)


def tile_pair(first_real, first_imag, second_real, second_imag, mask):
    real_rows = jnp.sum(first_real * second_real + first_imag * second_imag, axis=1)
    imag_rows = jnp.sum(first_imag * second_real - first_real * second_imag, axis=1)
    return jnp.stack([jnp.sum(mask * real_rows), jnp.sum(mask * imag_rows)]) / TILE


def per_device(vectors, momenta, diagrams):
    real_vec = vectors[0, 0]
    imag_vec = vectors[0, 1]
    sites_dev = real_vec.shape[1]
    site_ids = lax.axis_index("space") * sites_dev + jnp.arange(sites_dev, dtype=jnp.int32)
    right = right_block(real_vec, imag_vec)
    own_rows = PHASES * MODES // lax.axis_size("space")
    row_ids = jnp.arange(lax.axis_size("space") * own_rows, dtype=jnp.int32)
    mode_ids = row_ids % MODES
    phase_ids = row_ids // MODES
    field_rows = lax.psum_scatter(
        contract(
            phased_rows(
                jnp.take(real_vec, mode_ids, axis=0),
                jnp.take(imag_vec, mode_ids, axis=0),
                jnp.take(momenta, phase_ids, axis=0),
                site_ids,
            ),
            right,
        ),
        "space",
        scatter_dimension=0,
        tiled=True,
    )
    global_rows = lax.axis_index("space") * own_rows + jnp.arange(own_rows, dtype=jnp.int32)
    tiles_per = MODES // TILE

    def row_mask(entry):
        row_start = entry[3] * MODES + entry[0] // tiles_per * TILE
        return ((global_rows >= row_start) & (global_rows < row_start + TILE)).astype(jnp.float32)

    all_slices = lax.all_gather(field_rows[None], "cuts", axis=0, tiled=True)

    def one_product(entry):
        column_start = entry[0] % tiles_per * TILE
        first = lax.dynamic_index_in_dim(all_slices, entry[1], 0, keepdims=False)
        second = lax.dynamic_index_in_dim(all_slices, entry[2], 0, keepdims=False)
        first_real, first_imag = tile_columns(first, column_start)
        second_real, second_imag = tile_columns(second, column_start)
        return tile_pair(first_real, first_imag, second_real, second_imag, row_mask(entry))

    partial_value = lax.map(one_product, diagrams)
    totals = lax.psum(partial_value, "space")
    return (field_rows[None], totals)


def solution(mesh):
    placed = (P("cuts", None, None, "space"), P(), P())
    return jax.shard_map(
        per_device,
        mesh=mesh,
        in_specs=placed,
        out_specs=(P("cuts", "space", None), P()),
        check_vma=False,
    )
```

profile of v0, /device:TPU:0, one launch (start us, length us, event | category | flops | bytes accessed | tf_op | source)
XLA Modules:
  0.0 817.0 jit_solution(16971284501657460659)
XLA Ops:
  7.4 1.4 slice_bitcast_fusion.1
  9.6 3.7 gather_fusion.1
  13.3 4.7 gather_fusion.2
  18.0 2.6 gather_fusion
  22.3 7.5 multiply_add_fusion
  29.8 12.1 %fusion.2 = f32[1536,1024]{1,0:T(8,128)} fusion(f32[1536,256]{1,0:T(8,128)S(1)} %get-tuple-element.141, f32[1536,256]{1,0:T(8,128)S(1)} %get-tuple-element.140, f32[512,256]{1,0:T(8,128)S(1)} %get-tuple-element.142, f32[512,256]{1,0:T(8,128)S(1)} %get-tuple-element.143, f32[512,256]{1,0:T(8,128)S(1)} %copy-done.3), kind=kOutput, calls=%fused_computation.11 | convolution fusion | flops 9666035712 | bytes 11010048 | tf_op jit(solution)/shard_map/dot_general | solution.py:45
  42.0 88.0 %reduce-scatter.2.cloned.1.call-done = f32[96,1024]{1,0:T(8,128)} async-done(((f32[1536,1024]{1,0:T(8,128)}), f32[96,1024]{1,0:T(8,128)}) %reduce-scatter.2.cloned.1.call-update) | async-done | bytes 393232 | tf_op jit(solution)/shard_map/reduce_scatter | solution.py:76
  130.0 11.0 %all-gather = f32[192,1024]{1,0:T(8,128)S(1)} all-gather(f32[96,1024]{1,0:T(8,128)} %reduce-scatter.2.cloned.1.call-done), channel_id=2, replica_groups=mesh['space'=16,'cuts'=2] {'cuts'}, dimensions={0}, use_global_device_ids=true | all-gather | bytes 1179648 | tf_op jit(solution)/shard_map/all_gather | solution.py:97
  141.1 637.9 %while.14 = (s32[]{:T(128)}, f32[64,2]{0,1:T(2,128)S(1)}, s32[64,5]{0,1:T(8,128)S(1)}, f32[2,96,1024]{2,1,0:T(8,128)S(1)}, s32[]{:T(128)}, /*index=5*/s32[]{:T(1...) while((s32[]{:T(128)}, f32[64,2]{0,1:T(2,128)S(1)}, ...), condition=%wide.region_6.8_spmd.clone, body=%wide.region_1.0_spmd.clone.sunk | while | flops 197229 | bytes 395500 | solution.py:107
  149.6 1.3 maximum_multiply_fusion.2
  159.6 1.3 maximum_multiply_fusion.2
  169.5 1.3 maximum_multiply_fusion.2
  179.5 1.3 maximum_multiply_fusion.2
  189.5 1.3 maximum_multiply_fusion.2
  199.4 1.3 maximum_multiply_fusion.2
  209.4 1.3 maximum_multiply_fusion.2
  219.4 1.3 maximum_multiply_fusion.2
  229.3 1.3 maximum_multiply_fusion.2
  239.3 1.3 maximum_multiply_fusion.2
  249.3 1.3 maximum_multiply_fusion.2
  259.3 1.3 maximum_multiply_fusion.2
  269.2 1.3 maximum_multiply_fusion.2
  279.2 1.3 maximum_multiply_fusion.2
  289.2 1.3 maximum_multiply_fusion.2
  299.1 1.3 maximum_multiply_fusion.2
  309.1 1.3 maximum_multiply_fusion.2
  319.1 1.3 maximum_multiply_fusion.2
  329.0 1.3 maximum_multiply_fusion.2
  339.0 1.3 maximum_multiply_fusion.2
  349.0 1.3 maximum_multiply_fusion.2
  368.9 1.3 maximum_multiply_fusion.2
  378.9 1.3 maximum_multiply_fusion.2
  388.8 1.3 maximum_multiply_fusion.2
  398.8 1.3 maximum_multiply_fusion.2
  408.8 1.3 maximum_multiply_fusion.2
  418.7 1.3 maximum_multiply_fusion.2
  448.7 1.3 maximum_multiply_fusion.2
  458.6 1.3 maximum_multiply_fusion.2
  468.6 1.3 maximum_multiply_fusion.2
  478.6 1.3 maximum_multiply_fusion.2
  488.5 1.3 maximum_multiply_fusion.2
  498.5 1.3 maximum_multiply_fusion.2
  508.5 1.3 maximum_multiply_fusion.2
  538.4 1.3 maximum_multiply_fusion.2
  548.3 1.3 maximum_multiply_fusion.2
  558.3 1.3 maximum_multiply_fusion.2
  568.3 1.3 maximum_multiply_fusion.2
  588.2 1.3 maximum_multiply_fusion.2
  598.2 1.3 maximum_multiply_fusion.2
  608.2 1.3 maximum_multiply_fusion.2
  618.1 1.3 maximum_multiply_fusion.2
  628.1 1.3 maximum_multiply_fusion.2
  638.1 1.3 maximum_multiply_fusion.2
  648.0 1.3 maximum_multiply_fusion.2
  658.0 1.3 maximum_multiply_fusion.2
  668.0 1.3 maximum_multiply_fusion.2
  687.9 1.3 maximum_multiply_fusion.2
  697.9 1.3 maximum_multiply_fusion.2
  707.8 1.3 maximum_multiply_fusion.2
  717.8 1.3 maximum_multiply_fusion.2
  757.7 1.3 maximum_multiply_fusion.2
  767.7 1.3 maximum_multiply_fusion.2
  777.6 1.3 maximum_multiply_fusion.2
  779.0 31.1 %psum.7 = f32[64,2]{0,1:T(2,128)} all-reduce(f32[64,2]{0,1:T(2,128)S(1)} %get-tuple-element.105), channel_id=1, replica_groups=mesh['space'=16,'cuts'=2] {'space'}, use_global_device_ids=true, to_apply=%region_7.9 | all-reduce | flops 128 | bytes 1024 | tf_op jit(solution)/shard_map/psum | solution.py:108
  (354 shorter events, 127.7 us)
Async XLA Ops:
  7.2 10.8 %copy-start = (s32[3,3]{1,0:T(4,128)S(1)}, s32[3,3]{1,0:T(4,128)}, u32[]{:S(2)}) copy-start(s32[3,3]{1,0:T(4,128)} %param.8) | copy-start | bytes 112
  7.2 1.6 copy-start.2
  7.2 122.8 %reduce-scatter.2.cloned.1.call-start = ((), (), s32[]{:S(2)}) async-start(), calls=%async_computation.1 | async-start | bytes 6684672 | tf_op jit(solution)/shard_map/reduce_scatter | solution.py:76
  20.8 1.4 copy-start.1
  22.3 7.5 copy-start.3
  41.9 99.1 %copy-start.4 = (s32[64,5]{0,1:T(8,128)S(1)}, s32[64,5]{0,1:T(8,128)}, u32[]{:S(2)}) copy-start(s32[64,5]{0,1:T(8,128)} %param.9) | copy-start | bytes 3844
Sparse Core Ops, SparseCore 0:
  42.1 87.8 reduce-scatter.1
where the time goes:
time: 825 us; the launch traced here: 817 us
  loops' own time  445 us (54%)
  other arithmetic  151 us (18%)
  waiting for transfers between devices  88.1 us (11%)
  local copies, waits for them, and re-layouts  64.1 us (8%)
  blocking collectives  42.1 us (5%)
  between operations  14.2 us (2%)
  matrix products  12.1 us (1%)
    another operation x1, loops' own time, per_device(): partial_value = lax.map(one_product, diagrams)  445 us
    reduce_scatter x1, waiting for transfers between devices, per_device(): lax.psum_scatter(contract(phased_rows(jnp.take(real_vec, mode_ids, axis=0...  88 us
    div x64, other arithmetic, tile_pair(): jnp.stack([jnp.sum(mask * real_rows), jnp.sum(mask * imag_rows)]) / TILE  80.3 us
    reduce_sum x64, other arithmetic, tile_pair(): jnp.sum(mask * imag_rows)  44.4 us
    slice x64, local copies, waits for them, and re-layouts, row_mask(): row_start = entry[3] * MODES + entry[0] // tiles_per * TILE  38.7 us
    psum x1, blocking collectives, per_device(): totals = lax.psum(partial_value, 'space')  31.1 us
    reduce_sum x64, other arithmetic, tile_pair(): jnp.sum(first_real * second_real + first_imag * second_imag, axis=1)  17.7 us
  transfers between devices with their start and end apart: 1, of which 1 were waited for; matrix products, arithmetic and copies ran while one was open for 0% of the time, Pallas kernels for 0%

commit v1 on v0

v1 whole, which is shorter than its diff:
```python
import functools
import math

import jax
import jax.numpy as jnp
from jax import lax
from jax.experimental import pallas as pl
from jax.experimental.pallas import tpu as pltpu
from jax.sharding import PartitionSpec as P

MODES = 512
TILE = 256
PHASES = 3
EXTENT = 96

full_turn = 2.0 * math.pi
tiles_per = MODES // TILE
VMEM_LIMIT = 48 * 1024 * 1024


def angles_for(moment_rows, site_ids):
    coord_x = site_ids % EXTENT
    coord_y = site_ids // EXTENT % EXTENT
    coord_z = site_ids // (EXTENT * EXTENT)
    dotted = (
        moment_rows[:, 0:1] * coord_x[None, :]
        + moment_rows[:, 1:2] * coord_y[None, :]
        + moment_rows[:, 2:3] * coord_z[None, :]
    )
    return jnp.mod(dotted, EXTENT).astype(jnp.float32) * (full_turn / EXTENT)


def phased_rows(real_vec, imag_vec, moment_rows, site_ids):
    angle = angles_for(moment_rows, site_ids)
    cosine = jnp.cos(angle)
    sine = jnp.sin(angle)
    left_real = real_vec * cosine + imag_vec * sine
    left_imag = real_vec * sine - imag_vec * cosine
    return jnp.concatenate([left_real, left_imag], axis=1)


def right_block(real_vec, imag_vec):
    upper = jnp.concatenate([real_vec, -imag_vec], axis=1)
    lower = jnp.concatenate([imag_vec, real_vec], axis=1)
    return jnp.concatenate([upper, lower], axis=0)


def general(vectors, momenta, diagrams):
    real_vec = vectors[0, 0]
    imag_vec = vectors[0, 1]
    sites_dev = real_vec.shape[1]
    site_ids = lax.axis_index("space") * sites_dev + jnp.arange(sites_dev, dtype=jnp.int32)
    right = right_block(real_vec, imag_vec)
    own_rows = PHASES * MODES // lax.axis_size("space")
    left = jnp.concatenate(
        [phased_rows(real_vec, imag_vec, momenta[p : p + 1], site_ids) for p in range(PHASES)], axis=0
    )
    sums = lax.dot_general(
        left,
        right,
        (((1,), (1,)), ((), ())),
        precision=lax.Precision.HIGHEST,
        preferred_element_type=jnp.float32,
    )
    field_rows = lax.psum_scatter(sums, "space", scatter_dimension=0, tiled=True)
    slices = lax.all_gather(field_rows[None], "cuts", axis=0, tiled=True)
    count = slices.shape[0]
    group = (lax.axis_index("space") * own_rows + jnp.arange(own_rows, dtype=jnp.int32)) // TILE
    member = (group[None, :] == jnp.arange(PHASES * tiles_per)[:, None]).astype(jnp.float32)
    split = slices.reshape(count, own_rows, 2, tiles_per, TILE)
    real, imag = split[:, :, 0], split[:, :, 1]
    first_real, second_real = real[:, None], real[None, :]
    first_imag, second_imag = imag[:, None], imag[None, :]
    real_rows = jnp.sum(first_real * second_real + first_imag * second_imag, axis=-1)
    imag_rows = jnp.sum(first_imag * second_real - first_real * second_imag, axis=-1)
    rows = jnp.stack([real_rows, imag_rows])
    table = jnp.sum(rows[:, :, :, None] * member[None, None, None, :, :, None], axis=4)
    table = lax.psum(table, "space")
    tile, one, two, phase = (diagrams[:, i] for i in range(4))
    values = table[:, one, two, phase * tiles_per + tile // tiles_per, tile % tiles_per]
    return (field_rows[None], values.T / TILE)


CORE, Y, Z_NEAR, Z_FAR = 1, 2, 4, 8
CHUNKS = (24, 24, 24, 24)


def swap(array, bit):
    count = lax.axis_size("space")
    return lax.ppermute(array, "space", [(i, i ^ bit) for i in range(count)])


def split_kernel(own_ref, other_ref, high_ref, low_ref):
    sites = own_ref.shape[2]
    for part in range(2):
        for source, ref in enumerate((own_ref, other_ref)):
            value = ref[part]
            high = value.astype(jnp.bfloat16)
            low = (value - high.astype(jnp.float32)).astype(jnp.bfloat16)
            at = (2 * part + source) * sites
            high_ref[:, at : at + sites] = high
            low_ref[:, at : at + sites] = low


def rows_kernel(offset, rows, own_rows, own_ref, other_ref, cos_ref, sin_ref, high_ref, low_ref, send_ref, keep_ref, left_ref):
    me = lax.axis_index("space")
    sites = own_ref.shape[2]
    at = 0
    for dy in (Y, 0):
        for dn in (Z_NEAR, 0):
            for df in (Z_FAR, 0):
                block = me ^ (dy + dn + df)
                for group in range(rows // 8):
                    start = block * own_rows + (offset + 8 * group)
                    phase = start // MODES
                    mode = pl.multiple_of(start - phase * MODES, 8)
                    for source, ref in enumerate((own_ref, other_ref)):
                        real = ref[0, pl.ds(mode, 8), :]
                        imag = ref[1, pl.ds(mode, 8), :]
                        cosine = cos_ref[pl.ds(phase, 1), source * sites : (source + 1) * sites]
                        sine = sin_ref[pl.ds(phase, 1), source * sites : (source + 1) * sites]
                        left_ref[0, at : at + 8, source * sites : (source + 1) * sites] = real * cosine + imag * sine
                        left_ref[1, at : at + 8, source * sites : (source + 1) * sites] = real * sine - imag * cosine
                    at += 8
    half = at // 2
    for out_ref, begin in ((send_ref, 0), (keep_ref, half)):
        real = left_ref[0, begin : begin + half, :]
        imag = left_ref[1, begin : begin + half, :]
        real_high = real.astype(jnp.bfloat16)
        imag_high = imag.astype(jnp.bfloat16)
        real_low = (real - real_high.astype(jnp.float32)).astype(jnp.bfloat16)
        imag_low = (imag - imag_high.astype(jnp.float32)).astype(jnp.bfloat16)
        for column, parts in (
            (0, ((real_high, -imag_high), (real_low, -imag_low))),
            (1, ((imag_high, real_high), (imag_low, real_low))),
        ):
            high = jnp.concatenate(parts[0], axis=1)
            low = jnp.concatenate(parts[1], axis=1)

            def dot(a, b):
                return lax.dot_general(a, b, (((1,), (1,)), ((), ())), preferred_element_type=jnp.float32)

            out_ref[:, column * MODES : (column + 1) * MODES] = (
                dot(high, low_ref[...]) + dot(low, high_ref[...]) + dot(high, high_ref[...])
            )


def table_kernel(offset, own_rows, own_ref, other_ref, before_ref, table_ref):
    rows = own_ref.shape[0]
    first_row = lax.axis_index("space") * own_rows
    slice_index = lax.axis_index("cuts")
    first_group = first_row // TILE
    totals = [None, None]
    for at in range(0, rows, 8):
        entries = []
        for column in range(tiles_per):
            begin = column * TILE

            def cut(ref, start):
                return ref[at : at + 8, start : start + TILE]

            pairs = [(cut(own_ref, b), cut(other_ref, b)) for b in (begin, begin + MODES)]
            (real0, real1), (imag0, imag1) = [
                (jnp.where(slice_index == 0, a, b), jnp.where(slice_index == 0, b, a)) for a, b in pairs
            ]
            entries += [
                real0 * real0 + imag0 * imag0,
                real1 * real1 + imag1 * imag1,
                real0 * real1 + imag0 * imag1,
                imag0 * real1 - real0 * imag1,
            ]
        sums = jnp.concatenate(
            [jnp.sum(e[:, :128] + e[:, 128:], axis=0, keepdims=True) for e in entries], axis=0
        )
        local = (first_row + (offset + at)) // TILE - first_group
        for which in range(2):
            part = jnp.where(local == which, sums, 0.0)
            totals[which] = part if totals[which] is None else totals[which] + part
    lane = lax.broadcasted_iota(jnp.int32, (8, 128), 1)
    table = before_ref[...]
    for which in range(2):
        entry = jnp.sum(totals[which], axis=1, keepdims=True)
        entry = jnp.broadcast_to(entry, (8, 128))
        table = table + jnp.where(lane == first_group + which, entry, 0.0)
    table_ref[...] = table


def compiler_params():
    return pltpu.CompilerParams(vmem_limit_bytes=VMEM_LIMIT)


def in_vmem(count):
    return [pl.BlockSpec(memory_space=pltpu.VMEM)] * count


def halving(vectors, momenta, diagrams):
    own = vectors[0]
    sites = own.shape[2]
    me = lax.axis_index("space")
    own_rows = PHASES * MODES // lax.axis_size("space")
    within = jnp.arange(sites, dtype=jnp.int32)
    site_ids = jnp.concatenate([me * sites + within, (me ^ CORE) * sites + within])
    angle = angles_for(momenta, site_ids)
    cosine, sine = jnp.cos(angle), jnp.sin(angle)
    other = swap(own, CORE)
    high, low = pl.pallas_call(
        split_kernel,
        out_shape=[jax.ShapeDtypeStruct((MODES, 4 * sites), jnp.bfloat16)] * 2,
        in_specs=in_vmem(2),
        out_specs=in_vmem(2),
        compiler_params=compiler_params(),
        name="split",
    )(own, other)
    finished, table, offset = [], jnp.zeros((8, 128), jnp.float32), 0
    for rows in CHUNKS:
        depth = 4 * rows
        send, keep = pl.pallas_call(
            functools.partial(rows_kernel, offset, rows, own_rows),
            out_shape=[jax.ShapeDtypeStruct((depth, 2 * MODES), jnp.float32)] * 2,
            in_specs=in_vmem(6),
            out_specs=in_vmem(2),
            scratch_shapes=[pltpu.VMEM((2, 2 * depth, 2 * sites), jnp.float32)],
            compiler_params=compiler_params(),
            cost_estimate=pl.CostEstimate(
                flops=2 * 3 * 2 * depth * 2 * MODES * 4 * sites, bytes_accessed=4 * 1024 * 1024, transcendentals=0
            ),
            name="rows",
        )(own, other, cosine, sine, high, low)
        for bit in (Y, Z_NEAR, Z_FAR):
            came = swap(send, bit)
            if bit == Z_FAR:
                done = keep + came
            else:
                depth //= 2
                send = keep[:depth] + came[:depth]
                keep = keep[depth:] + came[depth:]
        across = lax.ppermute(done, "cuts", [(0, 1), (1, 0)])
        table = pl.pallas_call(
            functools.partial(table_kernel, offset, own_rows),
            out_shape=jax.ShapeDtypeStruct((8, 128), jnp.float32),
            in_specs=in_vmem(3),
            out_specs=in_vmem(1)[0],
            compiler_params=compiler_params(),
            name="table",
        )(done, across, table)
        finished.append(done)
        offset += rows
    for bit in (CORE, Y, Z_NEAR, Z_FAR):
        table = table + swap(table, bit)
    values = look_up(table, diagrams)
    return (jnp.concatenate(finished, axis=0)[None], values)


def look_up(table, diagrams):
    tile, one, two, phase = (diagrams[:, i : i + 1] for i in range(4))
    group = phase * tiles_per + tile // tiles_per
    column = tile % tiles_per
    lane = jnp.arange(128, dtype=jnp.int32)[None, :]
    picked = jnp.sum(jnp.where((lane == group)[:, None, :], table[None], 0.0), axis=2)
    kind = jnp.arange(8, dtype=jnp.int32)[None, :] - 4 * column
    same = one == two
    real = jnp.sum(jnp.where(kind == jnp.where(same, one, 2), picked, 0.0), axis=1)
    imag = jnp.sum(jnp.where((kind == 3) & ~same, picked, 0.0), axis=1)
    imag = jnp.where(one[:, 0] == 0, imag, -imag)
    return jnp.stack([real, imag], axis=1) / TILE


def solution(mesh):
    by_halves = mesh.shape["space"] == 16 and mesh.shape["cuts"] == 2
    placed = (P("cuts", None, None, "space"), P(), P())
    return jax.shard_map(
        halving if by_halves else general,
        mesh=mesh,
        in_specs=placed,
        out_specs=(P("cuts", "space", None), P()),
        check_vma=False,
    )
```

time: 825 us -> 88.9 us (0.11)
  loops' own time: 445 us -> 0 us
  other arithmetic: 151 us -> 2.31 us
  local copies, waits for them, and re-layouts: 64.1 us -> 2.07 us
  waiting for transfers between devices: 88.1 us -> 37.4 us
  blocking collectives: 42.1 us -> 0 us
  starting transfers between devices: 0.04 us -> 29.5 us
  Pallas kernels: 0 us -> 16.7 us
  between operations: 14.2 us -> 0.77 us
  matrix products: 12.1 us -> 0 us
    another operation x1 -> x0, loops' own time: 445 us -> none  [per_device(): partial_value = lax.map(one_product, diagrams)]
    reduce_scatter x1 -> x0, waiting for transfers between devices: 88 us -> none  [per_device(): lax.psum_scatter(contract(phased_rows(jnp.take(real_vec, mode_ids, axis=0...]
    div x64 -> x1, other arithmetic: 80.3 us -> 0.57 us  [look_up(): return jnp.stack([real, imag], axis=1) / TILE]
    reduce_sum x128 -> x2, other arithmetic: 62.1 us -> 0.33 us  [the longest x1 0.19 us: look_up(): jnp.sum(jnp.where(kind == jnp.where(same, one, 2), picked, 0.0), axis=1)]
    slice x64 -> x0, local copies, waits for them, and re-layouts: 38.7 us -> none  [row_mask(): row_start = entry[3] * MODES + entry[0] // tiles_per * TILE]
    ppermute x0 -> x21, waiting for transfers between devices: none -> 37.4 us  [the longest x17 33.7 us: swap(): return lax.ppermute(array, 'space', [(i, i ^ bit) for i in range(count)])]
    psum x1 -> x0, blocking collectives: 31.1 us -> none  [per_device(): totals = lax.psum(partial_value, 'space')]
    ppermute x0 -> x21, starting transfers between devices: none -> 29.5 us  [the longest x17 23.6 us: swap(): return lax.ppermute(array, 'space', [(i, i ^ bit) for i in range(count)])]
  transfers between devices with their start and end apart: 1 -> 21, of which waited for: 1 -> 12; matrix products, arithmetic and copies ran while one was open for 0% -> 2% of each run, Pallas kernels for 0% -> 14%
where the time goes in v1:
time: 88.9 us; the launch traced here: 88.7 us
  waiting for transfers between devices  37.4 us (42%)
  starting transfers between devices  29.5 us (33%)
  Pallas kernels  16.7 us (19%)
  other arithmetic  2.31 us (3%)
  local copies, waits for them, and re-layouts  2.07 us (2%)
    ppermute x17, waiting for transfers between devices, swap(): return lax.ppermute(array, 'space', [(i, i ^ bit) for i in range(count)])  33.7 us
    ppermute x17, starting transfers between devices, swap(): return lax.ppermute(array, 'space', [(i, i ^ bit) for i in range(count)])  23.6 us
    pallas_call x4, Pallas kernels, halving(): pl.pallas_call(functools.partial(rows_kernel, offset, rows, own_rows), ou...  15.7 us
    ppermute x4, starting transfers between devices, halving(): across = lax.ppermute(done, 'cuts', [(0, 1), (1, 0)])  5.98 us
    ppermute x4, waiting for transfers between devices, halving(): across = lax.ppermute(done, 'cuts', [(0, 1), (1, 0)])  3.62 us
    unnamed x6, local copies, waits for them, and re-layouts  1.88 us
  transfers between devices with their start and end apart: 21, of which 12 were waited for; matrix products, arithmetic and copies ran while one was open for 2% of the time, Pallas kernels for 14%

profile of v1, /device:TPU:0, one launch (start us, length us, event | category | flops | bytes accessed | tf_op | source)
XLA Modules:
  0.0 88.7 jit_solution(9452842379414770138)
XLA Ops:
  0.6 0.5 collective-permute-start
  1.2 0.0 copy-start.1
  1.2 0.7 copy-done.1
  1.8 0.2 slice_reduce_fusion.2
  2.0 0.2 fusion.11
  2.2 1.5 %collective-permute-done.other_ref = f32[2,512,256]{2,1,0:T(8,128)S(1)} collective-permute-done((f32[2,512,256]{2,1,0:T(8,128)}, f32[2,512,256]{2,1,0:T(8,128)S(1)}, u32[]{:S(2)}, u32[]{:S(2)}) %collective-permute-start) | collective-permute-done | bytes 1048608 | tf_op jit(solution)/shard_map/ppermute | solution.py:90
  3.6 0.0 copy-start
  3.6 1.2 %copy-done = f32[1,2,512,256]{3,2,1,0:T(8,128)S(1)} copy-done((f32[1,2,512,256]{3,2,1,0:T(8,128)S(1)}, f32[1,2,512,256]{3,2,1,0:T(8,128)}, u32[]{:S(2)}) %copy-start) | copy-done | bytes 1048600
  4.9 0.4 split.1
  5.3 3.9 %rows.7 = (f32[96,1024]{1,0:T(8,128)S(1)}, f32[96,1024]{1,0:T(8,128)S(1)}) custom-call(f32[2,512,256]{2,1,0:T(8,128)S(1)} %bitcast.16, f32[2,512,256]{2,1,0:T(8,128)S(1)} %collective-permute-done.other_ref, f32[3,512]{1,0:T(4,128)S(1)} %get-tuple-element.38.cos_ref, f32[3,512]{1,0:T(4,128)S(1)} %get-tuple-element.37.sin_ref, ...), custom_call_target="tpu_custom_call" | custom-call | flops 1207959552 | bytes 4194304 | tf_op jit(solution)/shard_map/rows/pallas_call | solution.py:217
  9.2 3.0 %collective-permute-start.10 = (f32[96,1024]{1,0:T(8,128)S(1)}, f32[96,1024]{1,0:T(8,128)S(1)}, u32[]{:S(2)}, u32[]{:S(2)}) collective-permute-start(f32[96,1024]{1,0:T(8,128)S(1)} %get-tuple-element.21), channel_id=1, source_target_pairs={{0,4},{2,6},{4,0},{6,2},{8,12},{10,14},{12,8},{14,10},{16,20},{18,... | collective-permute-start | bytes 1179656 | tf_op jit(solution)/shard_map/ppermute | solution.py:90
  12.2 3.9 %rows.6 = (f32[96,1024]{1,0:T(8,128)S(1)}, f32[96,1024]{1,0:T(8,128)S(1)}) custom-call(f32[2,512,256]{2,1,0:T(8,128)S(1)} %bitcast.17, f32[2,512,256]{2,1,0:T(8,128)S(1)} %collective-permute-done.other_ref, f32[3,512]{1,0:T(4,128)S(1)} %get-tuple-element.38.cos_ref, f32[3,512]{1,0:T(4,128)S(1)} %get-tuple-element.37.sin_ref, ...), custom_call_target="tpu_custom_call" | custom-call | flops 1207959552 | bytes 4194304 | tf_op jit(solution)/shard_map/rows/pallas_call | solution.py:217
  16.1 0.1 collective-permute-start.7
  16.2 3.9 %rows.5 = (f32[96,1024]{1,0:T(8,128)S(1)}, f32[96,1024]{1,0:T(8,128)S(1)}) custom-call(f32[2,512,256]{2,1,0:T(8,128)S(1)} %bitcast.18, f32[2,512,256]{2,1,0:T(8,128)S(1)} %collective-permute-done.other_ref, f32[3,512]{1,0:T(4,128)S(1)} %get-tuple-element.38.cos_ref, f32[3,512]{1,0:T(4,128)S(1)} %get-tuple-element.37.sin_ref, ...), custom_call_target="tpu_custom_call" | custom-call | flops 1207959552 | bytes 4194304 | tf_op jit(solution)/shard_map/rows/pallas_call | solution.py:217
  20.1 2.1 %collective-permute-start.4 = (f32[96,1024]{1,0:T(8,128)S(1)}, f32[96,1024]{1,0:T(8,128)S(1)}, u32[]{:S(2)}, u32[]{:S(2)}) collective-permute-start(f32[96,1024]{1,0:T(8,128)S(1)} %get-tuple-element.17), channel_id=1, source_target_pairs={{0,4},{2,6},{4,0},{6,2},{8,12},{10,14},{12,8},{14,10},{16,20},{18,... | collective-permute-start | bytes 1179656 | tf_op jit(solution)/shard_map/ppermute | solution.py:90
  22.2 3.9 %rows.4 = (f32[96,1024]{1,0:T(8,128)S(1)}, f32[96,1024]{1,0:T(8,128)S(1)}) custom-call(f32[2,512,256]{2,1,0:T(8,128)S(1)} %bitcast.19, f32[2,512,256]{2,1,0:T(8,128)S(1)} %collective-permute-done.other_ref, f32[3,512]{1,0:T(4,128)S(1)} %get-tuple-element.38.cos_ref, f32[3,512]{1,0:T(4,128)S(1)} %get-tuple-element.37.sin_ref, ...), custom_call_target="tpu_custom_call" | custom-call | flops 1207959552 | bytes 4194304 | tf_op jit(solution)/shard_map/rows/pallas_call | solution.py:217
  26.1 0.1 collective-permute-start.1
  26.2 0.0 collective-permute-done.10
  26.3 2.1 %collective-permute-start.11 = (f32[48,1024]{1,0:T(8,128)S(1)}, f32[48,1024]{1,0:T(8,128)S(1)}, u32[]{:S(2)}, u32[]{:S(2)}) collective-permute-start(f32[48,1024]{1,0:T(8,128)S(1)} %get-tuple-element.36), channel_id=1, source_target_pairs={{0,8},{2,10},{4,12},{6,14},{8,0},{10,2},{12,4},{14,6},{16,24},{18,... | collective-permute-start | bytes 589832 | tf_op jit(solution)/shard_map/ppermute | solution.py:90
  28.4 2.1 %collective-permute-done.7 = f32[96,1024]{1,0:T(8,128)S(1)} collective-permute-done((f32[96,1024]{1,0:T(8,128)S(1)}, f32[96,1024]{1,0:T(8,128)S(1)}, u32[]{:S(2)}, u32[]{:S(2)}) %collective-permute-start.7) | collective-permute-done | bytes 393248 | tf_op jit(solution)/shard_map/ppermute | solution.py:90
  30.6 2.2 %collective-permute-start.8 = (f32[48,1024]{1,0:T(8,128)S(1)}, f32[48,1024]{1,0:T(8,128)S(1)}, u32[]{:S(2)}, u32[]{:S(2)}) collective-permute-start(f32[48,1024]{1,0:T(8,128)S(1)} %get-tuple-element.34), channel_id=1, source_target_pairs={{0,8},{2,10},{4,12},{6,14},{8,0},{10,2},{12,4},{14,6},{16,24},{18,... | collective-permute-start | bytes 589832 | tf_op jit(solution)/shard_map/ppermute | solution.py:90
  32.7 6.2 %collective-permute-done.4 = f32[96,1024]{1,0:T(8,128)S(1)} collective-permute-done((f32[96,1024]{1,0:T(8,128)S(1)}, f32[96,1024]{1,0:T(8,128)S(1)}, u32[]{:S(2)}, u32[]{:S(2)}) %collective-permute-start.4) | collective-permute-done | bytes 393248 | tf_op jit(solution)/shard_map/ppermute | solution.py:90
  39.0 2.2 %collective-permute-start.5 = (f32[48,1024]{1,0:T(8,128)S(1)}, f32[48,1024]{1,0:T(8,128)S(1)}, u32[]{:S(2)}, u32[]{:S(2)}) collective-permute-start(f32[48,1024]{1,0:T(8,128)S(1)} %get-tuple-element.32), channel_id=1, source_target_pairs={{0,8},{2,10},{4,12},{6,14},{8,0},{10,2},{12,4},{14,6},{16,24},{18,... | collective-permute-start | bytes 589832 | tf_op jit(solution)/shard_map/ppermute | solution.py:90
  41.2 5.7 %collective-permute-done.1 = f32[96,1024]{1,0:T(8,128)S(1)} collective-permute-done((f32[96,1024]{1,0:T(8,128)S(1)}, f32[96,1024]{1,0:T(8,128)S(1)}, u32[]{:S(2)}, u32[]{:S(2)}) %collective-permute-start.1) | collective-permute-done | bytes 393248 | tf_op jit(solution)/shard_map/ppermute | solution.py:90
  46.9 1.9 %collective-permute-start.2 = (f32[48,1024]{1,0:T(8,128)S(1)}, f32[48,1024]{1,0:T(8,128)S(1)}, u32[]{:S(2)}, u32[]{:S(2)}) collective-permute-start(f32[48,1024]{1,0:T(8,128)S(1)} %get-tuple-element.30), channel_id=1, source_target_pairs={{0,8},{2,10},{4,12},{6,14},{8,0},{10,2},{12,4},{14,6},{16,24},{18,... | collective-permute-start | bytes 589832 | tf_op jit(solution)/shard_map/ppermute | solution.py:90
  48.8 0.0 collective-permute-done.11
  48.8 2.7 %collective-permute-start.12 = (f32[24,1024]{1,0:T(8,128)S(1)}, f32[24,1024]{1,0:T(8,128)S(1)}, u32[]{:S(2)}, u32[]{:S(2)}) collective-permute-start(f32[24,1024]{1,0:T(8,128)S(1)} %slice_add_fusion.8), channel_id=1, source_target_pairs={{0,16},{2,18},{4,20},{6,22},{8,24},{10,26},{12,28},{14,30},{16,0},... | collective-permute-start | bytes 294920 | tf_op jit(solution)/shard_map/ppermute | solution.py:90
  51.5 0.0 collective-permute-done.8
  51.5 0.4 collective-permute-start.9
  51.9 0.0 collective-permute-done.5
  51.9 2.7 %collective-permute-start.6 = (f32[24,1024]{1,0:T(8,128)S(1)}, f32[24,1024]{1,0:T(8,128)S(1)}, u32[]{:S(2)}, u32[]{:S(2)}) collective-permute-start(f32[24,1024]{1,0:T(8,128)S(1)} %slice_add_fusion.12), channel_id=1, source_target_pairs={{0,16},{2,18},{4,20},{6,22},{8,24},{10,26},{12,28},{14,30},{16,0},... | collective-permute-start | bytes 294920 | tf_op jit(solution)/shard_map/ppermute | solution.py:90
  54.5 1.3 %collective-permute-done.2 = f32[48,1024]{1,0:T(8,128)S(1)} collective-permute-done((f32[48,1024]{1,0:T(8,128)S(1)}, f32[48,1024]{1,0:T(8,128)S(1)}, u32[]{:S(2)}, u32[]{:S(2)}) %collective-permute-start.2) | collective-permute-done | bytes 196640 | tf_op jit(solution)/shard_map/ppermute | solution.py:90
  55.9 2.1 %collective-permute-start.3 = (f32[24,1024]{1,0:T(8,128)S(1)}, f32[24,1024]{1,0:T(8,128)S(1)}, u32[]{:S(2)}, u32[]{:S(2)}) collective-permute-start(f32[24,1024]{1,0:T(8,128)S(1)} %slice_add_fusion.14), channel_id=1, source_target_pairs={{0,16},{2,18},{4,20},{6,22},{8,24},{10,26},{12,28},{14,30},{16,0},... | collective-permute-start | bytes 294920 | tf_op jit(solution)/shard_map/ppermute | solution.py:90
  58.0 0.0 collective-permute-done.12
  58.0 1.6 %collective-permute-start.13 = (f32[24,1024]{1,0:T(8,128)S(1)}, f32[24,1024]{1,0:T(8,128)S(1)}, u32[]{:S(2)}, u32[]{:S(2)}) collective-permute-start(f32[24,1024]{1,0:T(8,128)S(1)} %fusion.own_ref), channel_id=1, source_target_pairs={{0,1},{1,0},{2,3},{3,2},{4,5},{5,4},{6,7},{7,6},{8,9},{9,8},{10,11... | collective-permute-start | bytes 294920 | tf_op jit(solution)/shard_map/ppermute | solution.py:237
  59.5 6.1 %collective-permute-done.9 = f32[24,1024]{1,0:T(8,128)S(1)} collective-permute-done((f32[24,1024]{1,0:T(8,128)S(1)}, f32[24,1024]{1,0:T(8,128)S(1)}, u32[]{:S(2)}, u32[]{:S(2)}) %collective-permute-start.9) | collective-permute-done | bytes 98336 | tf_op jit(solution)/shard_map/ppermute | solution.py:90
  65.7 1.6 %collective-permute-start.14 = (f32[24,1024]{1,0:T(8,128)S(1)}, f32[24,1024]{1,0:T(8,128)S(1)}, u32[]{:S(2)}, u32[]{:S(2)}) collective-permute-start(f32[24,1024]{1,0:T(8,128)S(1)} %fusion.1.own_ref), channel_id=1, source_target_pairs={{0,1},{1,0},{2,3},{3,2},{4,5},{5,4},{6,7},{7,6},{8,9},{9,8},{10,11... | collective-permute-start | bytes 294920 | tf_op jit(solution)/shard_map/ppermute | solution.py:237
  67.3 0.5 collective-permute-done.6
  67.8 0.0 copy-start.2
  67.8 1.6 %collective-permute-start.15 = (f32[24,1024]{1,0:T(8,128)S(1)}, f32[24,1024]{1,0:T(8,128)S(1)}, u32[]{:S(2)}, u32[]{:S(2)}) collective-permute-start(f32[24,1024]{1,0:T(8,128)S(1)} %fusion.2.own_ref), channel_id=1, source_target_pairs={{0,1},{1,0},{2,3},{3,2},{4,5},{5,4},{6,7},{7,6},{8,9},{9,8},{10,11... | collective-permute-start | bytes 294920 | tf_op jit(solution)/shard_map/ppermute | solution.py:237
  69.4 0.0 collective-permute-done.3
  69.4 1.3 %collective-permute-start.16 = (f32[24,1024]{1,0:T(8,128)S(1)}, f32[24,1024]{1,0:T(8,128)S(1)}, u32[]{:S(2)}, u32[]{:S(2)}) collective-permute-start(f32[24,1024]{1,0:T(8,128)S(1)} %fusion.3.own_ref), channel_id=1, source_target_pairs={{0,1},{1,0},{2,3},{3,2},{4,5},{5,4},{6,7},{7,6},{8,9},{9,8},{10,11... | collective-permute-start | bytes 294920 | tf_op jit(solution)/shard_map/ppermute | solution.py:237
  70.7 0.0 copy-done.2
  70.7 3.6 %collective-permute-done.16.other_ref = f32[24,1024]{1,0:T(8,128)S(1)} collective-permute-done((f32[24,1024]{1,0:T(8,128)S(1)}, f32[24,1024]{1,0:T(8,128)S(1)}, u32[]{:S(2)}, u32[]{:S(2)}) %collective-permute-start.16) | collective-permute-done | bytes 98336 | tf_op jit(solution)/shard_map/ppermute | solution.py:237
  74.3 0.1 table.4.before_ref
  74.5 0.0 collective-permute-done.15.other_ref
  74.5 0.1 table.5.before_ref
  74.6 0.0 collective-permute-done.14.other_ref
  74.6 0.1 table.6.before_ref
  74.8 0.0 collective-permute-done.13.other_ref
  74.8 0.1 table.7
  74.9 0.0 collective-permute-start.17
  74.9 1.1 %collective-permute-done.17 = f32[8,128]{1,0:T(8,128)S(1)} collective-permute-done((f32[8,128]{1,0:T(8,128)S(1)}, f32[8,128]{1,0:T(8,128)S(1)}, u32[]{:S(2)}, u32[]{:S(2)}) %collective-permute-start.17) | collective-permute-done | bytes 4128 | tf_op jit(solution)/shard_map/ppermute | solution.py:90
  76.1 1.5 %collective-permute-start.18 = (f32[8,128]{1,0:T(8,128)S(1)}, f32[8,128]{1,0:T(8,128)S(1)}, u32[]{:S(2)}, u32[]{:S(2)}) collective-permute-start(f32[8,128]{1,0:T(8,128)S(1)} %add.177), channel_id=1, source_target_pairs={{0,4},{2,6},{4,0},{6,2},{8,12},{10,14},{12,8},{14,10},{16,20},{18,... | collective-permute-start | bytes 12296 | tf_op jit(solution)/shard_map/ppermute | solution.py:90
  77.6 0.1 iota_compare_fusion
  77.7 2.0 %collective-permute-done.18 = f32[8,128]{1,0:T(8,128)S(1)} collective-permute-done((f32[8,128]{1,0:T(8,128)S(1)}, f32[8,128]{1,0:T(8,128)S(1)}, u32[]{:S(2)}, u32[]{:S(2)}) %collective-permute-start.18) | collective-permute-done | bytes 4128 | tf_op jit(solution)/shard_map/ppermute | solution.py:90
  79.7 0.0 collective-permute-start.19
  79.7 3.6 %collective-permute-done.19 = f32[8,128]{1,0:T(8,128)S(1)} collective-permute-done((f32[8,128]{1,0:T(8,128)S(1)}, f32[8,128]{1,0:T(8,128)S(1)}, u32[]{:S(2)}, u32[]{:S(2)}) %collective-permute-start.19) | collective-permute-done | bytes 4128 | tf_op jit(solution)/shard_map/ppermute | solution.py:90
  83.3 0.2 collective-permute-start.20
  83.5 0.8 maximum_bitcast_fusion
  84.3 3.5 %collective-permute-done.20 = f32[8,128]{1,0:T(8,128)S(1)} collective-permute-done((f32[8,128]{1,0:T(8,128)S(1)}, f32[8,128]{1,0:T(8,128)S(1)}, u32[]{:S(2)}, u32[]{:S(2)}) %collective-permute-start.20) | collective-permute-done | bytes 4128 | tf_op jit(solution)/shard_map/ppermute | solution.py:90
  87.8 0.1 select_reduce_fusion
  88.0 0.2 select_reduce_fusion.2
  88.2 0.6 maximum_multiply_fusion
  (23 shorter events, 0.4 us)
Async XLA Ops:
  0.6 3.0 %collective-permute-start = (f32[2,512,256]{2,1,0:T(8,128)}, f32[2,512,256]{2,1,0:T(8,128)S(1)}, u32[]{:S(2)}, u32[]{:S(2)}) collective-permute-start(f32[2,512,256]{2,1,0:T(8,128)} %bitcast.14), channel_id=1, source_target_pairs={{0,2},{2,0},{4,6},{6,4},{8,10},{10,8},{12,14},{14,12},{16,18},{18,... | collective-permute-start | bytes 3145736 | tf_op jit(solution)/shard_map/ppermute | solution.py:90
  1.2 0.7 copy-start.1
  3.6 1.2 %copy-start = (f32[1,2,512,256]{3,2,1,0:T(8,128)S(1)}, f32[1,2,512,256]{3,2,1,0:T(8,128)}, u32[]{:S(2)}) copy-start(f32[1,2,512,256]{3,2,1,0:T(8,128)} %param.3) | copy-start | bytes 3145732
  9.2 17.0 %collective-permute-start.10 = (f32[96,1024]{1,0:T(8,128)S(1)}, f32[96,1024]{1,0:T(8,128)S(1)}, u32[]{:S(2)}, u32[]{:S(2)}) collective-permute-start(f32[96,1024]{1,0:T(8,128)S(1)} %get-tuple-element.21), channel_id=1, source_target_pairs={{0,4},{2,6},{4,0},{6,2},{8,12},{10,14},{12,8},{14,10},{16,20},{18,... | collective-permute-start | bytes 1179656 | tf_op jit(solution)/shard_map/ppermute | solution.py:90
  16.1 14.4 %collective-permute-start.7 = (f32[96,1024]{1,0:T(8,128)S(1)}, f32[96,1024]{1,0:T(8,128)S(1)}, u32[]{:S(2)}, u32[]{:S(2)}) collective-permute-start(f32[96,1024]{1,0:T(8,128)S(1)} %get-tuple-element.19), channel_id=1, source_target_pairs={{0,4},{2,6},{4,0},{6,2},{8,12},{10,14},{12,8},{14,10},{16,20},{18,... | collective-permute-start | bytes 1179656 | tf_op jit(solution)/shard_map/ppermute | solution.py:90
  20.1 18.8 %collective-permute-start.4 = (f32[96,1024]{1,0:T(8,128)S(1)}, f32[96,1024]{1,0:T(8,128)S(1)}, u32[]{:S(2)}, u32[]{:S(2)}) collective-permute-start(f32[96,1024]{1,0:T(8,128)S(1)} %get-tuple-element.17), channel_id=1, source_target_pairs={{0,4},{2,6},{4,0},{6,2},{8,12},{10,14},{12,8},{14,10},{16,20},{18,... | collective-permute-start | bytes 1179656 | tf_op jit(solution)/shard_map/ppermute | solution.py:90
  26.1 20.7 %collective-permute-start.1 = (f32[96,1024]{1,0:T(8,128)S(1)}, f32[96,1024]{1,0:T(8,128)S(1)}, u32[]{:S(2)}, u32[]{:S(2)}) collective-permute-start(f32[96,1024]{1,0:T(8,128)S(1)} %get-tuple-element.15), channel_id=1, source_target_pairs={{0,4},{2,6},{4,0},{6,2},{8,12},{10,14},{12,8},{14,10},{16,20},{18,... | collective-permute-start | bytes 1179656 | tf_op jit(solution)/shard_map/ppermute | solution.py:90
  26.3 22.5 %collective-permute-start.11 = (f32[48,1024]{1,0:T(8,128)S(1)}, f32[48,1024]{1,0:T(8,128)S(1)}, u32[]{:S(2)}, u32[]{:S(2)}) collective-permute-start(f32[48,1024]{1,0:T(8,128)S(1)} %get-tuple-element.36), channel_id=1, source_target_pairs={{0,8},{2,10},{4,12},{6,14},{8,0},{10,2},{12,4},{14,6},{16,24},{18,... | collective-permute-start | bytes 589832 | tf_op jit(solution)/shard_map/ppermute | solution.py:90
  30.6 20.9 %collective-permute-start.8 = (f32[48,1024]{1,0:T(8,128)S(1)}, f32[48,1024]{1,0:T(8,128)S(1)}, u32[]{:S(2)}, u32[]{:S(2)}) collective-permute-start(f32[48,1024]{1,0:T(8,128)S(1)} %get-tuple-element.34), channel_id=1, source_target_pairs={{0,8},{2,10},{4,12},{6,14},{8,0},{10,2},{12,4},{14,6},{16,24},{18,... | collective-permute-start | bytes 589832 | tf_op jit(solution)/shard_map/ppermute | solution.py:90
  39.0 12.9 %collective-permute-start.5 = (f32[48,1024]{1,0:T(8,128)S(1)}, f32[48,1024]{1,0:T(8,128)S(1)}, u32[]{:S(2)}, u32[]{:S(2)}) collective-permute-start(f32[48,1024]{1,0:T(8,128)S(1)} %get-tuple-element.32), channel_id=1, source_target_pairs={{0,8},{2,10},{4,12},{6,14},{8,0},{10,2},{12,4},{14,6},{16,24},{18,... | collective-permute-start | bytes 589832 | tf_op jit(solution)/shard_map/ppermute | solution.py:90
  46.9 9.0 %collective-permute-start.2 = (f32[48,1024]{1,0:T(8,128)S(1)}, f32[48,1024]{1,0:T(8,128)S(1)}, u32[]{:S(2)}, u32[]{:S(2)}) collective-permute-start(f32[48,1024]{1,0:T(8,128)S(1)} %get-tuple-element.30), channel_id=1, source_target_pairs={{0,8},{2,10},{4,12},{6,14},{8,0},{10,2},{12,4},{14,6},{16,24},{18,... | collective-permute-start | bytes 589832 | tf_op jit(solution)/shard_map/ppermute | solution.py:90
  48.8 9.2 %collective-permute-start.12 = (f32[24,1024]{1,0:T(8,128)S(1)}, f32[24,1024]{1,0:T(8,128)S(1)}, u32[]{:S(2)}, u32[]{:S(2)}) collective-permute-start(f32[24,1024]{1,0:T(8,128)S(1)} %slice_add_fusion.8), channel_id=1, source_target_pairs={{0,16},{2,18},{4,20},{6,22},{8,24},{10,26},{12,28},{14,30},{16,0},... | collective-permute-start | bytes 294920 | tf_op jit(solution)/shard_map/ppermute | solution.py:90
  51.5 14.2 %collective-permute-start.9 = (f32[24,1024]{1,0:T(8,128)S(1)}, f32[24,1024]{1,0:T(8,128)S(1)}, u32[]{:S(2)}, u32[]{:S(2)}) collective-permute-start(f32[24,1024]{1,0:T(8,128)S(1)} %slice_add_fusion.10), channel_id=1, source_target_pairs={{0,16},{2,18},{4,20},{6,22},{8,24},{10,26},{12,28},{14,30},{16,0},... | collective-permute-start | bytes 294920 | tf_op jit(solution)/shard_map/ppermute | solution.py:90
  51.9 15.9 %collective-permute-start.6 = (f32[24,1024]{1,0:T(8,128)S(1)}, f32[24,1024]{1,0:T(8,128)S(1)}, u32[]{:S(2)}, u32[]{:S(2)}) collective-permute-start(f32[24,1024]{1,0:T(8,128)S(1)} %slice_add_fusion.12), channel_id=1, source_target_pairs={{0,16},{2,18},{4,20},{6,22},{8,24},{10,26},{12,28},{14,30},{16,0},... | collective-permute-start | bytes 294920 | tf_op jit(solution)/shard_map/ppermute | solution.py:90
  55.9 13.5 %collective-permute-start.3 = (f32[24,1024]{1,0:T(8,128)S(1)}, f32[24,1024]{1,0:T(8,128)S(1)}, u32[]{:S(2)}, u32[]{:S(2)}) collective-permute-start(f32[24,1024]{1,0:T(8,128)S(1)} %slice_add_fusion.14), channel_id=1, source_target_pairs={{0,16},{2,18},{4,20},{6,22},{8,24},{10,26},{12,28},{14,30},{16,0},... | collective-permute-start | bytes 294920 | tf_op jit(solution)/shard_map/ppermute | solution.py:90
  58.0 16.8 %collective-permute-start.13 = (f32[24,1024]{1,0:T(8,128)S(1)}, f32[24,1024]{1,0:T(8,128)S(1)}, u32[]{:S(2)}, u32[]{:S(2)}) collective-permute-start(f32[24,1024]{1,0:T(8,128)S(1)} %fusion.own_ref), channel_id=1, source_target_pairs={{0,1},{1,0},{2,3},{3,2},{4,5},{5,4},{6,7},{7,6},{8,9},{9,8},{10,11... | collective-permute-start | bytes 294920 | tf_op jit(solution)/shard_map/ppermute | solution.py:237
  65.7 8.9 %collective-permute-start.14 = (f32[24,1024]{1,0:T(8,128)S(1)}, f32[24,1024]{1,0:T(8,128)S(1)}, u32[]{:S(2)}, u32[]{:S(2)}) collective-permute-start(f32[24,1024]{1,0:T(8,128)S(1)} %fusion.1.own_ref), channel_id=1, source_target_pairs={{0,1},{1,0},{2,3},{3,2},{4,5},{5,4},{6,7},{7,6},{8,9},{9,8},{10,11... | collective-permute-start | bytes 294920 | tf_op jit(solution)/shard_map/ppermute | solution.py:237
  67.8 2.9 %copy-start.2 = (s32[64,5]{0,1:T(8,128)S(1)}, s32[64,5]{0,1:T(8,128)}, u32[]{:S(2)}) copy-start(s32[64,5]{0,1:T(8,128)} %param.5) | copy-start | bytes 3844
  67.8 6.7 %collective-permute-start.15 = (f32[24,1024]{1,0:T(8,128)S(1)}, f32[24,1024]{1,0:T(8,128)S(1)}, u32[]{:S(2)}, u32[]{:S(2)}) collective-permute-start(f32[24,1024]{1,0:T(8,128)S(1)} %fusion.2.own_ref), channel_id=1, source_target_pairs={{0,1},{1,0},{2,3},{3,2},{4,5},{5,4},{6,7},{7,6},{8,9},{9,8},{10,11... | collective-permute-start | bytes 294920 | tf_op jit(solution)/shard_map/ppermute | solution.py:237
  69.4 4.9 %collective-permute-start.16 = (f32[24,1024]{1,0:T(8,128)S(1)}, f32[24,1024]{1,0:T(8,128)S(1)}, u32[]{:S(2)}, u32[]{:S(2)}) collective-permute-start(f32[24,1024]{1,0:T(8,128)S(1)} %fusion.3.own_ref), channel_id=1, source_target_pairs={{0,1},{1,0},{2,3},{3,2},{4,5},{5,4},{6,7},{7,6},{8,9},{9,8},{10,11... | collective-permute-start | bytes 294920 | tf_op jit(solution)/shard_map/ppermute | solution.py:237
  74.9 1.2 %collective-permute-start.17 = (f32[8,128]{1,0:T(8,128)S(1)}, f32[8,128]{1,0:T(8,128)S(1)}, u32[]{:S(2)}, u32[]{:S(2)}) collective-permute-start(f32[8,128]{1,0:T(8,128)S(1)} %table.7), channel_id=1, source_target_pairs={{0,2},{2,0},{4,6},{6,4},{8,10},{10,8},{12,14},{14,12},{16,18},{18,... | collective-permute-start | bytes 12296 | tf_op jit(solution)/shard_map/ppermute | solution.py:90
  76.1 3.6 %collective-permute-start.18 = (f32[8,128]{1,0:T(8,128)S(1)}, f32[8,128]{1,0:T(8,128)S(1)}, u32[]{:S(2)}, u32[]{:S(2)}) collective-permute-start(f32[8,128]{1,0:T(8,128)S(1)} %add.177), channel_id=1, source_target_pairs={{0,4},{2,6},{4,0},{6,2},{8,12},{10,14},{12,8},{14,10},{16,20},{18,... | collective-permute-start | bytes 12296 | tf_op jit(solution)/shard_map/ppermute | solution.py:90
  79.7 3.6 %collective-permute-start.19 = (f32[8,128]{1,0:T(8,128)S(1)}, f32[8,128]{1,0:T(8,128)S(1)}, u32[]{:S(2)}, u32[]{:S(2)}) collective-permute-start(f32[8,128]{1,0:T(8,128)S(1)} %add.178), channel_id=1, source_target_pairs={{0,8},{2,10},{4,12},{6,14},{8,0},{10,2},{12,4},{14,6},{16,24},{18,... | collective-permute-start | bytes 12296 | tf_op jit(solution)/shard_map/ppermute | solution.py:90
  83.3 4.5 %collective-permute-start.20 = (f32[8,128]{1,0:T(8,128)S(1)}, f32[8,128]{1,0:T(8,128)S(1)}, u32[]{:S(2)}, u32[]{:S(2)}) collective-permute-start(f32[8,128]{1,0:T(8,128)S(1)} %add.179), channel_id=1, source_target_pairs={{0,16},{2,18},{4,20},{6,22},{8,24},{10,26},{12,28},{14,30},{16,0},... | collective-permute-start | bytes 12296 | tf_op jit(solution)/shard_map/ppermute | solution.py:90

commit v2 on v1

--- a/solution.py
+++ b/solution.py
@@ -82,12 +82,13 @@
 
 
 CORE, Y, Z_NEAR, Z_FAR = 1, 2, 4, 8
-CHUNKS = (24, 24, 24, 24)
-
-
-def swap(array, bit):
+STEPS = ((Y, Z_NEAR), (Z_NEAR, Y), (Z_FAR | Z_NEAR, Z_FAR | Z_NEAR))
+CHUNKS = (24, 40, 32)
+
+
+def swap(array, masks):
     count = lax.axis_size("space")
-    return lax.ppermute(array, "space", [(i, i ^ bit) for i in range(count)])
+    return lax.ppermute(array, "space", [(i, i ^ masks[i % 2]) for i in range(count)])
 
 
 def split_kernel(own_ref, other_ref, high_ref, low_ref):
@@ -105,11 +106,12 @@
 def rows_kernel(offset, rows, own_rows, own_ref, other_ref, cos_ref, sin_ref, high_ref, low_ref, send_ref, keep_ref, left_ref):
     me = lax.axis_index("space")
     sites = own_ref.shape[2]
+    masks = [jnp.where(me % 2 == 0, even, odd) for even, odd in STEPS]
     at = 0
-    for dy in (Y, 0):
-        for dn in (Z_NEAR, 0):
-            for df in (Z_FAR, 0):
-                block = me ^ (dy + dn + df)
+    for one in (masks[0], 0):
+        for two in (masks[1], 0):
+            for three in (masks[2], 0):
+                block = me ^ one ^ two ^ three
                 for group in range(rows // 8):
                     start = block * own_rows + (offset + 8 * group)
                     phase = start // MODES
@@ -122,27 +124,26 @@
                         left_ref[0, at : at + 8, source * sites : (source + 1) * sites] = real * cosine + imag * sine
                         left_ref[1, at : at + 8, source * sites : (source + 1) * sites] = real * sine - imag * cosine
                     at += 8
+    real, imag = left_ref[0], left_ref[1]
+    real_high, imag_high = real.astype(jnp.bfloat16), imag.astype(jnp.bfloat16)
+    real_low = (real - real_high.astype(jnp.float32)).astype(jnp.bfloat16)
+    imag_low = (imag - imag_high.astype(jnp.float32)).astype(jnp.bfloat16)
+
+    def both(real, imag):
+        return jnp.concatenate(
+            [jnp.concatenate([real, -imag], axis=1), jnp.concatenate([imag, real], axis=1)], axis=0
+        )
+
+    def dot(a, b):
+        return lax.dot_general(a, b, (((1,), (1,)), ((), ())), preferred_element_type=jnp.float32)
+
+    left_high, left_low = both(real_high, imag_high), both(real_low, imag_low)
+    out = dot(left_high, low_ref[...]) + dot(left_low, high_ref[...]) + dot(left_high, high_ref[...])
     half = at // 2
-    for out_ref, begin in ((send_ref, 0), (keep_ref, half)):
-        real = left_ref[0, begin : begin + half, :]
-        imag = left_ref[1, begin : begin + half, :]
-        real_high = real.astype(jnp.bfloat16)
-        imag_high = imag.astype(jnp.bfloat16)
-        real_low = (real - real_high.astype(jnp.float32)).astype(jnp.bfloat16)
-        imag_low = (imag - imag_high.astype(jnp.float32)).astype(jnp.bfloat16)
-        for column, parts in (
-            (0, ((real_high, -imag_high), (real_low, -imag_low))),
-            (1, ((imag_high, real_high), (imag_low, real_low))),
-        ):
-            high = jnp.concatenate(parts[0], axis=1)
-            low = jnp.concatenate(parts[1], axis=1)
-
-            def dot(a, b):
-                return lax.dot_general(a, b, (((1,), (1,)), ((), ())), preferred_element_type=jnp.float32)
-
-            out_ref[:, column * MODES : (column + 1) * MODES] = (
-                dot(high, low_ref[...]) + dot(low, high_ref[...]) + dot(high, high_ref[...])
-            )
+    for column in range(2):
+        columns = slice(column * MODES, (column + 1) * MODES)
+        send_ref[:, columns] = out[column * at : column * at + half]
+        keep_ref[:, columns] = out[column * at + half : (column + 1) * at]
 
 
 def table_kernel(offset, own_rows, own_ref, other_ref, before_ref, table_ref):
@@ -202,7 +203,7 @@
     site_ids = jnp.concatenate([me * sites + within, (me ^ CORE) * sites + within])
     angle = angles_for(momenta, site_ids)
     cosine, sine = jnp.cos(angle), jnp.sin(angle)
-    other = swap(own, CORE)
+    other = swap(own, (CORE, CORE))
     high, low = pl.pallas_call(
         split_kernel,
         out_shape=[jax.ShapeDtypeStruct((MODES, 4 * sites), jnp.bfloat16)] * 2,
@@ -226,9 +227,9 @@
             ),
             name="rows",
         )(own, other, cosine, sine, high, low)
-        for bit in (Y, Z_NEAR, Z_FAR):
-            came = swap(send, bit)
-            if bit == Z_FAR:
+        for masks in STEPS:
+            came = swap(send, masks)
+            if depth == rows:
                 done = keep + came
             else:
                 depth //= 2
@@ -246,7 +247,7 @@
         finished.append(done)
         offset += rows
     for bit in (CORE, Y, Z_NEAR, Z_FAR):
-        table = table + swap(table, bit)
+        table = table + swap(table, (bit, bit))
     values = look_up(table, diagrams)
     return (jnp.concatenate(finished, axis=0)[None], values)
 

time: 88.9 us -> 71.2 us (0.80)
  waiting for transfers between devices: 37.4 us -> 25.2 us
  Pallas kernels: 16.7 us -> 6.93 us
  starting transfers between devices: 29.5 us -> 33.7 us
    ppermute x17 -> x14, waiting for transfers between devices: 33.7 us -> 21.5 us  [swap(): lax.ppermute(array, 'space', [(i, i ^ masks[i % 2]) for i in range(count)])]
    pallas_call x4 -> x3, Pallas kernels: 15.7 us -> 6.05 us  [halving(): pl.pallas_call(functools.partial(rows_kernel, offset, rows, own_rows), ou...]
    ppermute x17 -> x14, starting transfers between devices: 23.6 us -> 29 us  [swap(): lax.ppermute(array, 'space', [(i, i ^ masks[i % 2]) for i in range(count)])]
    ppermute x4 -> x3, starting transfers between devices: 5.98 us -> 4.66 us  [halving(): across = lax.ppermute(done, 'cuts', [(0, 1), (1, 0)])]
    ppermute x4 -> x3, waiting for transfers between devices: 3.62 us -> 3.66 us  [halving(): across = lax.ppermute(done, 'cuts', [(0, 1), (1, 0)])]
  transfers between devices with their start and end apart: 21 -> 17, of which waited for: 12 -> 11; matrix products, arithmetic and copies ran while one was open for 2% -> 2% of each run, Pallas kernels for 14% -> 7%
where the time goes in v2:
time: 71.2 us; the launch traced here: 71 us
  starting transfers between devices  33.7 us (47%)
  waiting for transfers between devices  25.2 us (35%)
  Pallas kernels  6.93 us (10%)
  other arithmetic  2.34 us (3%)
  local copies, waits for them, and re-layouts  2.07 us (3%)
  between operations  0.77 us (1%)
    ppermute x14, starting transfers between devices, swap(): lax.ppermute(array, 'space', [(i, i ^ masks[i % 2]) for i in range(count)])  29 us
    ppermute x14, waiting for transfers between devices, swap(): lax.ppermute(array, 'space', [(i, i ^ masks[i % 2]) for i in range(count)])  21.5 us
    pallas_call x3, Pallas kernels, halving(): pl.pallas_call(functools.partial(rows_kernel, offset, rows, own_rows), ou...  6.05 us
    ppermute x3, starting transfers between devices, halving(): across = lax.ppermute(done, 'cuts', [(0, 1), (1, 0)])  4.66 us
    ppermute x3, waiting for transfers between devices, halving(): across = lax.ppermute(done, 'cuts', [(0, 1), (1, 0)])  3.66 us
    unnamed x6, local copies, waits for them, and re-layouts  1.88 us
  transfers between devices with their start and end apart: 17, of which 11 were waited for; matrix products, arithmetic and copies ran while one was open for 2% of the time, Pallas kernels for 7%

profile of v2, /device:TPU:0, one launch (start us, length us, event | category | flops | bytes accessed | tf_op | source)
XLA Modules:
  0.0 71.0 jit_solution(16759243428545548864)
XLA Ops:
  0.6 0.5 collective-permute-start
  1.2 0.0 copy-start.1
  1.2 0.7 copy-done.1
  1.8 0.2 slice_reduce_fusion.2
  2.0 0.2 fusion.10
  2.2 1.5 %collective-permute-done.other_ref = f32[2,512,256]{2,1,0:T(8,128)S(1)} collective-permute-done((f32[2,512,256]{2,1,0:T(8,128)}, f32[2,512,256]{2,1,0:T(8,128)S(1)}, u32[]{:S(2)}, u32[]{:S(2)}) %collective-permute-start) | collective-permute-done | bytes 1048608 | tf_op jit(solution)/shard_map/ppermute | solution.py:91
  3.6 0.0 copy-start
  3.6 1.2 %copy-done = f32[1,2,512,256]{3,2,1,0:T(8,128)S(1)} copy-done((f32[1,2,512,256]{3,2,1,0:T(8,128)S(1)}, f32[1,2,512,256]{3,2,1,0:T(8,128)}, u32[]{:S(2)}) %copy-start) | copy-done | bytes 1048600
  4.9 0.4 split.1
  5.3 1.6 %rows.3 = (f32[96,1024]{1,0:T(8,128)S(1)}, f32[96,1024]{1,0:T(8,128)S(1)}) custom-call(f32[2,512,256]{2,1,0:T(8,128)S(1)} %bitcast.16, f32[2,512,256]{2,1,0:T(8,128)S(1)} %collective-permute-done.other_ref, f32[3,512]{1,0:T(4,128)S(1)} %get-tuple-element.32.cos_ref, f32[3,512]{1,0:T(4,128)S(1)} %get-tuple-element.31.sin_ref, ...), custom_call_target="tpu_custom_call" | custom-call | flops 1207959552 | bytes 4194304 | tf_op jit(solution)/shard_map/rows/pallas_call | solution.py:218
  6.8 3.0 %collective-permute-start.1 = (f32[96,1024]{1,0:T(8,128)S(1)}, f32[96,1024]{1,0:T(8,128)S(1)}, u32[]{:S(2)}, u32[]{:S(2)}) collective-permute-start(f32[96,1024]{1,0:T(8,128)S(1)} %get-tuple-element.13), channel_id=1, source_target_pairs={{0,4},{2,10},{4,0},{6,14},{8,12},{10,2},{12,8},{14,6},{16,20},{18,... | collective-permute-start | bytes 1179656 | tf_op jit(solution)/shard_map/ppermute | solution.py:91
  9.8 2.0 %rows.5 = (f32[128,1024]{1,0:T(8,128)S(1)}, f32[128,1024]{1,0:T(8,128)S(1)}) custom-call(f32[2,512,256]{2,1,0:T(8,128)S(1)} %bitcast.17, f32[2,512,256]{2,1,0:T(8,128)S(1)} %collective-permute-done.other_ref, f32[3,512]{1,0:T(4,128)S(1)} %get-tuple-element.32.cos_ref, f32[3,512]{1,0:T(4,128)S(1)} %get-tuple-element.31.sin_ref, ...), custom_call_target="tpu_custom_call" | custom-call | flops 1610612736 | bytes 4194304 | tf_op jit(solution)/shard_map/rows/pallas_call | solution.py:218
  11.8 0.1 collective-permute-start.7
  11.9 2.5 %rows.4 = (f32[160,1024]{1,0:T(8,128)S(1)}, f32[160,1024]{1,0:T(8,128)S(1)}) custom-call(f32[2,512,256]{2,1,0:T(8,128)S(1)} %bitcast.18, f32[2,512,256]{2,1,0:T(8,128)S(1)} %collective-permute-done.other_ref, f32[3,512]{1,0:T(4,128)S(1)} %get-tuple-element.32.cos_ref, f32[3,512]{1,0:T(4,128)S(1)} %get-tuple-element.31.sin_ref, ...), custom_call_target="tpu_custom_call" | custom-call | flops 2013265920 | bytes 4194304 | tf_op jit(solution)/shard_map/rows/pallas_call | solution.py:218
  14.4 2.1 %collective-permute-start.4 = (f32[160,1024]{1,0:T(8,128)S(1)}, f32[160,1024]{1,0:T(8,128)S(1)}, u32[]{:S(2)}, u32[]{:S(2)}) collective-permute-start(f32[160,1024]{1,0:T(8,128)S(1)} %get-tuple-element.15), channel_id=1, source_target_pairs={{0,4},{2,10},{4,0},{6,14},{8,12},{10,2},{12,8},{14,6},{16,20},{18,... | collective-permute-start | bytes 1966088 | tf_op jit(solution)/shard_map/ppermute | solution.py:91
  16.5 0.0 collective-permute-done.1
  16.5 0.1 slice_add_fusion.5
  16.5 1.6 %collective-permute-start.2 = (f32[48,1024]{1,0:T(8,128)S(1)}, f32[48,1024]{1,0:T(8,128)S(1)}, u32[]{:S(2)}, u32[]{:S(2)}) collective-permute-start(f32[48,1024]{1,0:T(8,128)S(1)} %get-tuple-element.30), channel_id=1, source_target_pairs={{0,8},{2,6},{4,12},{6,2},{8,0},{10,14},{12,4},{14,10},{16,24},{18,... | collective-permute-start | bytes 589832 | tf_op jit(solution)/shard_map/ppermute | solution.py:91
  18.2 5.1 %collective-permute-done.7 = f32[128,1024]{1,0:T(8,128)S(1)} collective-permute-done((f32[128,1024]{1,0:T(8,128)S(1)}, f32[128,1024]{1,0:T(8,128)S(1)}, u32[]{:S(2)}, u32[]{:S(2)}) %collective-permute-start.7) | collective-permute-done | bytes 524320 | tf_op jit(solution)/shard_map/ppermute | solution.py:91
  23.3 0.1 slice_add_fusion.3
  23.4 2.1 %collective-permute-start.8 = (f32[64,1024]{1,0:T(8,128)S(1)}, f32[64,1024]{1,0:T(8,128)S(1)}, u32[]{:S(2)}, u32[]{:S(2)}) collective-permute-start(f32[64,1024]{1,0:T(8,128)S(1)} %get-tuple-element.28), channel_id=1, source_target_pairs={{0,8},{2,6},{4,12},{6,2},{8,0},{10,14},{12,4},{14,10},{16,24},{18,... | collective-permute-start | bytes 786440 | tf_op jit(solution)/shard_map/ppermute | solution.py:91
  25.5 0.0 collective-permute-done.2
  25.5 2.6 %collective-permute-start.3 = (f32[24,1024]{1,0:T(8,128)S(1)}, f32[24,1024]{1,0:T(8,128)S(1)}, u32[]{:S(2)}, u32[]{:S(2)}) collective-permute-start(f32[24,1024]{1,0:T(8,128)S(1)} %slice_add_fusion.10), channel_id=1, source_target_pairs={{0,24},{2,26},{4,28},{6,30},{8,16},{10,18},{12,20},{14,22},{16,8},... | collective-permute-start | bytes 294920 | tf_op jit(solution)/shard_map/ppermute | solution.py:91
  28.1 5.0 %collective-permute-done.4 = f32[160,1024]{1,0:T(8,128)S(1)} collective-permute-done((f32[160,1024]{1,0:T(8,128)S(1)}, f32[160,1024]{1,0:T(8,128)S(1)}, u32[]{:S(2)}, u32[]{:S(2)}) %collective-permute-start.4) | collective-permute-done | bytes 655392 | tf_op jit(solution)/shard_map/ppermute | solution.py:91
  33.1 0.1 slice_add_fusion.1
  33.2 2.1 %collective-permute-start.5 = (f32[80,1024]{1,0:T(8,128)S(1)}, f32[80,1024]{1,0:T(8,128)S(1)}, u32[]{:S(2)}, u32[]{:S(2)}) collective-permute-start(f32[80,1024]{1,0:T(8,128)S(1)} %get-tuple-element.26), channel_id=1, source_target_pairs={{0,8},{2,6},{4,12},{6,2},{8,0},{10,14},{12,4},{14,10},{16,24},{18,... | collective-permute-start | bytes 983048 | tf_op jit(solution)/shard_map/ppermute | solution.py:91
  35.3 1.6 %collective-permute-done.3 = f32[24,1024]{1,0:T(8,128)S(1)} collective-permute-done((f32[24,1024]{1,0:T(8,128)S(1)}, f32[24,1024]{1,0:T(8,128)S(1)}, u32[]{:S(2)}, u32[]{:S(2)}) %collective-permute-start.3) | collective-permute-done | bytes 98336 | tf_op jit(solution)/shard_map/ppermute | solution.py:91
  36.9 1.6 %collective-permute-start.12 = (f32[24,1024]{1,0:T(8,128)S(1)}, f32[24,1024]{1,0:T(8,128)S(1)}, u32[]{:S(2)}, u32[]{:S(2)}) collective-permute-start(f32[24,1024]{1,0:T(8,128)S(1)} %fusion.2.own_ref), channel_id=1, source_target_pairs={{0,1},{1,0},{2,3},{3,2},{4,5},{5,4},{6,7},{7,6},{8,9},{9,8},{10,11... | collective-permute-start | bytes 294920 | tf_op jit(solution)/shard_map/ppermute | solution.py:238
  38.5 0.0 collective-permute-done.8
  38.5 1.5 %collective-permute-start.9 = (f32[32,1024]{1,0:T(8,128)S(1)}, f32[32,1024]{1,0:T(8,128)S(1)}, u32[]{:S(2)}, u32[]{:S(2)}) collective-permute-start(f32[32,1024]{1,0:T(8,128)S(1)} %slice_add_fusion.8), channel_id=1, source_target_pairs={{0,24},{2,26},{4,28},{6,30},{8,16},{10,18},{12,20},{14,22},{16,8},... | collective-permute-start | bytes 393224 | tf_op jit(solution)/shard_map/ppermute | solution.py:91
  40.0 0.4 collective-permute-done.5
  40.4 7.5 %collective-permute-start.6 = (f32[40,1024]{1,0:T(8,128)S(1)}, f32[40,1024]{1,0:T(8,128)S(1)}, u32[]{:S(2)}, u32[]{:S(2)}) collective-permute-start(f32[40,1024]{1,0:T(8,128)S(1)} %slice_add_fusion.6), channel_id=1, source_target_pairs={{0,24},{2,26},{4,28},{6,30},{8,16},{10,18},{12,20},{14,22},{16,8},... | collective-permute-start | bytes 491528 | tf_op jit(solution)/shard_map/ppermute | solution.py:91
  48.0 0.0 collective-permute-done.9
  48.0 0.0 copy-start.2
  48.0 1.6 %collective-permute-start.10 = (f32[32,1024]{1,0:T(8,128)S(1)}, f32[32,1024]{1,0:T(8,128)S(1)}, u32[]{:S(2)}, u32[]{:S(2)}) collective-permute-start(f32[32,1024]{1,0:T(8,128)S(1)} %fusion.1.own_ref), channel_id=1, source_target_pairs={{0,1},{1,0},{2,3},{3,2},{4,5},{5,4},{6,7},{7,6},{8,9},{9,8},{10,11... | collective-permute-start | bytes 393224 | tf_op jit(solution)/shard_map/ppermute | solution.py:238
  49.6 1.8 %collective-permute-done.6 = f32[40,1024]{1,0:T(8,128)S(1)} collective-permute-done((f32[40,1024]{1,0:T(8,128)S(1)}, f32[40,1024]{1,0:T(8,128)S(1)}, u32[]{:S(2)}, u32[]{:S(2)}) %collective-permute-start.6) | collective-permute-done | bytes 163872 | tf_op jit(solution)/shard_map/ppermute | solution.py:91
  51.4 1.6 %collective-permute-start.11 = (f32[40,1024]{1,0:T(8,128)S(1)}, f32[40,1024]{1,0:T(8,128)S(1)}, u32[]{:S(2)}, u32[]{:S(2)}) collective-permute-start(f32[40,1024]{1,0:T(8,128)S(1)} %fusion.own_ref), channel_id=1, source_target_pairs={{0,1},{1,0},{2,3},{3,2},{4,5},{5,4},{6,7},{7,6},{8,9},{9,8},{10,11... | collective-permute-start | bytes 491528 | tf_op jit(solution)/shard_map/ppermute | solution.py:238
  53.0 0.0 copy-done.2
  53.0 0.0 collective-permute-done.12.other_ref
  53.0 0.1 table.3.before_ref
  53.2 3.7 %collective-permute-done.11.other_ref = f32[40,1024]{1,0:T(8,128)S(1)} collective-permute-done((f32[40,1024]{1,0:T(8,128)S(1)}, f32[40,1024]{1,0:T(8,128)S(1)}, u32[]{:S(2)}, u32[]{:S(2)}) %collective-permute-start.11) | collective-permute-done | bytes 163872 | tf_op jit(solution)/shard_map/ppermute | solution.py:238
  56.8 0.2 table.4.before_ref
  57.0 0.0 collective-permute-done.10.other_ref
  57.0 0.2 table.5
  57.1 0.0 collective-permute-start.13
  57.2 1.1 %collective-permute-done.13 = f32[8,128]{1,0:T(8,128)S(1)} collective-permute-done((f32[8,128]{1,0:T(8,128)S(1)}, f32[8,128]{1,0:T(8,128)S(1)}, u32[]{:S(2)}, u32[]{:S(2)}) %collective-permute-start.13) | collective-permute-done | bytes 4128 | tf_op jit(solution)/shard_map/ppermute | solution.py:91
  58.3 1.5 %collective-permute-start.14 = (f32[8,128]{1,0:T(8,128)S(1)}, f32[8,128]{1,0:T(8,128)S(1)}, u32[]{:S(2)}, u32[]{:S(2)}) collective-permute-start(f32[8,128]{1,0:T(8,128)S(1)} %add.157), channel_id=1, source_target_pairs={{0,4},{2,6},{4,0},{6,2},{8,12},{10,14},{12,8},{14,10},{16,20},{18,... | collective-permute-start | bytes 12296 | tf_op jit(solution)/shard_map/ppermute | solution.py:91
  59.8 0.1 iota_compare_fusion
  59.9 2.0 %collective-permute-done.14 = f32[8,128]{1,0:T(8,128)S(1)} collective-permute-done((f32[8,128]{1,0:T(8,128)S(1)}, f32[8,128]{1,0:T(8,128)S(1)}, u32[]{:S(2)}, u32[]{:S(2)}) %collective-permute-start.14) | collective-permute-done | bytes 4128 | tf_op jit(solution)/shard_map/ppermute | solution.py:91
  61.9 2.0 %collective-permute-start.15 = (f32[8,128]{1,0:T(8,128)S(1)}, f32[8,128]{1,0:T(8,128)S(1)}, u32[]{:S(2)}, u32[]{:S(2)}) collective-permute-start(f32[8,128]{1,0:T(8,128)S(1)} %add.158), channel_id=1, source_target_pairs={{0,8},{2,10},{4,12},{6,14},{8,0},{10,2},{12,4},{14,6},{16,24},{18,... | collective-permute-start | bytes 12296 | tf_op jit(solution)/shard_map/ppermute | solution.py:91
  63.9 1.6 %collective-permute-done.15 = f32[8,128]{1,0:T(8,128)S(1)} collective-permute-done((f32[8,128]{1,0:T(8,128)S(1)}, f32[8,128]{1,0:T(8,128)S(1)}, u32[]{:S(2)}, u32[]{:S(2)}) %collective-permute-start.15) | collective-permute-done | bytes 4128 | tf_op jit(solution)/shard_map/ppermute | solution.py:91
  65.5 2.3 %collective-permute-start.16 = (f32[8,128]{1,0:T(8,128)S(1)}, f32[8,128]{1,0:T(8,128)S(1)}, u32[]{:S(2)}, u32[]{:S(2)}) collective-permute-start(f32[8,128]{1,0:T(8,128)S(1)} %add.159), channel_id=1, source_target_pairs={{0,16},{2,18},{4,20},{6,22},{8,24},{10,26},{12,28},{14,30},{16,0},... | collective-permute-start | bytes 12296 | tf_op jit(solution)/shard_map/ppermute | solution.py:91
  67.9 0.8 %maximum_bitcast_fusion = f32[1,96,1024]{2,1,0:T(8,128)} fusion(f32[32,1024]{1,0:T(8,128)S(1)} %fusion.1.own_ref, f32[40,1024]{1,0:T(8,128)S(1)} %fusion.own_ref, f32[24,1024]{1,0:T(8,128)S(1)} %fusion.2.own_ref), kind=kLoop, calls=%fused_computation | loop fusion | flops 196608 | bytes 786432 | tf_op jit(solution)/shard_map/broadcast_in_dim | solution.py:252
  68.7 1.4 %collective-permute-done.16 = f32[8,128]{1,0:T(8,128)S(1)} collective-permute-done((f32[8,128]{1,0:T(8,128)S(1)}, f32[8,128]{1,0:T(8,128)S(1)}, u32[]{:S(2)}, u32[]{:S(2)}) %collective-permute-start.16) | collective-permute-done | bytes 4128 | tf_op jit(solution)/shard_map/ppermute | solution.py:91
  70.1 0.1 select_reduce_fusion
  70.2 0.2 select_reduce_fusion.2
  70.4 0.6 maximum_multiply_fusion
  (17 shorter events, 0.2 us)
Async XLA Ops:
  0.6 3.0 %collective-permute-start = (f32[2,512,256]{2,1,0:T(8,128)}, f32[2,512,256]{2,1,0:T(8,128)S(1)}, u32[]{:S(2)}, u32[]{:S(2)}) collective-permute-start(f32[2,512,256]{2,1,0:T(8,128)} %bitcast.14), channel_id=1, source_target_pairs={{0,2},{2,0},{4,6},{6,4},{8,10},{10,8},{12,14},{14,12},{16,18},{18,... | collective-permute-start | bytes 3145736 | tf_op jit(solution)/shard_map/ppermute | solution.py:91
  1.2 0.7 copy-start.1
  3.6 1.2 %copy-start = (f32[1,2,512,256]{3,2,1,0:T(8,128)S(1)}, f32[1,2,512,256]{3,2,1,0:T(8,128)}, u32[]{:S(2)}) copy-start(f32[1,2,512,256]{3,2,1,0:T(8,128)} %param.3) | copy-start | bytes 3145732
  6.8 9.6 %collective-permute-start.1 = (f32[96,1024]{1,0:T(8,128)S(1)}, f32[96,1024]{1,0:T(8,128)S(1)}, u32[]{:S(2)}, u32[]{:S(2)}) collective-permute-start(f32[96,1024]{1,0:T(8,128)S(1)} %get-tuple-element.13), channel_id=1, source_target_pairs={{0,4},{2,10},{4,0},{6,14},{8,12},{10,2},{12,8},{14,6},{16,20},{18,... | collective-permute-start | bytes 1179656 | tf_op jit(solution)/shard_map/ppermute | solution.py:91
  11.8 11.4 %collective-permute-start.7 = (f32[128,1024]{1,0:T(8,128)S(1)}, f32[128,1024]{1,0:T(8,128)S(1)}, u32[]{:S(2)}, u32[]{:S(2)}) collective-permute-start(f32[128,1024]{1,0:T(8,128)S(1)} %get-tuple-element.17), channel_id=1, source_target_pairs={{0,4},{2,10},{4,0},{6,14},{8,12},{10,2},{12,8},{14,6},{16,20},{18,... | collective-permute-start | bytes 1572872 | tf_op jit(solution)/shard_map/ppermute | solution.py:91
  14.4 18.7 %collective-permute-start.4 = (f32[160,1024]{1,0:T(8,128)S(1)}, f32[160,1024]{1,0:T(8,128)S(1)}, u32[]{:S(2)}, u32[]{:S(2)}) collective-permute-start(f32[160,1024]{1,0:T(8,128)S(1)} %get-tuple-element.15), channel_id=1, source_target_pairs={{0,4},{2,10},{4,0},{6,14},{8,12},{10,2},{12,8},{14,6},{16,20},{18,... | collective-permute-start | bytes 1966088 | tf_op jit(solution)/shard_map/ppermute | solution.py:91
  16.5 9.0 %collective-permute-start.2 = (f32[48,1024]{1,0:T(8,128)S(1)}, f32[48,1024]{1,0:T(8,128)S(1)}, u32[]{:S(2)}, u32[]{:S(2)}) collective-permute-start(f32[48,1024]{1,0:T(8,128)S(1)} %get-tuple-element.30), channel_id=1, source_target_pairs={{0,8},{2,6},{4,12},{6,2},{8,0},{10,14},{12,4},{14,10},{16,24},{18,... | collective-permute-start | bytes 589832 | tf_op jit(solution)/shard_map/ppermute | solution.py:91
  23.4 15.1 %collective-permute-start.8 = (f32[64,1024]{1,0:T(8,128)S(1)}, f32[64,1024]{1,0:T(8,128)S(1)}, u32[]{:S(2)}, u32[]{:S(2)}) collective-permute-start(f32[64,1024]{1,0:T(8,128)S(1)} %get-tuple-element.28), channel_id=1, source_target_pairs={{0,8},{2,6},{4,12},{6,2},{8,0},{10,14},{12,4},{14,10},{16,24},{18,... | collective-permute-start | bytes 786440 | tf_op jit(solution)/shard_map/ppermute | solution.py:91
  25.5 11.4 %collective-permute-start.3 = (f32[24,1024]{1,0:T(8,128)S(1)}, f32[24,1024]{1,0:T(8,128)S(1)}, u32[]{:S(2)}, u32[]{:S(2)}) collective-permute-start(f32[24,1024]{1,0:T(8,128)S(1)} %slice_add_fusion.10), channel_id=1, source_target_pairs={{0,24},{2,26},{4,28},{6,30},{8,16},{10,18},{12,20},{14,22},{16,8},... | collective-permute-start | bytes 294920 | tf_op jit(solution)/shard_map/ppermute | solution.py:91
  33.2 7.2 %collective-permute-start.5 = (f32[80,1024]{1,0:T(8,128)S(1)}, f32[80,1024]{1,0:T(8,128)S(1)}, u32[]{:S(2)}, u32[]{:S(2)}) collective-permute-start(f32[80,1024]{1,0:T(8,128)S(1)} %get-tuple-element.26), channel_id=1, source_target_pairs={{0,8},{2,6},{4,12},{6,2},{8,0},{10,14},{12,4},{14,10},{16,24},{18,... | collective-permute-start | bytes 983048 | tf_op jit(solution)/shard_map/ppermute | solution.py:91
  36.9 16.1 %collective-permute-start.12 = (f32[24,1024]{1,0:T(8,128)S(1)}, f32[24,1024]{1,0:T(8,128)S(1)}, u32[]{:S(2)}, u32[]{:S(2)}) collective-permute-start(f32[24,1024]{1,0:T(8,128)S(1)} %fusion.2.own_ref), channel_id=1, source_target_pairs={{0,1},{1,0},{2,3},{3,2},{4,5},{5,4},{6,7},{7,6},{8,9},{9,8},{10,11... | collective-permute-start | bytes 294920 | tf_op jit(solution)/shard_map/ppermute | solution.py:238
  38.5 9.5 %collective-permute-start.9 = (f32[32,1024]{1,0:T(8,128)S(1)}, f32[32,1024]{1,0:T(8,128)S(1)}, u32[]{:S(2)}, u32[]{:S(2)}) collective-permute-start(f32[32,1024]{1,0:T(8,128)S(1)} %slice_add_fusion.8), channel_id=1, source_target_pairs={{0,24},{2,26},{4,28},{6,30},{8,16},{10,18},{12,20},{14,22},{16,8},... | collective-permute-start | bytes 393224 | tf_op jit(solution)/shard_map/ppermute | solution.py:91
  40.4 10.9 %collective-permute-start.6 = (f32[40,1024]{1,0:T(8,128)S(1)}, f32[40,1024]{1,0:T(8,128)S(1)}, u32[]{:S(2)}, u32[]{:S(2)}) collective-permute-start(f32[40,1024]{1,0:T(8,128)S(1)} %slice_add_fusion.6), channel_id=1, source_target_pairs={{0,24},{2,26},{4,28},{6,30},{8,16},{10,18},{12,20},{14,22},{16,8},... | collective-permute-start | bytes 491528 | tf_op jit(solution)/shard_map/ppermute | solution.py:91
  48.0 5.0 %copy-start.2 = (s32[64,5]{0,1:T(8,128)S(1)}, s32[64,5]{0,1:T(8,128)}, u32[]{:S(2)}) copy-start(s32[64,5]{0,1:T(8,128)} %param.5) | copy-start | bytes 3844
  48.0 9.0 %collective-permute-start.10 = (f32[32,1024]{1,0:T(8,128)S(1)}, f32[32,1024]{1,0:T(8,128)S(1)}, u32[]{:S(2)}, u32[]{:S(2)}) collective-permute-start(f32[32,1024]{1,0:T(8,128)S(1)} %fusion.1.own_ref), channel_id=1, source_target_pairs={{0,1},{1,0},{2,3},{3,2},{4,5},{5,4},{6,7},{7,6},{8,9},{9,8},{10,11... | collective-permute-start | bytes 393224 | tf_op jit(solution)/shard_map/ppermute | solution.py:238
  51.4 5.4 %collective-permute-start.11 = (f32[40,1024]{1,0:T(8,128)S(1)}, f32[40,1024]{1,0:T(8,128)S(1)}, u32[]{:S(2)}, u32[]{:S(2)}) collective-permute-start(f32[40,1024]{1,0:T(8,128)S(1)} %fusion.own_ref), channel_id=1, source_target_pairs={{0,1},{1,0},{2,3},{3,2},{4,5},{5,4},{6,7},{7,6},{8,9},{9,8},{10,11... | collective-permute-start | bytes 491528 | tf_op jit(solution)/shard_map/ppermute | solution.py:238
  57.1 1.2 %collective-permute-start.13 = (f32[8,128]{1,0:T(8,128)S(1)}, f32[8,128]{1,0:T(8,128)S(1)}, u32[]{:S(2)}, u32[]{:S(2)}) collective-permute-start(f32[8,128]{1,0:T(8,128)S(1)} %table.5), channel_id=1, source_target_pairs={{0,2},{2,0},{4,6},{6,4},{8,10},{10,8},{12,14},{14,12},{16,18},{18,... | collective-permute-start | bytes 12296 | tf_op jit(solution)/shard_map/ppermute | solution.py:91
  58.3 3.6 %collective-permute-start.14 = (f32[8,128]{1,0:T(8,128)S(1)}, f32[8,128]{1,0:T(8,128)S(1)}, u32[]{:S(2)}, u32[]{:S(2)}) collective-permute-start(f32[8,128]{1,0:T(8,128)S(1)} %add.157), channel_id=1, source_target_pairs={{0,4},{2,6},{4,0},{6,2},{8,12},{10,14},{12,8},{14,10},{16,20},{18,... | collective-permute-start | bytes 12296 | tf_op jit(solution)/shard_map/ppermute | solution.py:91
  61.9 3.6 %collective-permute-start.15 = (f32[8,128]{1,0:T(8,128)S(1)}, f32[8,128]{1,0:T(8,128)S(1)}, u32[]{:S(2)}, u32[]{:S(2)}) collective-permute-start(f32[8,128]{1,0:T(8,128)S(1)} %add.158), channel_id=1, source_target_pairs={{0,8},{2,10},{4,12},{6,14},{8,0},{10,2},{12,4},{14,6},{16,24},{18,... | collective-permute-start | bytes 12296 | tf_op jit(solution)/shard_map/ppermute | solution.py:91
  65.5 4.5 %collective-permute-start.16 = (f32[8,128]{1,0:T(8,128)S(1)}, f32[8,128]{1,0:T(8,128)S(1)}, u32[]{:S(2)}, u32[]{:S(2)}) collective-permute-start(f32[8,128]{1,0:T(8,128)S(1)} %add.159), channel_id=1, source_target_pairs={{0,16},{2,18},{4,20},{6,22},{8,24},{10,26},{12,28},{14,30},{16,0},... | collective-permute-start | bytes 12296 | tf_op jit(solution)/shard_map/ppermute | solution.py:91

commit v3 on v2

v3 whole, which is shorter than its diff:
```python
import functools
import math

import jax
import jax.numpy as jnp
from jax import lax
from jax.experimental import pallas as pl
from jax.experimental.pallas import tpu as pltpu
from jax.sharding import PartitionSpec as P

MODES = 512
TILE = 256
PHASES = 3
EXTENT = 96

full_turn = 2.0 * math.pi
tiles_per = MODES // TILE
VMEM_LIMIT = 48 * 1024 * 1024


def angles_for(moment_rows, site_ids):
    coord_x = site_ids % EXTENT
    coord_y = site_ids // EXTENT % EXTENT
    coord_z = site_ids // (EXTENT * EXTENT)
    dotted = (
        moment_rows[:, 0:1] * coord_x[None, :]
        + moment_rows[:, 1:2] * coord_y[None, :]
        + moment_rows[:, 2:3] * coord_z[None, :]
    )
    return jnp.mod(dotted, EXTENT).astype(jnp.float32) * (full_turn / EXTENT)


def phased_rows(real_vec, imag_vec, moment_rows, site_ids):
    angle = angles_for(moment_rows, site_ids)
    cosine = jnp.cos(angle)
    sine = jnp.sin(angle)
    left_real = real_vec * cosine + imag_vec * sine
    left_imag = real_vec * sine - imag_vec * cosine
    return jnp.concatenate([left_real, left_imag], axis=1)


def right_block(real_vec, imag_vec):
    upper = jnp.concatenate([real_vec, -imag_vec], axis=1)
    lower = jnp.concatenate([imag_vec, real_vec], axis=1)
    return jnp.concatenate([upper, lower], axis=0)


def general(vectors, momenta, diagrams):
    real_vec = vectors[0, 0]
    imag_vec = vectors[0, 1]
    sites_dev = real_vec.shape[1]
    site_ids = lax.axis_index("space") * sites_dev + jnp.arange(sites_dev, dtype=jnp.int32)
    right = right_block(real_vec, imag_vec)
    own_rows = PHASES * MODES // lax.axis_size("space")
    left = jnp.concatenate(
        [phased_rows(real_vec, imag_vec, momenta[p : p + 1], site_ids) for p in range(PHASES)], axis=0
    )
    sums = lax.dot_general(
        left,
        right,
        (((1,), (1,)), ((), ())),
        precision=lax.Precision.HIGHEST,
        preferred_element_type=jnp.float32,
    )
    field_rows = lax.psum_scatter(sums, "space", scatter_dimension=0, tiled=True)
    slices = lax.all_gather(field_rows[None], "cuts", axis=0, tiled=True)
    count = slices.shape[0]
    group = (lax.axis_index("space") * own_rows + jnp.arange(own_rows, dtype=jnp.int32)) // TILE
    member = (group[None, :] == jnp.arange(PHASES * tiles_per)[:, None]).astype(jnp.float32)
    split = slices.reshape(count, own_rows, 2, tiles_per, TILE)
    real, imag = split[:, :, 0], split[:, :, 1]
    first_real, second_real = real[:, None], real[None, :]
    first_imag, second_imag = imag[:, None], imag[None, :]
    real_rows = jnp.sum(first_real * second_real + first_imag * second_imag, axis=-1)
    imag_rows = jnp.sum(first_imag * second_real - first_real * second_imag, axis=-1)
    rows = jnp.stack([real_rows, imag_rows])
    table = jnp.sum(rows[:, :, :, None] * member[None, None, None, :, :, None], axis=4)
    table = lax.psum(table, "space")
    tile, one, two, phase = (diagrams[:, i] for i in range(4))
    values = table[:, one, two, phase * tiles_per + tile // tiles_per, tile % tiles_per]
    return (field_rows[None], values.T / TILE)


CORE, Y, Z_NEAR, Z_FAR = 1, 2, 4, 8
FAR = (Z_FAR | Z_NEAR, Z_FAR)
STEPS = {
    "both": ((Y, Z_NEAR), (Z_NEAR, Y), FAR),
    "y": ((Y, Y), (Z_NEAR, Z_NEAR), FAR),
    "z": ((Z_NEAR, Z_NEAR), (Y, Y), FAR),
}
KINDS = ("both",) * 4
CHUNKS = (16, 32, 32, 16)
GROUPS = ((0, 1), (2,), (3,))
PLAN = (
    ("rows", 0), ("rows", 1), ("add", 0, 0), ("add", 1, 0), ("rows", 2), ("add", 0, 1), ("add", 1, 1), ("rows", 3),
    ("add", 0, 2), ("add", 2, 0), ("add", 3, 0), ("add", 1, 2), ("add", 2, 1), ("add", 3, 1), ("add", 2, 2), ("add", 3, 2),
    ("table", 0), ("table", 1), ("table", 2),
)
AFTER = {
    ("add", 1, 0): (("add", 0, 0),),
    ("rows", 2): (("add", 1, 0),),
    ("add", 1, 1): (("add", 0, 1),),
    ("rows", 3): (("add", 1, 1),),
    ("add", 2, 0): (("add", 0, 2),),
    ("add", 3, 0): (("add", 2, 0),),
    ("add", 1, 2): (("add", 3, 0),),
    ("add", 2, 1): (("add", 1, 2),),
    ("add", 3, 1): (("add", 2, 1),),
    ("add", 2, 2): (("add", 3, 1),),
    ("add", 3, 2): (("add", 2, 2),),
}


def swap(array, masks):
    count = lax.axis_size("space")
    return lax.ppermute(array, "space", [(i, i ^ masks[i % 2]) for i in range(count)])


def in_two(value):
    high = value.astype(jnp.bfloat16)
    return high, (value - high.astype(jnp.float32)).astype(jnp.bfloat16)


def split_kernel(value_ref, *refs):
    high_ref, low_ref = refs[-2:]
    sites = value_ref.shape[2]
    for part in range(2):
        columns = slice(part * sites, (part + 1) * sites)
        high_ref[:, columns], low_ref[:, columns] = in_two(value_ref[part])


def rows_kernel(offset, rows, own_rows, steps, sources, started, *refs):
    refs = list(refs)
    inputs = [tuple(refs.pop(0) for _ in range(3)) for _ in sources]
    cos_ref, sin_ref = refs.pop(0), refs.pop(0)
    before = (refs.pop(0), refs.pop(0)) if started else None
    send_ref, keep_ref, left_ref = refs
    me = lax.axis_index("space")
    masks = [jnp.where(me % 2 == 0, even, odd) for even, odd in steps]
    at = 0
    for one in (masks[0], 0):
        for two in (masks[1], 0):
            for three in (masks[2], 0):
                block = me ^ one ^ two ^ three
                for group in range(rows // 8):
                    start = block * own_rows + (offset + 8 * group)
                    phase = start // MODES
                    mode = pl.multiple_of(start - phase * MODES, 8)
                    for place, (source, (ref, _, _)) in enumerate(zip(sources, inputs)):
                        real = ref[0, pl.ds(mode, 8), :]
                        imag = ref[1, pl.ds(mode, 8), :]
                        cosine = cos_ref[source, pl.ds(phase, 1), :]
                        sine = sin_ref[source, pl.ds(phase, 1), :]
                        left_ref[2 * place, at : at + 8, :] = real * cosine + imag * sine
                        left_ref[2 * place + 1, at : at + 8, :] = real * sine - imag * cosine
                    at += 8

    def both(real, imag):
        return jnp.concatenate(
            [jnp.concatenate([real, -imag], axis=1), jnp.concatenate([imag, real], axis=1)], axis=0
        )

    def dot(a, b):
        return lax.dot_general(a, b, (((1,), (1,)), ((), ())), preferred_element_type=jnp.float32)

    out = None
    for place, (_, high_ref, low_ref) in enumerate(inputs):
        real_high, real_low = in_two(left_ref[2 * place])
        imag_high, imag_low = in_two(left_ref[2 * place + 1])
        left_high, left_low = both(real_high, imag_high), both(real_low, imag_low)
        part = dot(left_high, low_ref[...]) + dot(left_low, high_ref[...]) + dot(left_high, high_ref[...])
        out = part if out is None else out + part
    half = at // 2
    for column in range(2):
        columns = slice(column * MODES, (column + 1) * MODES)
        for place, ref in enumerate((send_ref, keep_ref)):
            part = out[column * at + place * half : column * at + (place + 1) * half]
            ref[:, columns] = part + before[place][:, columns] if started else part


def halve_kernel(keep_ref, came_ref, *refs):
    send_ref, rest_ref = refs[-2:]
    half = keep_ref.shape[0] // 2
    send_ref[...] = keep_ref[:half, :] + came_ref[:half, :]
    rest_ref[...] = keep_ref[half:, :] + came_ref[half:, :]


def finish_kernel(keep_ref, came_ref, *refs):
    out_ref = refs[-1]
    rows = keep_ref.shape[0]
    done = out_ref.shape[0] - rows
    if done:
        out_ref[:done, :] = refs[0][...]
    out_ref[done:, :] = keep_ref[...] + came_ref[...]


def table_kernel(offset, own_rows, own_ref, other_ref, before_ref, table_ref):
    rows = own_ref.shape[0]
    first_row = lax.axis_index("space") * own_rows
    slice_index = lax.axis_index("cuts")
    first_group = first_row // TILE
    totals = [None, None]
    for at in range(0, rows, 8):
        entries = []
        for column in range(tiles_per):
            begin = column * TILE

            def cut(ref, start):
                return ref[at : at + 8, start : start + TILE]

            pairs = [(cut(own_ref, b), cut(other_ref, b)) for b in (begin, begin + MODES)]
            (real0, real1), (imag0, imag1) = [
                (jnp.where(slice_index == 0, a, b), jnp.where(slice_index == 0, b, a)) for a, b in pairs
            ]
            entries += [
                real0 * real0 + imag0 * imag0,
                real1 * real1 + imag1 * imag1,
                real0 * real1 + imag0 * imag1,
                imag0 * real1 - real0 * imag1,
            ]
        sums = jnp.concatenate(
            [jnp.sum(e[:, :128] + e[:, 128:], axis=0, keepdims=True) for e in entries], axis=0
        )
        local = (first_row + (offset + at)) // TILE - first_group
        for which in range(2):
            part = jnp.where(local == which, sums, 0.0)
            totals[which] = part if totals[which] is None else totals[which] + part
    lane = lax.broadcasted_iota(jnp.int32, (8, 128), 1)
    table = before_ref[...]
    for which in range(2):
        entry = jnp.broadcast_to(jnp.sum(totals[which], axis=1, keepdims=True), (8, 128))
        table = table + jnp.where(lane == first_group + which, entry, 0.0)
    table_ref[...] = table


def look_up_kernel(table_ref, where_ref, scale_ref, values_ref):
    lanes = values_ref.shape[1]
    kind = lax.broadcasted_iota(jnp.int32, (8, lanes), 0)
    lane = jnp.broadcast_to(where_ref[0:1, :], (8, lanes))
    picked = jnp.zeros((8, lanes), jnp.float32)
    for group in range(PHASES * tiles_per):
        picked = picked + jnp.where(lane == group, table_ref[:, group : group + 1], 0.0)
    for part in range(2):
        row = jnp.sum(jnp.where(kind == where_ref[part + 1 : part + 2, :], picked, 0.0), axis=0, keepdims=True)
        values_ref[part : part + 1, :] = row * scale_ref[part : part + 1, :]


VMEM_SPEC = pl.BlockSpec(memory_space=pltpu.VMEM)
ANY_SPEC = pl.BlockSpec(memory_space=pl.ANY)
TOKEN = jax.ShapeDtypeStruct((8, 128), jnp.float32)


def kernel_call(body, name, ins, outs, tokens=(), scratch=(), flops=0):
    return pl.pallas_call(
        body,
        out_shape=outs,
        in_specs=[VMEM_SPEC] * len(ins) + [ANY_SPEC] * len(tokens),
        out_specs=[VMEM_SPEC] * len(outs),
        scratch_shapes=scratch,
        compiler_params=pltpu.CompilerParams(vmem_limit_bytes=VMEM_LIMIT),
        cost_estimate=pl.CostEstimate(flops=flops, bytes_accessed=1024 * 1024, transcendentals=0),
        name=name,
    )(*ins, *tokens)


def floats(*shape):
    return jax.ShapeDtypeStruct(shape, jnp.float32)


def halving(vectors, momenta, diagrams):
    own = vectors[0]
    sites = own.shape[2]
    me = lax.axis_index("space")
    own_rows = PHASES * MODES // lax.axis_size("space")
    within = jnp.arange(sites, dtype=jnp.int32)
    site_ids = jnp.concatenate([me * sites + within, (me ^ CORE) * sites + within])
    angle = angles_for(momenta, site_ids)
    cosine, sine = (jnp.swapaxes(f(angle).reshape(PHASES, 2, sites), 0, 1) for f in (jnp.cos, jnp.sin))
    other = swap(own, (CORE, CORE))
    halves = [jax.ShapeDtypeStruct((MODES, 2 * sites), jnp.bfloat16)] * 2
    mine = own, *kernel_call(split_kernel, "split", [own], halves, (cosine, sine))

    def products(chunk, sources, inputs, started=()):
        rows = CHUNKS[chunk]
        depth = 4 * rows
        ins = [a for i in inputs for a in i] + [cosine, sine, *started]
        return kernel_call(
            functools.partial(rows_kernel, sum(CHUNKS[:chunk]), rows, own_rows, STEPS[KINDS[chunk]], sources, bool(started)),
            "rows",
            ins,
            [floats(depth, 2 * MODES)] * 2,
            scratch=[pltpu.VMEM((2 * len(sources), 2 * depth, sites), jnp.float32)],
            flops=2 * 3 * 4 * depth * MODES * 2 * sites * len(sources),
        )

    begun = products(0, (0,), (mine,))
    theirs = other, *kernel_call(split_kernel, "split", [other], halves)
    keeps, flights, groups, tokens = {}, {}, {}, {}
    table = jnp.zeros((8, 128), jnp.float32)
    for event in PLAN:
        kind, which = event[:2]
        after = [tokens[e] for e in AFTER.get(event, ())]
        if kind == "rows":
            if which == 0:
                send, keep = products(0, (1,), (theirs,), begun)
            else:
                send, keep = products(which, (0, 1), (mine, theirs))
            keeps[which], flights[which] = keep, swap(send, STEPS[KINDS[which]][0])
        elif kind == "add" and event[2] < 2:
            keep, came = keeps[which], flights[which]
            half = keep.shape[0] // 2
            if after:
                send, keep = kernel_call(halve_kernel, "halve", [keep, came], [floats(half, 2 * MODES)] * 2, after)
            else:
                send, keep = keep[:half] + came[:half], keep[half:] + came[half:]
            tokens[event] = keep
            keeps[which], flights[which] = keep, swap(send, STEPS[KINDS[which]][event[2] + 1])
        elif kind == "add":
            group = next(g for g in GROUPS if which in g)
            keep, came = keeps[which], flights[which]
            before = [groups[group]] if group in groups else []
            if after or before:
                rows = CHUNKS[which] + sum(b.shape[0] for b in before)
                (done,) = kernel_call(finish_kernel, "finish", [keep, came, *before], [floats(rows, 2 * MODES)], after)
            else:
                done = keep + came
            tokens[event] = groups[group] = done
            if which == group[-1]:
                flights[group] = lax.ppermute(done, "cuts", [(0, 1), (1, 0)])
        else:
            group = GROUPS[which]
            (table,) = kernel_call(
                functools.partial(table_kernel, sum(CHUNKS[: group[0]]), own_rows),
                "table",
                [groups[group], flights[group], table],
                [TOKEN],
                after,
            )
    for bit in (CORE, Y, Z_NEAR, Z_FAR):
        table = table + swap(table, (bit, bit))
    tile, one, two, phase = (diagrams[:, i] for i in range(4))
    column = 4 * (tile % tiles_per)
    same = one == two
    where = jnp.stack([phase * tiles_per + tile // tiles_per, column + jnp.where(same, one, 2), column + 3])
    sign = jnp.where(same, 0.0, jnp.where(one == 0, 1.0, -1.0))
    scale = jnp.stack([jnp.ones_like(sign), sign]) / TILE
    (values,) = kernel_call(look_up_kernel, "look_up", [table, where, scale], [floats(2, diagrams.shape[0])])
    return (jnp.concatenate([groups[g] for g in GROUPS], axis=0)[None], values.T)


def solution(mesh):
    by_halves = mesh.shape["space"] == 16 and mesh.shape["cuts"] == 2
    placed = (P("cuts", None, None, "space"), P(), P())
    return jax.shard_map(
        halving if by_halves else general,
        mesh=mesh,
        in_specs=placed,
        out_specs=(P("cuts", "space", None), P()),
        check_vma=False,
    )
```

time: 71.2 us -> 67.5 us (0.948)
  starting transfers between devices: 33.7 us -> 28.9 us
  Pallas kernels: 6.93 us -> 8.13 us
  other arithmetic: 2.34 us -> 1.14 us
  waiting for transfers between devices: 25.2 us -> 26.1 us
    ppermute x14 -> x17, starting transfers between devices: 29 us -> 24.3 us  [swap(): lax.ppermute(array, 'space', [(i, i ^ masks[i % 2]) for i in range(count)])]
    ppermute x14 -> x17, waiting for transfers between devices: 21.5 us -> 23.7 us  [swap(): lax.ppermute(array, 'space', [(i, i ^ masks[i % 2]) for i in range(count)])]
    ppermute x3, waiting for transfers between devices: 3.66 us -> 2.4 us  [halving(): flights[group] = lax.ppermute(done, 'cuts', [(0, 1), (1, 0)])]
    pallas_call x7 -> x20, Pallas kernels: 6.93 us -> 8.13 us  [kernel_call(): pl.pallas_call(body, out_shape=outs, in_specs=[VMEM_SPEC] * len(ins) + [A...]
    unnamed x6 -> x8, local copies, waits for them, and re-layouts: 1.88 us -> 1.89 us
  transfers between devices with their start and end apart: 17 -> 20, of which waited for: 11 -> 15; matrix products, arithmetic and copies ran while one was open for 2% -> 2% of each run, Pallas kernels for 7% -> 10%
where the time goes in v3:
time: 67.5 us; the launch traced here: 67.3 us
  starting transfers between devices  28.9 us (43%)
  waiting for transfers between devices  26.1 us (39%)
  Pallas kernels  8.13 us (12%)
  local copies, waits for them, and re-layouts  2.15 us (3%)
  other arithmetic  1.14 us (2%)
  between operations  0.83 us (1%)
    ppermute x17, starting transfers between devices, swap(): lax.ppermute(array, 'space', [(i, i ^ masks[i % 2]) for i in range(count)])  24.3 us
    ppermute x17, waiting for transfers between devices, swap(): lax.ppermute(array, 'space', [(i, i ^ masks[i % 2]) for i in range(count)])  23.7 us
    pallas_call x20, Pallas kernels, kernel_call(): pl.pallas_call(body, out_shape=outs, in_specs=[VMEM_SPEC] * len(ins) + [A...  8.13 us
    ppermute x3, starting transfers between devices, halving(): flights[group] = lax.ppermute(done, 'cuts', [(0, 1), (1, 0)])  4.68 us
    ppermute x3, waiting for transfers between devices, halving(): flights[group] = lax.ppermute(done, 'cuts', [(0, 1), (1, 0)])  2.4 us
    unnamed x8, local copies, waits for them, and re-layouts  1.89 us
  transfers between devices with their start and end apart: 20, of which 15 were waited for; matrix products, arithmetic and copies ran while one was open for 2% of the time, Pallas kernels for 10%

profile of v3, /device:TPU:0, one launch (start us, length us, event | category | flops | bytes accessed | tf_op | source)
XLA Modules:
  0.0 67.3 jit_solution(905573087506064707)
XLA Ops:
  0.6 0.5 collective-permute-start
  1.3 0.0 copy-start.2
  1.3 0.7 copy-done.2
  2.0 0.2 slice_reduce_fusion.2
  2.2 0.2 fusion.3
  2.3 0.0 copy-start
  2.3 1.2 %copy-done = f32[1,2,512,256]{3,2,1,0:T(8,128)S(1)} copy-done((f32[1,2,512,256]{3,2,1,0:T(8,128)S(1)}, f32[1,2,512,256]{3,2,1,0:T(8,128)}, u32[]{:S(2)}) %copy-start) | copy-done | bytes 1048600
  3.6 0.2 split.2
  3.8 0.6 rows.6
  4.4 0.0 collective-permute-done.value_ref.refs_3_.refs_0_
  4.4 0.2 split.3
  4.6 0.0 copy-start.1
  4.6 0.7 rows.7
  5.3 2.6 %collective-permute-start.2 = (f32[64,1024]{1,0:T(8,128)S(1)}, f32[64,1024]{1,0:T(8,128)S(1)}, u32[]{:S(2)}, u32[]{:S(2)}) collective-permute-start(f32[64,1024]{1,0:T(8,128)S(1)} %get-tuple-element.37), channel_id=1, source_target_pairs={{0,4},{2,10},{4,0},{6,14},{8,12},{10,2},{12,8},{14,6},{16,20},{18,... | collective-permute-start | bytes 786440 | tf_op jit(solution)/shard_map/ppermute | solution.py:116
  7.9 0.0 copy-done.1
  7.9 2.0 %rows.5 = (f32[128,1024]{1,0:T(8,128)S(1)}, f32[128,1024]{1,0:T(8,128)S(1)}) custom-call(f32[2,512,256]{2,1,0:T(8,128)S(1)} %bitcast.29, bf16[512,512]{1,0:T(8,128)(2,1)S(1)} %get-tuple-element.28.refs_1_, bf16[512,512]{1,0:T(8,128)(2,1)S(1)} %get-tuple-element.29.refs_2_, f32[2,512,256]{2,1,0:T(8,128)S(1)} %collective-permute-done.value_ref.refs_3_.refs_0_, ...), custom_call_target="tpu_custom_call" | custom-call | flops 1610612736 | bytes 1048576 | tf_op jit(solution)/shard_map/rows/pallas_call | solution.py:254
  9.9 0.5 collective-permute-start.1
  10.5 1.8 %collective-permute-done.2 = f32[64,1024]{1,0:T(8,128)S(1)} collective-permute-done((f32[64,1024]{1,0:T(8,128)S(1)}, f32[64,1024]{1,0:T(8,128)S(1)}, u32[]{:S(2)}, u32[]{:S(2)}) %collective-permute-start.2) | collective-permute-done | bytes 262176 | tf_op jit(solution)/shard_map/ppermute | solution.py:116
  12.3 2.1 %collective-permute-start.4 = (f32[32,1024]{1,0:T(8,128)S(1)}, f32[32,1024]{1,0:T(8,128)S(1)}, u32[]{:S(2)}, u32[]{:S(2)}) collective-permute-start(f32[32,1024]{1,0:T(8,128)S(1)} %get-tuple-element.68), channel_id=1, source_target_pairs={{0,8},{2,6},{4,12},{6,2},{8,0},{10,14},{12,4},{14,10},{16,24},{18,... | collective-permute-start | bytes 393224 | tf_op jit(solution)/shard_map/ppermute | solution.py:116
  14.4 2.0 %rows.9 = (f32[128,1024]{1,0:T(8,128)S(1)}, f32[128,1024]{1,0:T(8,128)S(1)}) custom-call(f32[2,512,256]{2,1,0:T(8,128)S(1)} %bitcast.30, bf16[512,512]{1,0:T(8,128)(2,1)S(1)} %get-tuple-element.28.refs_1_, bf16[512,512]{1,0:T(8,128)(2,1)S(1)} %get-tuple-element.29.refs_2_, f32[2,512,256]{2,1,0:T(8,128)S(1)} %collective-permute-done.value_ref.refs_3_.refs_0_, ...), custom_call_target="tpu_custom_call" | custom-call | flops 1610612736 | bytes 1048576 | tf_op jit(solution)/shard_map/rows/pallas_call | solution.py:254
  16.4 1.6 %collective-permute-start.8 = (f32[128,1024]{1,0:T(8,128)S(1)}, f32[128,1024]{1,0:T(8,128)S(1)}, u32[]{:S(2)}, u32[]{:S(2)}) collective-permute-start(f32[128,1024]{1,0:T(8,128)S(1)} %get-tuple-element.45), channel_id=1, source_target_pairs={{0,4},{2,10},{4,0},{6,14},{8,12},{10,2},{12,8},{14,6},{16,20},{18,... | collective-permute-start | bytes 1572872 | tf_op jit(solution)/shard_map/ppermute | solution.py:116
  18.0 0.8 %collective-permute-done.4 = f32[32,1024]{1,0:T(8,128)S(1)} collective-permute-done((f32[32,1024]{1,0:T(8,128)S(1)}, f32[32,1024]{1,0:T(8,128)S(1)}, u32[]{:S(2)}, u32[]{:S(2)}) %collective-permute-start.4) | collective-permute-done | bytes 131104 | tf_op jit(solution)/shard_map/ppermute | solution.py:116
  18.9 4.1 %collective-permute-start.6 = (f32[16,1024]{1,0:T(8,128)S(1)}, f32[16,1024]{1,0:T(8,128)S(1)}, u32[]{:S(2)}, u32[]{:S(2)}) collective-permute-start(f32[16,1024]{1,0:T(8,128)S(1)} %slice_add_fusion.2), channel_id=1, source_target_pairs={{0,24},{2,18},{4,28},{6,22},{8,16},{10,26},{12,20},{14,30},{16,8},... | collective-permute-start | bytes 196616 | tf_op jit(solution)/shard_map/ppermute | solution.py:116
  23.0 1.1 %rows.8 = (f32[64,1024]{1,0:T(8,128)S(1)}, f32[64,1024]{1,0:T(8,128)S(1)}) custom-call(f32[2,512,256]{2,1,0:T(8,128)S(1)} %bitcast.31, bf16[512,512]{1,0:T(8,128)(2,1)S(1)} %get-tuple-element.28.refs_1_, bf16[512,512]{1,0:T(8,128)(2,1)S(1)} %get-tuple-element.29.refs_2_, f32[2,512,256]{2,1,0:T(8,128)S(1)} %collective-permute-done.value_ref.refs_3_.refs_0_, ...), custom_call_target="tpu_custom_call" | custom-call | flops 805306368 | bytes 1048576 | tf_op jit(solution)/shard_map/rows/pallas_call | solution.py:254
  24.1 1.6 %collective-permute-start.7 = (f32[64,1024]{1,0:T(8,128)S(1)}, f32[64,1024]{1,0:T(8,128)S(1)}, u32[]{:S(2)}, u32[]{:S(2)}) collective-permute-start(f32[64,1024]{1,0:T(8,128)S(1)} %get-tuple-element.43), channel_id=1, source_target_pairs={{0,4},{2,10},{4,0},{6,14},{8,12},{10,2},{12,8},{14,6},{16,20},{18,... | collective-permute-start | bytes 786440 | tf_op jit(solution)/shard_map/ppermute | solution.py:116
  25.6 0.0 collective-permute-done.1.came_ref
  25.6 0.1 halve.6
  25.7 0.1 collective-permute-start.3
  25.8 0.2 collective-permute-done.6
  26.0 0.7 %collective-permute-done.8.came_ref = f32[128,1024]{1,0:T(8,128)S(1)} collective-permute-done((f32[128,1024]{1,0:T(8,128)S(1)}, f32[128,1024]{1,0:T(8,128)S(1)}, u32[]{:S(2)}, u32[]{:S(2)}) %collective-permute-start.8) | collective-permute-done | bytes 524320 | tf_op jit(solution)/shard_map/ppermute | solution.py:116
  26.7 0.1 halve.8
  26.7 2.8 %collective-permute-start.9 = (f32[64,1024]{1,0:T(8,128)S(1)}, f32[64,1024]{1,0:T(8,128)S(1)}, u32[]{:S(2)}, u32[]{:S(2)}) collective-permute-start(f32[64,1024]{1,0:T(8,128)S(1)} %get-tuple-element.48), channel_id=1, source_target_pairs={{0,8},{2,6},{4,12},{6,2},{8,0},{10,14},{12,4},{14,10},{16,24},{18,... | collective-permute-start | bytes 786440 | tf_op jit(solution)/shard_map/ppermute | solution.py:116
  29.5 3.0 %collective-permute-done.3.came_ref = f32[64,1024]{1,0:T(8,128)S(1)} collective-permute-done((f32[64,1024]{1,0:T(8,128)S(1)}, f32[64,1024]{1,0:T(8,128)S(1)}, u32[]{:S(2)}, u32[]{:S(2)}) %collective-permute-start.3) | collective-permute-done | bytes 262176 | tf_op jit(solution)/shard_map/ppermute | solution.py:116
  32.5 2.9 %collective-permute-start.5 = (f32[32,1024]{1,0:T(8,128)S(1)}, f32[32,1024]{1,0:T(8,128)S(1)}, u32[]{:S(2)}, u32[]{:S(2)}) collective-permute-start(f32[32,1024]{1,0:T(8,128)S(1)} %get-tuple-element.41), channel_id=1, source_target_pairs={{0,24},{2,18},{4,28},{6,22},{8,16},{10,26},{12,20},{14,30},{16,8},... | collective-permute-start | bytes 393224 | tf_op jit(solution)/shard_map/ppermute | solution.py:116
  35.5 0.0 collective-permute-done.7.came_ref
  35.5 0.1 collective-permute-start.11
  35.6 4.9 %collective-permute-done.5.came_ref = f32[32,1024]{1,0:T(8,128)S(1)} collective-permute-done((f32[32,1024]{1,0:T(8,128)S(1)}, f32[32,1024]{1,0:T(8,128)S(1)}, u32[]{:S(2)}, u32[]{:S(2)}) %collective-permute-start.5) | collective-permute-done | bytes 131104 | tf_op jit(solution)/shard_map/ppermute | solution.py:116
  40.5 0.0 collective-permute-done.9.came_ref
  40.5 1.9 %collective-permute-start.10 = (f32[32,1024]{1,0:T(8,128)S(1)}, f32[32,1024]{1,0:T(8,128)S(1)}, u32[]{:S(2)}, u32[]{:S(2)}) collective-permute-start(f32[32,1024]{1,0:T(8,128)S(1)} %get-tuple-element.50), channel_id=1, source_target_pairs={{0,24},{2,18},{4,28},{6,22},{8,16},{10,26},{12,20},{14,30},{16,8},... | collective-permute-start | bytes 393224 | tf_op jit(solution)/shard_map/ppermute | solution.py:116
  42.5 0.7 collective-permute-done.11.came_ref
  43.1 0.0 copy-start.3
  43.2 1.9 %collective-permute-start.12 = (f32[16,1024]{1,0:T(8,128)S(1)}, f32[16,1024]{1,0:T(8,128)S(1)}, u32[]{:S(2)}, u32[]{:S(2)}) collective-permute-start(f32[16,1024]{1,0:T(8,128)S(1)} %get-tuple-element.53), channel_id=1, source_target_pairs={{0,24},{2,18},{4,28},{6,22},{8,16},{10,26},{12,20},{14,30},{16,8},... | collective-permute-start | bytes 196616 | tf_op jit(solution)/shard_map/ppermute | solution.py:116
  45.0 0.0 copy-done.3
  45.1 1.6 %collective-permute-start.15 = (f32[48,1024]{1,0:T(8,128)S(1)}, f32[48,1024]{1,0:T(8,128)S(1)}, u32[]{:S(2)}, u32[]{:S(2)}) collective-permute-start(f32[48,1024]{1,0:T(8,128)S(1)} %finish.3.refs_0_.own_ref), channel_id=1, source_target_pairs={{0,1},{1,0},{2,3},{3,2},{4,5},{5,4},{6,7},{7,6},{8,9},{9,8},{10,11... | collective-permute-start | bytes 589832 | tf_op jit(solution)/shard_map/ppermute | solution.py:329
  46.6 0.9 %collective-permute-done.10.came_ref = f32[32,1024]{1,0:T(8,128)S(1)} collective-permute-done((f32[32,1024]{1,0:T(8,128)S(1)}, f32[32,1024]{1,0:T(8,128)S(1)}, u32[]{:S(2)}, u32[]{:S(2)}) %collective-permute-start.10) | collective-permute-done | bytes 131104 | tf_op jit(solution)/shard_map/ppermute | solution.py:116
  47.5 1.6 %collective-permute-start.14 = (f32[32,1024]{1,0:T(8,128)S(1)}, f32[32,1024]{1,0:T(8,128)S(1)}, u32[]{:S(2)}, u32[]{:S(2)}) collective-permute-start(f32[32,1024]{1,0:T(8,128)S(1)} %finish.4.refs_0_.own_ref), channel_id=1, source_target_pairs={{0,1},{1,0},{2,3},{3,2},{4,5},{5,4},{6,7},{7,6},{8,9},{9,8},{10,11... | collective-permute-start | bytes 393224 | tf_op jit(solution)/shard_map/ppermute | solution.py:329
  49.1 0.2 collective-permute-done.12.came_ref
  49.3 1.6 %collective-permute-start.13 = (f32[16,1024]{1,0:T(8,128)S(1)}, f32[16,1024]{1,0:T(8,128)S(1)}, u32[]{:S(2)}, u32[]{:S(2)}) collective-permute-start(f32[16,1024]{1,0:T(8,128)S(1)} %finish.5.own_ref), channel_id=1, source_target_pairs={{0,1},{1,0},{2,3},{3,2},{4,5},{5,4},{6,7},{7,6},{8,9},{9,8},{10,11... | collective-permute-start | bytes 196616 | tf_op jit(solution)/shard_map/ppermute | solution.py:329
  50.9 0.0 collective-permute-done.15.other_ref
  50.9 0.2 table.3.before_ref
  51.1 1.4 %collective-permute-done.14.other_ref = f32[32,1024]{1,0:T(8,128)S(1)} collective-permute-done((f32[32,1024]{1,0:T(8,128)S(1)}, f32[32,1024]{1,0:T(8,128)S(1)}, u32[]{:S(2)}, u32[]{:S(2)}) %collective-permute-start.14) | collective-permute-done | bytes 131104 | tf_op jit(solution)/shard_map/ppermute | solution.py:329
  52.5 0.2 table.4.before_ref
  52.7 0.9 %collective-permute-done.13.other_ref = f32[16,1024]{1,0:T(8,128)S(1)} collective-permute-done((f32[16,1024]{1,0:T(8,128)S(1)}, f32[16,1024]{1,0:T(8,128)S(1)}, u32[]{:S(2)}, u32[]{:S(2)}) %collective-permute-start.13) | collective-permute-done | bytes 65568 | tf_op jit(solution)/shard_map/ppermute | solution.py:329
  53.6 0.1 table.5
  53.8 0.0 collective-permute-start.16
  53.8 1.1 %collective-permute-done.16 = f32[8,128]{1,0:T(8,128)S(1)} collective-permute-done((f32[8,128]{1,0:T(8,128)S(1)}, f32[8,128]{1,0:T(8,128)S(1)}, u32[]{:S(2)}, u32[]{:S(2)}) %collective-permute-start.16) | collective-permute-done | bytes 4128 | tf_op jit(solution)/shard_map/ppermute | solution.py:116
  54.9 1.2 %collective-permute-start.17 = (f32[8,128]{1,0:T(8,128)S(1)}, f32[8,128]{1,0:T(8,128)S(1)}, u32[]{:S(2)}, u32[]{:S(2)}) collective-permute-start(f32[8,128]{1,0:T(8,128)S(1)} %add.183), channel_id=1, source_target_pairs={{0,4},{2,6},{4,0},{6,2},{8,12},{10,14},{12,8},{14,10},{16,20},{18,... | collective-permute-start | bytes 12296 | tf_op jit(solution)/shard_map/ppermute | solution.py:116
  56.1 2.4 %collective-permute-done.17 = f32[8,128]{1,0:T(8,128)S(1)} collective-permute-done((f32[8,128]{1,0:T(8,128)S(1)}, f32[8,128]{1,0:T(8,128)S(1)}, u32[]{:S(2)}, u32[]{:S(2)}) %collective-permute-start.17) | collective-permute-done | bytes 4128 | tf_op jit(solution)/shard_map/ppermute | solution.py:116
  58.5 0.0 collective-permute-start.18
  58.6 3.6 %collective-permute-done.18 = f32[8,128]{1,0:T(8,128)S(1)} collective-permute-done((f32[8,128]{1,0:T(8,128)S(1)}, f32[8,128]{1,0:T(8,128)S(1)}, u32[]{:S(2)}, u32[]{:S(2)}) %collective-permute-start.18) | collective-permute-done | bytes 4128 | tf_op jit(solution)/shard_map/ppermute | solution.py:116
  62.2 0.3 collective-permute-start.19
  62.5 0.8 %maximum_bitcast_fusion = f32[1,96,1024]{2,1,0:T(8,128)} fusion(f32[16,1024]{1,0:T(8,128)S(1)} %finish.5.own_ref, f32[32,1024]{1,0:T(8,128)S(1)} %finish.4.refs_0_.own_ref, f32[48,1024]{1,0:T(8,128)S(1)} %finish.3.refs_0_.own_ref), kind=kLoop, calls=%fused_computation | loop fusion | flops 196608 | bytes 786432 | tf_op jit(solution)/shard_map/broadcast_in_dim | solution.py:348
  63.3 3.4 %collective-permute-done.19 = f32[8,128]{1,0:T(8,128)S(1)} collective-permute-done((f32[8,128]{1,0:T(8,128)S(1)}, f32[8,128]{1,0:T(8,128)S(1)}, u32[]{:S(2)}, u32[]{:S(2)}) %collective-permute-start.19) | collective-permute-done | bytes 4128 | tf_op jit(solution)/shard_map/ppermute | solution.py:116
  66.7 0.7 look_up.1
  (29 shorter events, 0.4 us)
Async XLA Ops:
  0.6 3.8 %collective-permute-start = (f32[2,512,256]{2,1,0:T(8,128)}, f32[2,512,256]{2,1,0:T(8,128)S(1)}, u32[]{:S(2)}, u32[]{:S(2)}) collective-permute-start(f32[2,512,256]{2,1,0:T(8,128)} %bitcast.26), channel_id=1, source_target_pairs={{0,2},{2,0},{4,6},{6,4},{8,10},{10,8},{12,14},{14,12},{16,18},{18,... | collective-permute-start | bytes 3145736 | tf_op jit(solution)/shard_map/ppermute | solution.py:116
  1.3 0.7 %copy-start.2 = (s32[3,3]{1,0:T(4,128)S(1)}, s32[3,3]{1,0:T(4,128)}, u32[]{:S(2)}) copy-start(s32[3,3]{1,0:T(4,128)} %param.4) | copy-start | bytes 112
  2.3 1.2 %copy-start = (f32[1,2,512,256]{3,2,1,0:T(8,128)S(1)}, f32[1,2,512,256]{3,2,1,0:T(8,128)}, u32[]{:S(2)}) copy-start(f32[1,2,512,256]{3,2,1,0:T(8,128)} %param.3) | copy-start | bytes 3145732
  4.6 3.3 %copy-start.1 = (f32[1,2,512,256]{3,2,1,0:T(8,128)S(1)}, f32[1,2,512,256]{3,2,1,0:T(8,128)}, u32[]{:S(2)}) copy-start(f32[1,2,512,256]{3,2,1,0:T(8,128)} %param.3) | copy-start | bytes 3145732
  5.3 7.0 %collective-permute-start.2 = (f32[64,1024]{1,0:T(8,128)S(1)}, f32[64,1024]{1,0:T(8,128)S(1)}, u32[]{:S(2)}, u32[]{:S(2)}) collective-permute-start(f32[64,1024]{1,0:T(8,128)S(1)} %get-tuple-element.37), channel_id=1, source_target_pairs={{0,4},{2,10},{4,0},{6,14},{8,12},{10,2},{12,8},{14,6},{16,20},{18,... | collective-permute-start | bytes 786440 | tf_op jit(solution)/shard_map/ppermute | solution.py:116
  9.9 15.7 %collective-permute-start.1 = (f32[128,1024]{1,0:T(8,128)S(1)}, f32[128,1024]{1,0:T(8,128)S(1)}, u32[]{:S(2)}, u32[]{:S(2)}) collective-permute-start(f32[128,1024]{1,0:T(8,128)S(1)} %get-tuple-element.33), channel_id=1, source_target_pairs={{0,4},{2,10},{4,0},{6,14},{8,12},{10,2},{12,8},{14,6},{16,20},{18,... | collective-permute-start | bytes 1572872 | tf_op jit(solution)/shard_map/ppermute | solution.py:116
  12.3 6.6 %collective-permute-start.4 = (f32[32,1024]{1,0:T(8,128)S(1)}, f32[32,1024]{1,0:T(8,128)S(1)}, u32[]{:S(2)}, u32[]{:S(2)}) collective-permute-start(f32[32,1024]{1,0:T(8,128)S(1)} %get-tuple-element.68), channel_id=1, source_target_pairs={{0,8},{2,6},{4,12},{6,2},{8,0},{10,14},{12,4},{14,10},{16,24},{18,... | collective-permute-start | bytes 393224 | tf_op jit(solution)/shard_map/ppermute | solution.py:116
  16.4 10.2 %collective-permute-start.8 = (f32[128,1024]{1,0:T(8,128)S(1)}, f32[128,1024]{1,0:T(8,128)S(1)}, u32[]{:S(2)}, u32[]{:S(2)}) collective-permute-start(f32[128,1024]{1,0:T(8,128)S(1)} %get-tuple-element.45), channel_id=1, source_target_pairs={{0,4},{2,10},{4,0},{6,14},{8,12},{10,2},{12,8},{14,6},{16,20},{18,... | collective-permute-start | bytes 1572872 | tf_op jit(solution)/shard_map/ppermute | solution.py:116
  18.9 7.1 %collective-permute-start.6 = (f32[16,1024]{1,0:T(8,128)S(1)}, f32[16,1024]{1,0:T(8,128)S(1)}, u32[]{:S(2)}, u32[]{:S(2)}) collective-permute-start(f32[16,1024]{1,0:T(8,128)S(1)} %slice_add_fusion.2), channel_id=1, source_target_pairs={{0,24},{2,18},{4,28},{6,22},{8,16},{10,26},{12,20},{14,30},{16,8},... | collective-permute-start | bytes 196616 | tf_op jit(solution)/shard_map/ppermute | solution.py:116
  24.1 11.4 %collective-permute-start.7 = (f32[64,1024]{1,0:T(8,128)S(1)}, f32[64,1024]{1,0:T(8,128)S(1)}, u32[]{:S(2)}, u32[]{:S(2)}) collective-permute-start(f32[64,1024]{1,0:T(8,128)S(1)} %get-tuple-element.43), channel_id=1, source_target_pairs={{0,4},{2,10},{4,0},{6,14},{8,12},{10,2},{12,8},{14,6},{16,20},{18,... | collective-permute-start | bytes 786440 | tf_op jit(solution)/shard_map/ppermute | solution.py:116
  25.7 6.8 %collective-permute-start.3 = (f32[64,1024]{1,0:T(8,128)S(1)}, f32[64,1024]{1,0:T(8,128)S(1)}, u32[]{:S(2)}, u32[]{:S(2)}) collective-permute-start(f32[64,1024]{1,0:T(8,128)S(1)} %get-tuple-element.39), channel_id=1, source_target_pairs={{0,8},{2,6},{4,12},{6,2},{8,0},{10,14},{12,4},{14,10},{16,24},{18,... | collective-permute-start | bytes 786440 | tf_op jit(solution)/shard_map/ppermute | solution.py:116
  26.7 13.7 %collective-permute-start.9 = (f32[64,1024]{1,0:T(8,128)S(1)}, f32[64,1024]{1,0:T(8,128)S(1)}, u32[]{:S(2)}, u32[]{:S(2)}) collective-permute-start(f32[64,1024]{1,0:T(8,128)S(1)} %get-tuple-element.48), channel_id=1, source_target_pairs={{0,8},{2,6},{4,12},{6,2},{8,0},{10,14},{12,4},{14,10},{16,24},{18,... | collective-permute-start | bytes 786440 | tf_op jit(solution)/shard_map/ppermute | solution.py:116
  32.5 7.9 %collective-permute-start.5 = (f32[32,1024]{1,0:T(8,128)S(1)}, f32[32,1024]{1,0:T(8,128)S(1)}, u32[]{:S(2)}, u32[]{:S(2)}) collective-permute-start(f32[32,1024]{1,0:T(8,128)S(1)} %get-tuple-element.41), channel_id=1, source_target_pairs={{0,24},{2,18},{4,28},{6,22},{8,16},{10,26},{12,20},{14,30},{16,8},... | collective-permute-start | bytes 393224 | tf_op jit(solution)/shard_map/ppermute | solution.py:116
  35.5 7.6 %collective-permute-start.11 = (f32[32,1024]{1,0:T(8,128)S(1)}, f32[32,1024]{1,0:T(8,128)S(1)}, u32[]{:S(2)}, u32[]{:S(2)}) collective-permute-start(f32[32,1024]{1,0:T(8,128)S(1)} %get-tuple-element.51), channel_id=1, source_target_pairs={{0,8},{2,6},{4,12},{6,2},{8,0},{10,14},{12,4},{14,10},{16,24},{18,... | collective-permute-start | bytes 393224 | tf_op jit(solution)/shard_map/ppermute | solution.py:116
  40.5 6.9 %collective-permute-start.10 = (f32[32,1024]{1,0:T(8,128)S(1)}, f32[32,1024]{1,0:T(8,128)S(1)}, u32[]{:S(2)}, u32[]{:S(2)}) collective-permute-start(f32[32,1024]{1,0:T(8,128)S(1)} %get-tuple-element.50), channel_id=1, source_target_pairs={{0,24},{2,18},{4,28},{6,22},{8,16},{10,26},{12,20},{14,30},{16,8},... | collective-permute-start | bytes 393224 | tf_op jit(solution)/shard_map/ppermute | solution.py:116
  43.1 1.9 %copy-start.3 = (s32[64,5]{0,1:T(8,128)S(1)}, s32[64,5]{0,1:T(8,128)}, u32[]{:S(2)}) copy-start(s32[64,5]{0,1:T(8,128)} %param.5) | copy-start | bytes 3844
  43.2 6.1 %collective-permute-start.12 = (f32[16,1024]{1,0:T(8,128)S(1)}, f32[16,1024]{1,0:T(8,128)S(1)}, u32[]{:S(2)}, u32[]{:S(2)}) collective-permute-start(f32[16,1024]{1,0:T(8,128)S(1)} %get-tuple-element.53), channel_id=1, source_target_pairs={{0,24},{2,18},{4,28},{6,22},{8,16},{10,26},{12,20},{14,30},{16,8},... | collective-permute-start | bytes 196616 | tf_op jit(solution)/shard_map/ppermute | solution.py:116
  45.1 5.8 %collective-permute-start.15 = (f32[48,1024]{1,0:T(8,128)S(1)}, f32[48,1024]{1,0:T(8,128)S(1)}, u32[]{:S(2)}, u32[]{:S(2)}) collective-permute-start(f32[48,1024]{1,0:T(8,128)S(1)} %finish.3.refs_0_.own_ref), channel_id=1, source_target_pairs={{0,1},{1,0},{2,3},{3,2},{4,5},{5,4},{6,7},{7,6},{8,9},{9,8},{10,11... | collective-permute-start | bytes 589832 | tf_op jit(solution)/shard_map/ppermute | solution.py:329
  47.5 5.0 %collective-permute-start.14 = (f32[32,1024]{1,0:T(8,128)S(1)}, f32[32,1024]{1,0:T(8,128)S(1)}, u32[]{:S(2)}, u32[]{:S(2)}) collective-permute-start(f32[32,1024]{1,0:T(8,128)S(1)} %finish.4.refs_0_.own_ref), channel_id=1, source_target_pairs={{0,1},{1,0},{2,3},{3,2},{4,5},{5,4},{6,7},{7,6},{8,9},{9,8},{10,11... | collective-permute-start | bytes 393224 | tf_op jit(solution)/shard_map/ppermute | solution.py:329
  49.3 4.3 %collective-permute-start.13 = (f32[16,1024]{1,0:T(8,128)S(1)}, f32[16,1024]{1,0:T(8,128)S(1)}, u32[]{:S(2)}, u32[]{:S(2)}) collective-permute-start(f32[16,1024]{1,0:T(8,128)S(1)} %finish.5.own_ref), channel_id=1, source_target_pairs={{0,1},{1,0},{2,3},{3,2},{4,5},{5,4},{6,7},{7,6},{8,9},{9,8},{10,11... | collective-permute-start | bytes 196616 | tf_op jit(solution)/shard_map/ppermute | solution.py:329
  53.8 1.2 %collective-permute-start.16 = (f32[8,128]{1,0:T(8,128)S(1)}, f32[8,128]{1,0:T(8,128)S(1)}, u32[]{:S(2)}, u32[]{:S(2)}) collective-permute-start(f32[8,128]{1,0:T(8,128)S(1)} %table.5), channel_id=1, source_target_pairs={{0,2},{2,0},{4,6},{6,4},{8,10},{10,8},{12,14},{14,12},{16,18},{18,... | collective-permute-start | bytes 12296 | tf_op jit(solution)/shard_map/ppermute | solution.py:116
  54.9 3.6 %collective-permute-start.17 = (f32[8,128]{1,0:T(8,128)S(1)}, f32[8,128]{1,0:T(8,128)S(1)}, u32[]{:S(2)}, u32[]{:S(2)}) collective-permute-start(f32[8,128]{1,0:T(8,128)S(1)} %add.183), channel_id=1, source_target_pairs={{0,4},{2,6},{4,0},{6,2},{8,12},{10,14},{12,8},{14,10},{16,20},{18,... | collective-permute-start | bytes 12296 | tf_op jit(solution)/shard_map/ppermute | solution.py:116
  58.5 3.6 %collective-permute-start.18 = (f32[8,128]{1,0:T(8,128)S(1)}, f32[8,128]{1,0:T(8,128)S(1)}, u32[]{:S(2)}, u32[]{:S(2)}) collective-permute-start(f32[8,128]{1,0:T(8,128)S(1)} %add.184), channel_id=1, source_target_pairs={{0,8},{2,10},{4,12},{6,14},{8,0},{10,2},{12,4},{14,6},{16,24},{18,... | collective-permute-start | bytes 12296 | tf_op jit(solution)/shard_map/ppermute | solution.py:116
  62.2 4.5 %collective-permute-start.19 = (f32[8,128]{1,0:T(8,128)S(1)}, f32[8,128]{1,0:T(8,128)S(1)}, u32[]{:S(2)}, u32[]{:S(2)}) collective-permute-start(f32[8,128]{1,0:T(8,128)S(1)} %add.185), channel_id=1, source_target_pairs={{0,16},{2,18},{4,20},{6,22},{8,24},{10,26},{12,28},{14,30},{16,0},... | collective-permute-start | bytes 12296 | tf_op jit(solution)/shard_map/ppermute | solution.py:116

commit v4 on v3

--- a/solution.py
+++ b/solution.py
@@ -82,13 +82,12 @@
 
 
 CORE, Y, Z_NEAR, Z_FAR = 1, 2, 4, 8
-FAR = (Z_FAR | Z_NEAR, Z_FAR)
-STEPS = {
-    "both": ((Y, Z_NEAR), (Z_NEAR, Y), FAR),
-    "y": ((Y, Y), (Z_NEAR, Z_NEAR), FAR),
-    "z": ((Z_NEAR, Z_NEAR), (Y, Y), FAR),
-}
-KINDS = ("both",) * 4
+STEPS = (
+    ((Y, Z_NEAR), (Z_NEAR, Y), (Z_FAR | Z_NEAR, Z_FAR)),
+    ((Y, Z_NEAR), (Z_NEAR, Y), (Z_FAR | Z_NEAR, Z_FAR)),
+    ((Y, Z_NEAR), (Z_NEAR, Y), (Z_FAR | Z_NEAR, Z_FAR)),
+    ((Y, Z_NEAR), (Z_NEAR, Y), (Z_FAR, Z_FAR)),
+)
 CHUNKS = (16, 32, 32, 16)
 GROUPS = ((0, 1), (2,), (3,))
 PLAN = (
@@ -97,10 +96,9 @@
     ("table", 0), ("table", 1), ("table", 2),
 )
 AFTER = {
+    ("rows", 1): (("rows", 0),),
     ("add", 1, 0): (("add", 0, 0),),
-    ("rows", 2): (("add", 1, 0),),
     ("add", 1, 1): (("add", 0, 1),),
-    ("rows", 3): (("add", 1, 1),),
     ("add", 2, 0): (("add", 0, 2),),
     ("add", 3, 0): (("add", 2, 0),),
     ("add", 1, 2): (("add", 3, 0),),
@@ -121,20 +119,17 @@
     return high, (value - high.astype(jnp.float32)).astype(jnp.bfloat16)
 
 
-def split_kernel(value_ref, *refs):
-    high_ref, low_ref = refs[-2:]
+def split_kernel(value_ref, high_ref, low_ref):
     sites = value_ref.shape[2]
     for part in range(2):
         columns = slice(part * sites, (part + 1) * sites)
         high_ref[:, columns], low_ref[:, columns] = in_two(value_ref[part])
 
 
-def rows_kernel(offset, rows, own_rows, steps, sources, started, *refs):
-    refs = list(refs)
-    inputs = [tuple(refs.pop(0) for _ in range(3)) for _ in sources]
-    cos_ref, sin_ref = refs.pop(0), refs.pop(0)
-    before = (refs.pop(0), refs.pop(0)) if started else None
-    send_ref, keep_ref, left_ref = refs
+def rows_kernel(offset, rows, own_rows, steps, count, *refs):
+    inputs = [refs[3 * source : 3 * source + 3] for source in range(count)]
+    cos_ref, sin_ref = refs[3 * count : 3 * count + 2]
+    send_ref, keep_ref, left_ref = refs[-3:]
     me = lax.axis_index("space")
     masks = [jnp.where(me % 2 == 0, even, odd) for even, odd in steps]
     at = 0
@@ -146,11 +141,11 @@
                     start = block * own_rows + (offset + 8 * group)
                     phase = start // MODES
                     mode = pl.multiple_of(start - phase * MODES, 8)
-                    for place, (source, (ref, _, _)) in enumerate(zip(sources, inputs)):
+                    for place, (ref, _, _) in enumerate(inputs):
                         real = ref[0, pl.ds(mode, 8), :]
                         imag = ref[1, pl.ds(mode, 8), :]
-                        cosine = cos_ref[source, pl.ds(phase, 1), :]
-                        sine = sin_ref[source, pl.ds(phase, 1), :]
+                        cosine = cos_ref[place, pl.ds(phase, 1), :]
+                        sine = sin_ref[place, pl.ds(phase, 1), :]
                         left_ref[2 * place, at : at + 8, :] = real * cosine + imag * sine
                         left_ref[2 * place + 1, at : at + 8, :] = real * sine - imag * cosine
                     at += 8
@@ -174,8 +169,7 @@
     for column in range(2):
         columns = slice(column * MODES, (column + 1) * MODES)
         for place, ref in enumerate((send_ref, keep_ref)):
-            part = out[column * at + place * half : column * at + (place + 1) * half]
-            ref[:, columns] = part + before[place][:, columns] if started else part
+            ref[:, columns] = out[column * at + place * half : column * at + (place + 1) * half]
 
 
 def halve_kernel(keep_ref, came_ref, *refs):
@@ -278,22 +272,22 @@
     cosine, sine = (jnp.swapaxes(f(angle).reshape(PHASES, 2, sites), 0, 1) for f in (jnp.cos, jnp.sin))
     other = swap(own, (CORE, CORE))
     halves = [jax.ShapeDtypeStruct((MODES, 2 * sites), jnp.bfloat16)] * 2
-    mine = own, *kernel_call(split_kernel, "split", [own], halves, (cosine, sine))
-
-    def products(chunk, sources, inputs, started=()):
+    mine = own, *kernel_call(split_kernel, "split", [own], halves)
+
+    def products(chunk, inputs, after):
         rows = CHUNKS[chunk]
         depth = 4 * rows
-        ins = [a for i in inputs for a in i] + [cosine, sine, *started]
+        ins = [a for i in inputs for a in i] + [cosine, sine]
         return kernel_call(
-            functools.partial(rows_kernel, sum(CHUNKS[:chunk]), rows, own_rows, STEPS[KINDS[chunk]], sources, bool(started)),
+            functools.partial(rows_kernel, sum(CHUNKS[:chunk]), rows, own_rows, STEPS[chunk], len(inputs)),
             "rows",
             ins,
             [floats(depth, 2 * MODES)] * 2,
-            scratch=[pltpu.VMEM((2 * len(sources), 2 * depth, sites), jnp.float32)],
-            flops=2 * 3 * 4 * depth * MODES * 2 * sites * len(sources),
+            after,
+            scratch=[pltpu.VMEM((2 * len(inputs), 2 * depth, sites), jnp.float32)],
+            flops=2 * 3 * 4 * depth * MODES * 2 * sites * len(inputs),
         )
 
-    begun = products(0, (0,), (mine,))
     theirs = other, *kernel_call(split_kernel, "split", [other], halves)
     keeps, flights, groups, tokens = {}, {}, {}, {}
     table = jnp.zeros((8, 128), jnp.float32)
@@ -301,11 +295,9 @@
         kind, which = event[:2]
         after = [tokens[e] for e in AFTER.get(event, ())]
         if kind == "rows":
-            if which == 0:
-                send, keep = products(0, (1,), (theirs,), begun)
-            else:
-                send, keep = products(which, (0, 1), (mine, theirs))
-            keeps[which], flights[which] = keep, swap(send, STEPS[KINDS[which]][0])
+            send, keep = products(which, (mine, theirs), after)
+            tokens[event] = keep
+            keeps[which], flights[which] = keep, swap(send, STEPS[which][0])
         elif kind == "add" and event[2] < 2:
             keep, came = keeps[which], flights[which]
             half = keep.shape[0] // 2
@@ -314,7 +306,7 @@
             else:
                 send, keep = keep[:half] + came[:half], keep[half:] + came[half:]
             tokens[event] = keep
-            keeps[which], flights[which] = keep, swap(send, STEPS[KINDS[which]][event[2] + 1])
+            keeps[which], flights[which] = keep, swap(send, STEPS[which][event[2] + 1])
         elif kind == "add":
             group = next(g for g in GROUPS if which in g)
             keep, came = keeps[which], flights[which]
@@ -336,7 +328,7 @@
                 [TOKEN],
                 after,
             )
-    for bit in (CORE, Y, Z_NEAR, Z_FAR):
+    for bit in (CORE, Z_NEAR, Y, Z_FAR):
         table = table + swap(table, (bit, bit))
     tile, one, two, phase = (diagrams[:, i] for i in range(4))
     column = 4 * (tile % tiles_per)

time: 67.5 us -> 67.2 us (level)
  starting transfers between devices: 28.9 us -> 27.1 us
  waiting for transfers between devices: 26.1 us -> 27.3 us
    ppermute x17, starting transfers between devices: 24.3 us -> 22.6 us  [swap(): lax.ppermute(array, 'space', [(i, i ^ masks[i % 2]) for i in range(count)])]
    ppermute x17, waiting for transfers between devices: 23.7 us -> 24.7 us  [swap(): lax.ppermute(array, 'space', [(i, i ^ masks[i % 2]) for i in range(count)])]
    pallas_call x20 -> x19, Pallas kernels: 8.13 us -> 7.89 us  [kernel_call(): pl.pallas_call(body, out_shape=outs, in_specs=[VMEM_SPEC] * len(ins) + [A...]
  transfers between devices with their start and end apart: 20 -> 20, of which waited for: 15 -> 14; matrix products, arithmetic and copies ran while one was open for 2% -> 2% of each run, Pallas kernels for 10% -> 9%
where the time goes in v4:
time: 67.2 us; the launch traced here: 67 us
  waiting for transfers between devices  27.3 us (41%)
  starting transfers between devices  27.1 us (40%)
  Pallas kernels  7.89 us (12%)
  local copies, waits for them, and re-layouts  2.74 us (4%)
  other arithmetic  1.13 us (2%)
  between operations  0.84 us (1%)
    ppermute x17, waiting for transfers between devices, swap(): lax.ppermute(array, 'space', [(i, i ^ masks[i % 2]) for i in range(count)])  24.7 us
    ppermute x17, starting transfers between devices, swap(): lax.ppermute(array, 'space', [(i, i ^ masks[i % 2]) for i in range(count)])  22.6 us
    pallas_call x19, Pallas kernels, kernel_call(): pl.pallas_call(body, out_shape=outs, in_specs=[VMEM_SPEC] * len(ins) + [A...  7.89 us
    ppermute x3, starting transfers between devices, halving(): flights[group] = lax.ppermute(done, 'cuts', [(0, 1), (1, 0)])  4.49 us
    ppermute x3, waiting for transfers between devices, halving(): flights[group] = lax.ppermute(done, 'cuts', [(0, 1), (1, 0)])  2.58 us
    unnamed x8, local copies, waits for them, and re-layouts  2.48 us
  transfers between devices with their start and end apart: 20, of which 14 were waited for; matrix products, arithmetic and copies ran while one was open for 2% of the time, Pallas kernels for 9%

profile of v4, /device:TPU:0, one launch (start us, length us, event | category | flops | bytes accessed | tf_op | source)
XLA Modules:
  0.0 67.0 jit_solution(15289548024331986087)
XLA Ops:
  0.6 0.5 collective-permute-start
  1.1 0.0 copy-start
  1.1 1.2 %copy-done = f32[1,2,512,256]{3,2,1,0:T(8,128)S(1)} copy-done((f32[1,2,512,256]{3,2,1,0:T(8,128)S(1)}, f32[1,2,512,256]{3,2,1,0:T(8,128)}, u32[]{:S(2)}) %copy-start) | copy-done | bytes 1048600
  2.4 0.0 copy-start.1
  2.4 0.2 split.2
  2.7 0.0 copy-start.2
  2.7 0.7 copy-done.2
  3.4 0.2 slice_reduce_fusion.2
  3.6 0.2 fusion.3
  3.8 0.0 collective-permute-done.value_ref.refs_3_
  3.8 0.2 split.3
  4.0 0.0 copy-done.1
  4.0 1.1 %rows.4 = (f32[64,1024]{1,0:T(8,128)S(1)}, f32[64,1024]{1,0:T(8,128)S(1)}) custom-call(f32[2,512,256]{2,1,0:T(8,128)S(1)} %bitcast.28, bf16[512,512]{1,0:T(8,128)(2,1)S(1)} %get-tuple-element.26.refs_1_, bf16[512,512]{1,0:T(8,128)(2,1)S(1)} %get-tuple-element.27.refs_2_, f32[2,512,256]{2,1,0:T(8,128)S(1)} %collective-permute-done.value_ref.refs_3_, ...), custom_call_target="tpu_custom_call" | custom-call | flops 805306368 | bytes 1048576 | tf_op jit(solution)/shard_map/rows/pallas_call | solution.py:248
  5.1 2.8 %collective-permute-start.2 = (f32[64,1024]{1,0:T(8,128)S(1)}, f32[64,1024]{1,0:T(8,128)S(1)}, u32[]{:S(2)}, u32[]{:S(2)}) collective-permute-start(f32[64,1024]{1,0:T(8,128)S(1)} %get-tuple-element.33), channel_id=1, source_target_pairs={{0,4},{2,10},{4,0},{6,14},{8,12},{10,2},{12,8},{14,6},{16,20},{18,... | collective-permute-start | bytes 786440 | tf_op jit(solution)/shard_map/ppermute | solution.py:114
  7.9 2.0 %rows.5 = (f32[128,1024]{1,0:T(8,128)S(1)}, f32[128,1024]{1,0:T(8,128)S(1)}) custom-call(f32[2,512,256]{2,1,0:T(8,128)S(1)} %bitcast.29, bf16[512,512]{1,0:T(8,128)(2,1)S(1)} %get-tuple-element.26.refs_1_, bf16[512,512]{1,0:T(8,128)(2,1)S(1)} %get-tuple-element.27.refs_2_, f32[2,512,256]{2,1,0:T(8,128)S(1)} %collective-permute-done.value_ref.refs_3_, ...), custom_call_target="tpu_custom_call" | custom-call | flops 1610612736 | bytes 1048576 | tf_op jit(solution)/shard_map/rows/pallas_call | solution.py:248
  9.9 0.1 collective-permute-start.1
  10.0 2.3 %collective-permute-done.2 = f32[64,1024]{1,0:T(8,128)S(1)} collective-permute-done((f32[64,1024]{1,0:T(8,128)S(1)}, f32[64,1024]{1,0:T(8,128)S(1)}, u32[]{:S(2)}, u32[]{:S(2)}) %collective-permute-start.2) | collective-permute-done | bytes 262176 | tf_op jit(solution)/shard_map/ppermute | solution.py:114
  12.3 2.1 %collective-permute-start.4 = (f32[32,1024]{1,0:T(8,128)S(1)}, f32[32,1024]{1,0:T(8,128)S(1)}, u32[]{:S(2)}, u32[]{:S(2)}) collective-permute-start(f32[32,1024]{1,0:T(8,128)S(1)} %get-tuple-element.64), channel_id=1, source_target_pairs={{0,8},{2,6},{4,12},{6,2},{8,0},{10,14},{12,4},{14,10},{16,24},{18,... | collective-permute-start | bytes 393224 | tf_op jit(solution)/shard_map/ppermute | solution.py:114
  14.4 2.0 %rows.7 = (f32[128,1024]{1,0:T(8,128)S(1)}, f32[128,1024]{1,0:T(8,128)S(1)}) custom-call(f32[2,512,256]{2,1,0:T(8,128)S(1)} %bitcast.30, bf16[512,512]{1,0:T(8,128)(2,1)S(1)} %get-tuple-element.26.refs_1_, bf16[512,512]{1,0:T(8,128)(2,1)S(1)} %get-tuple-element.27.refs_2_, f32[2,512,256]{2,1,0:T(8,128)S(1)} %collective-permute-done.value_ref.refs_3_, ...), custom_call_target="tpu_custom_call" | custom-call | flops 1610612736 | bytes 1048576 | tf_op jit(solution)/shard_map/rows/pallas_call | solution.py:248
  16.4 1.6 %collective-permute-start.8 = (f32[128,1024]{1,0:T(8,128)S(1)}, f32[128,1024]{1,0:T(8,128)S(1)}, u32[]{:S(2)}, u32[]{:S(2)}) collective-permute-start(f32[128,1024]{1,0:T(8,128)S(1)} %get-tuple-element.41), channel_id=1, source_target_pairs={{0,4},{2,10},{4,0},{6,14},{8,12},{10,2},{12,8},{14,6},{16,20},{18,... | collective-permute-start | bytes 1572872 | tf_op jit(solution)/shard_map/ppermute | solution.py:114
  18.0 0.8 %collective-permute-done.4 = f32[32,1024]{1,0:T(8,128)S(1)} collective-permute-done((f32[32,1024]{1,0:T(8,128)S(1)}, f32[32,1024]{1,0:T(8,128)S(1)}, u32[]{:S(2)}, u32[]{:S(2)}) %collective-permute-start.4) | collective-permute-done | bytes 131104 | tf_op jit(solution)/shard_map/ppermute | solution.py:114
  18.8 4.1 %collective-permute-start.6 = (f32[16,1024]{1,0:T(8,128)S(1)}, f32[16,1024]{1,0:T(8,128)S(1)}, u32[]{:S(2)}, u32[]{:S(2)}) collective-permute-start(f32[16,1024]{1,0:T(8,128)S(1)} %slice_add_fusion.2), channel_id=1, source_target_pairs={{0,24},{2,18},{4,28},{6,22},{8,16},{10,26},{12,20},{14,30},{16,8},... | collective-permute-start | bytes 196616 | tf_op jit(solution)/shard_map/ppermute | solution.py:114
  22.9 1.1 %rows.6 = (f32[64,1024]{1,0:T(8,128)S(1)}, f32[64,1024]{1,0:T(8,128)S(1)}) custom-call(f32[2,512,256]{2,1,0:T(8,128)S(1)} %bitcast.31, bf16[512,512]{1,0:T(8,128)(2,1)S(1)} %get-tuple-element.26.refs_1_, bf16[512,512]{1,0:T(8,128)(2,1)S(1)} %get-tuple-element.27.refs_2_, f32[2,512,256]{2,1,0:T(8,128)S(1)} %collective-permute-done.value_ref.refs_3_, ...), custom_call_target="tpu_custom_call" | custom-call | flops 805306368 | bytes 1048576 | tf_op jit(solution)/shard_map/rows/pallas_call | solution.py:248
  24.0 1.6 %collective-permute-start.7 = (f32[64,1024]{1,0:T(8,128)S(1)}, f32[64,1024]{1,0:T(8,128)S(1)}, u32[]{:S(2)}, u32[]{:S(2)}) collective-permute-start(f32[64,1024]{1,0:T(8,128)S(1)} %get-tuple-element.39), channel_id=1, source_target_pairs={{0,4},{2,10},{4,0},{6,14},{8,12},{10,2},{12,8},{14,6},{16,20},{18,... | collective-permute-start | bytes 786440 | tf_op jit(solution)/shard_map/ppermute | solution.py:114
  25.6 0.0 collective-permute-done.1.came_ref
  25.6 0.1 halve.6
  25.7 0.1 collective-permute-start.3
  25.8 0.2 collective-permute-done.6
  26.0 0.9 %collective-permute-done.8.came_ref = f32[128,1024]{1,0:T(8,128)S(1)} collective-permute-done((f32[128,1024]{1,0:T(8,128)S(1)}, f32[128,1024]{1,0:T(8,128)S(1)}, u32[]{:S(2)}, u32[]{:S(2)}) %collective-permute-start.8) | collective-permute-done | bytes 524320 | tf_op jit(solution)/shard_map/ppermute | solution.py:114
  26.9 0.1 halve.8
  26.9 2.8 %collective-permute-start.9 = (f32[64,1024]{1,0:T(8,128)S(1)}, f32[64,1024]{1,0:T(8,128)S(1)}, u32[]{:S(2)}, u32[]{:S(2)}) collective-permute-start(f32[64,1024]{1,0:T(8,128)S(1)} %get-tuple-element.44), channel_id=1, source_target_pairs={{0,8},{2,6},{4,12},{6,2},{8,0},{10,14},{12,4},{14,10},{16,24},{18,... | collective-permute-start | bytes 786440 | tf_op jit(solution)/shard_map/ppermute | solution.py:114
  29.7 2.6 %collective-permute-done.3.came_ref = f32[64,1024]{1,0:T(8,128)S(1)} collective-permute-done((f32[64,1024]{1,0:T(8,128)S(1)}, f32[64,1024]{1,0:T(8,128)S(1)}, u32[]{:S(2)}, u32[]{:S(2)}) %collective-permute-start.3) | collective-permute-done | bytes 262176 | tf_op jit(solution)/shard_map/ppermute | solution.py:114
  32.3 3.1 %collective-permute-start.5 = (f32[32,1024]{1,0:T(8,128)S(1)}, f32[32,1024]{1,0:T(8,128)S(1)}, u32[]{:S(2)}, u32[]{:S(2)}) collective-permute-start(f32[32,1024]{1,0:T(8,128)S(1)} %get-tuple-element.37), channel_id=1, source_target_pairs={{0,24},{2,18},{4,28},{6,22},{8,16},{10,26},{12,20},{14,30},{16,8},... | collective-permute-start | bytes 393224 | tf_op jit(solution)/shard_map/ppermute | solution.py:114
  35.4 0.0 collective-permute-done.7.came_ref
  35.4 0.1 collective-permute-start.11
  35.5 5.0 %collective-permute-done.5.came_ref = f32[32,1024]{1,0:T(8,128)S(1)} collective-permute-done((f32[32,1024]{1,0:T(8,128)S(1)}, f32[32,1024]{1,0:T(8,128)S(1)}, u32[]{:S(2)}, u32[]{:S(2)}) %collective-permute-start.5) | collective-permute-done | bytes 131104 | tf_op jit(solution)/shard_map/ppermute | solution.py:114
  40.5 0.0 collective-permute-done.9.came_ref
  40.6 1.8 %collective-permute-start.10 = (f32[32,1024]{1,0:T(8,128)S(1)}, f32[32,1024]{1,0:T(8,128)S(1)}, u32[]{:S(2)}, u32[]{:S(2)}) collective-permute-start(f32[32,1024]{1,0:T(8,128)S(1)} %get-tuple-element.46), channel_id=1, source_target_pairs={{0,24},{2,18},{4,28},{6,22},{8,16},{10,26},{12,20},{14,30},{16,8},... | collective-permute-start | bytes 393224 | tf_op jit(solution)/shard_map/ppermute | solution.py:114
  42.4 0.7 %collective-permute-done.11.came_ref = f32[32,1024]{1,0:T(8,128)S(1)} collective-permute-done((f32[32,1024]{1,0:T(8,128)S(1)}, f32[32,1024]{1,0:T(8,128)S(1)}, u32[]{:S(2)}, u32[]{:S(2)}) %collective-permute-start.11) | collective-permute-done | bytes 131104 | tf_op jit(solution)/shard_map/ppermute | solution.py:114
  43.1 0.0 copy-start.3
  43.2 0.1 collective-permute-start.12
  43.2 0.6 copy-done.3
  43.8 1.6 %collective-permute-start.15 = (f32[48,1024]{1,0:T(8,128)S(1)}, f32[48,1024]{1,0:T(8,128)S(1)}, u32[]{:S(2)}, u32[]{:S(2)}) collective-permute-start(f32[48,1024]{1,0:T(8,128)S(1)} %finish.3.refs_0_.own_ref), channel_id=1, source_target_pairs={{0,1},{1,0},{2,3},{3,2},{4,5},{5,4},{6,7},{7,6},{8,9},{9,8},{10,11... | collective-permute-start | bytes 589832 | tf_op jit(solution)/shard_map/ppermute | solution.py:321
  45.4 2.0 %collective-permute-done.10.came_ref = f32[32,1024]{1,0:T(8,128)S(1)} collective-permute-done((f32[32,1024]{1,0:T(8,128)S(1)}, f32[32,1024]{1,0:T(8,128)S(1)}, u32[]{:S(2)}, u32[]{:S(2)}) %collective-permute-start.10) | collective-permute-done | bytes 131104 | tf_op jit(solution)/shard_map/ppermute | solution.py:114
  47.4 1.6 %collective-permute-start.14 = (f32[32,1024]{1,0:T(8,128)S(1)}, f32[32,1024]{1,0:T(8,128)S(1)}, u32[]{:S(2)}, u32[]{:S(2)}) collective-permute-start(f32[32,1024]{1,0:T(8,128)S(1)} %finish.4.refs_0_.own_ref), channel_id=1, source_target_pairs={{0,1},{1,0},{2,3},{3,2},{4,5},{5,4},{6,7},{7,6},{8,9},{9,8},{10,11... | collective-permute-start | bytes 393224 | tf_op jit(solution)/shard_map/ppermute | solution.py:321
  49.0 0.0 collective-permute-done.12.came_ref
  49.0 1.4 %collective-permute-start.13 = (f32[16,1024]{1,0:T(8,128)S(1)}, f32[16,1024]{1,0:T(8,128)S(1)}, u32[]{:S(2)}, u32[]{:S(2)}) collective-permute-start(f32[16,1024]{1,0:T(8,128)S(1)} %finish.5.own_ref), channel_id=1, source_target_pairs={{0,1},{1,0},{2,3},{3,2},{4,5},{5,4},{6,7},{7,6},{8,9},{9,8},{10,11... | collective-permute-start | bytes 196616 | tf_op jit(solution)/shard_map/ppermute | solution.py:321
  50.4 0.0 collective-permute-done.15.other_ref
  50.4 0.2 table.3.before_ref
  50.6 1.9 %collective-permute-done.14.other_ref = f32[32,1024]{1,0:T(8,128)S(1)} collective-permute-done((f32[32,1024]{1,0:T(8,128)S(1)}, f32[32,1024]{1,0:T(8,128)S(1)}, u32[]{:S(2)}, u32[]{:S(2)}) %collective-permute-start.14) | collective-permute-done | bytes 131104 | tf_op jit(solution)/shard_map/ppermute | solution.py:321
  52.4 0.2 table.4.before_ref
  52.6 0.7 %collective-permute-done.13.other_ref = f32[16,1024]{1,0:T(8,128)S(1)} collective-permute-done((f32[16,1024]{1,0:T(8,128)S(1)}, f32[16,1024]{1,0:T(8,128)S(1)}, u32[]{:S(2)}, u32[]{:S(2)}) %collective-permute-start.13) | collective-permute-done | bytes 65568 | tf_op jit(solution)/shard_map/ppermute | solution.py:321
  53.3 0.1 table.5
  53.4 0.0 collective-permute-start.16
  53.5 1.1 %collective-permute-done.16 = f32[8,128]{1,0:T(8,128)S(1)} collective-permute-done((f32[8,128]{1,0:T(8,128)S(1)}, f32[8,128]{1,0:T(8,128)S(1)}, u32[]{:S(2)}, u32[]{:S(2)}) %collective-permute-start.16) | collective-permute-done | bytes 4128 | tf_op jit(solution)/shard_map/ppermute | solution.py:114
  54.6 0.0 collective-permute-start.17
  54.6 3.6 %collective-permute-done.17 = f32[8,128]{1,0:T(8,128)S(1)} collective-permute-done((f32[8,128]{1,0:T(8,128)S(1)}, f32[8,128]{1,0:T(8,128)S(1)}, u32[]{:S(2)}, u32[]{:S(2)}) %collective-permute-start.17) | collective-permute-done | bytes 4128 | tf_op jit(solution)/shard_map/ppermute | solution.py:114
  58.2 1.1 %collective-permute-start.18 = (f32[8,128]{1,0:T(8,128)S(1)}, f32[8,128]{1,0:T(8,128)S(1)}, u32[]{:S(2)}, u32[]{:S(2)}) collective-permute-start(f32[8,128]{1,0:T(8,128)S(1)} %add.184), channel_id=1, source_target_pairs={{0,4},{2,6},{4,0},{6,2},{8,12},{10,14},{12,8},{14,10},{16,20},{18,... | collective-permute-start | bytes 12296 | tf_op jit(solution)/shard_map/ppermute | solution.py:114
  59.4 2.5 %collective-permute-done.18 = f32[8,128]{1,0:T(8,128)S(1)} collective-permute-done((f32[8,128]{1,0:T(8,128)S(1)}, f32[8,128]{1,0:T(8,128)S(1)}, u32[]{:S(2)}, u32[]{:S(2)}) %collective-permute-start.18) | collective-permute-done | bytes 4128 | tf_op jit(solution)/shard_map/ppermute | solution.py:114
  61.8 0.7 %collective-permute-start.19 = (f32[8,128]{1,0:T(8,128)S(1)}, f32[8,128]{1,0:T(8,128)S(1)}, u32[]{:S(2)}, u32[]{:S(2)}) collective-permute-start(f32[8,128]{1,0:T(8,128)S(1)} %add.185), channel_id=1, source_target_pairs={{0,16},{2,18},{4,20},{6,22},{8,24},{10,26},{12,28},{14,30},{16,0},... | collective-permute-start | bytes 12296 | tf_op jit(solution)/shard_map/ppermute | solution.py:114
  62.5 0.8 %maximum_bitcast_fusion = f32[1,96,1024]{2,1,0:T(8,128)} fusion(f32[16,1024]{1,0:T(8,128)S(1)} %finish.5.own_ref, f32[32,1024]{1,0:T(8,128)S(1)} %finish.4.refs_0_.own_ref, f32[48,1024]{1,0:T(8,128)S(1)} %finish.3.refs_0_.own_ref), kind=kLoop, calls=%fused_computation | loop fusion | flops 196608 | bytes 786432 | tf_op jit(solution)/shard_map/broadcast_in_dim | solution.py:340
  63.3 3.0 %collective-permute-done.19 = f32[8,128]{1,0:T(8,128)S(1)} collective-permute-done((f32[8,128]{1,0:T(8,128)S(1)}, f32[8,128]{1,0:T(8,128)S(1)}, u32[]{:S(2)}, u32[]{:S(2)}) %collective-permute-start.19) | collective-permute-done | bytes 4128 | tf_op jit(solution)/shard_map/ppermute | solution.py:114
  66.3 0.7 look_up.1
  (29 shorter events, 0.4 us)
Async XLA Ops:
  0.6 3.1 %collective-permute-start = (f32[2,512,256]{2,1,0:T(8,128)}, f32[2,512,256]{2,1,0:T(8,128)S(1)}, u32[]{:S(2)}, u32[]{:S(2)}) collective-permute-start(f32[2,512,256]{2,1,0:T(8,128)} %bitcast.26), channel_id=1, source_target_pairs={{0,2},{2,0},{4,6},{6,4},{8,10},{10,8},{12,14},{14,12},{16,18},{18,... | collective-permute-start | bytes 3145736 | tf_op jit(solution)/shard_map/ppermute | solution.py:114
  1.1 1.2 %copy-start = (f32[1,2,512,256]{3,2,1,0:T(8,128)S(1)}, f32[1,2,512,256]{3,2,1,0:T(8,128)}, u32[]{:S(2)}) copy-start(f32[1,2,512,256]{3,2,1,0:T(8,128)} %param.3) | copy-start | bytes 3145732
  2.4 1.6 %copy-start.1 = (f32[1,2,512,256]{3,2,1,0:T(8,128)S(1)}, f32[1,2,512,256]{3,2,1,0:T(8,128)}, u32[]{:S(2)}) copy-start(f32[1,2,512,256]{3,2,1,0:T(8,128)} %param.3) | copy-start | bytes 3145732
  2.7 0.7 %copy-start.2 = (s32[3,3]{1,0:T(4,128)S(1)}, s32[3,3]{1,0:T(4,128)}, u32[]{:S(2)}) copy-start(s32[3,3]{1,0:T(4,128)} %param.4) | copy-start | bytes 112
  5.1 7.2 %collective-permute-start.2 = (f32[64,1024]{1,0:T(8,128)S(1)}, f32[64,1024]{1,0:T(8,128)S(1)}, u32[]{:S(2)}, u32[]{:S(2)}) collective-permute-start(f32[64,1024]{1,0:T(8,128)S(1)} %get-tuple-element.33), channel_id=1, source_target_pairs={{0,4},{2,10},{4,0},{6,14},{8,12},{10,2},{12,8},{14,6},{16,20},{18,... | collective-permute-start | bytes 786440 | tf_op jit(solution)/shard_map/ppermute | solution.py:114
  9.9 15.7 %collective-permute-start.1 = (f32[128,1024]{1,0:T(8,128)S(1)}, f32[128,1024]{1,0:T(8,128)S(1)}, u32[]{:S(2)}, u32[]{:S(2)}) collective-permute-start(f32[128,1024]{1,0:T(8,128)S(1)} %get-tuple-element.32), channel_id=1, source_target_pairs={{0,4},{2,10},{4,0},{6,14},{8,12},{10,2},{12,8},{14,6},{16,20},{18,... | collective-permute-start | bytes 1572872 | tf_op jit(solution)/shard_map/ppermute | solution.py:114
  12.3 6.6 %collective-permute-start.4 = (f32[32,1024]{1,0:T(8,128)S(1)}, f32[32,1024]{1,0:T(8,128)S(1)}, u32[]{:S(2)}, u32[]{:S(2)}) collective-permute-start(f32[32,1024]{1,0:T(8,128)S(1)} %get-tuple-element.64), channel_id=1, source_target_pairs={{0,8},{2,6},{4,12},{6,2},{8,0},{10,14},{12,4},{14,10},{16,24},{18,... | collective-permute-start | bytes 393224 | tf_op jit(solution)/shard_map/ppermute | solution.py:114
  16.4 10.5 %collective-permute-start.8 = (f32[128,1024]{1,0:T(8,128)S(1)}, f32[128,1024]{1,0:T(8,128)S(1)}, u32[]{:S(2)}, u32[]{:S(2)}) collective-permute-start(f32[128,1024]{1,0:T(8,128)S(1)} %get-tuple-element.41), channel_id=1, source_target_pairs={{0,4},{2,10},{4,0},{6,14},{8,12},{10,2},{12,8},{14,6},{16,20},{18,... | collective-permute-start | bytes 1572872 | tf_op jit(solution)/shard_map/ppermute | solution.py:114
  18.8 7.1 %collective-permute-start.6 = (f32[16,1024]{1,0:T(8,128)S(1)}, f32[16,1024]{1,0:T(8,128)S(1)}, u32[]{:S(2)}, u32[]{:S(2)}) collective-permute-start(f32[16,1024]{1,0:T(8,128)S(1)} %slice_add_fusion.2), channel_id=1, source_target_pairs={{0,24},{2,18},{4,28},{6,22},{8,16},{10,26},{12,20},{14,30},{16,8},... | collective-permute-start | bytes 196616 | tf_op jit(solution)/shard_map/ppermute | solution.py:114
  24.0 11.4 %collective-permute-start.7 = (f32[64,1024]{1,0:T(8,128)S(1)}, f32[64,1024]{1,0:T(8,128)S(1)}, u32[]{:S(2)}, u32[]{:S(2)}) collective-permute-start(f32[64,1024]{1,0:T(8,128)S(1)} %get-tuple-element.39), channel_id=1, source_target_pairs={{0,4},{2,10},{4,0},{6,14},{8,12},{10,2},{12,8},{14,6},{16,20},{18,... | collective-permute-start | bytes 786440 | tf_op jit(solution)/shard_map/ppermute | solution.py:114
  25.7 6.6 %collective-permute-start.3 = (f32[64,1024]{1,0:T(8,128)S(1)}, f32[64,1024]{1,0:T(8,128)S(1)}, u32[]{:S(2)}, u32[]{:S(2)}) collective-permute-start(f32[64,1024]{1,0:T(8,128)S(1)} %get-tuple-element.35), channel_id=1, source_target_pairs={{0,8},{2,6},{4,12},{6,2},{8,0},{10,14},{12,4},{14,10},{16,24},{18,... | collective-permute-start | bytes 786440 | tf_op jit(solution)/shard_map/ppermute | solution.py:114
  26.9 13.6 %collective-permute-start.9 = (f32[64,1024]{1,0:T(8,128)S(1)}, f32[64,1024]{1,0:T(8,128)S(1)}, u32[]{:S(2)}, u32[]{:S(2)}) collective-permute-start(f32[64,1024]{1,0:T(8,128)S(1)} %get-tuple-element.44), channel_id=1, source_target_pairs={{0,8},{2,6},{4,12},{6,2},{8,0},{10,14},{12,4},{14,10},{16,24},{18,... | collective-permute-start | bytes 786440 | tf_op jit(solution)/shard_map/ppermute | solution.py:114
  32.3 8.2 %collective-permute-start.5 = (f32[32,1024]{1,0:T(8,128)S(1)}, f32[32,1024]{1,0:T(8,128)S(1)}, u32[]{:S(2)}, u32[]{:S(2)}) collective-permute-start(f32[32,1024]{1,0:T(8,128)S(1)} %get-tuple-element.37), channel_id=1, source_target_pairs={{0,24},{2,18},{4,28},{6,22},{8,16},{10,26},{12,20},{14,30},{16,8},... | collective-permute-start | bytes 393224 | tf_op jit(solution)/shard_map/ppermute | solution.py:114
  35.4 7.7 %collective-permute-start.11 = (f32[32,1024]{1,0:T(8,128)S(1)}, f32[32,1024]{1,0:T(8,128)S(1)}, u32[]{:S(2)}, u32[]{:S(2)}) collective-permute-start(f32[32,1024]{1,0:T(8,128)S(1)} %get-tuple-element.47), channel_id=1, source_target_pairs={{0,8},{2,6},{4,12},{6,2},{8,0},{10,14},{12,4},{14,10},{16,24},{18,... | collective-permute-start | bytes 393224 | tf_op jit(solution)/shard_map/ppermute | solution.py:114
  40.6 6.8 %collective-permute-start.10 = (f32[32,1024]{1,0:T(8,128)S(1)}, f32[32,1024]{1,0:T(8,128)S(1)}, u32[]{:S(2)}, u32[]{:S(2)}) collective-permute-start(f32[32,1024]{1,0:T(8,128)S(1)} %get-tuple-element.46), channel_id=1, source_target_pairs={{0,24},{2,18},{4,28},{6,22},{8,16},{10,26},{12,20},{14,30},{16,8},... | collective-permute-start | bytes 393224 | tf_op jit(solution)/shard_map/ppermute | solution.py:114
  43.1 0.7 %copy-start.3 = (s32[64,5]{0,1:T(8,128)S(1)}, s32[64,5]{0,1:T(8,128)}, u32[]{:S(2)}) copy-start(s32[64,5]{0,1:T(8,128)} %param.5) | copy-start | bytes 3844
  43.2 5.8 %collective-permute-start.12 = (f32[16,1024]{1,0:T(8,128)S(1)}, f32[16,1024]{1,0:T(8,128)S(1)}, u32[]{:S(2)}, u32[]{:S(2)}) collective-permute-start(f32[16,1024]{1,0:T(8,128)S(1)} %get-tuple-element.49), channel_id=1, source_target_pairs={{0,16},{2,18},{4,20},{6,22},{8,24},{10,26},{12,28},{14,30},{16,0},... | collective-permute-start | bytes 196616 | tf_op jit(solution)/shard_map/ppermute | solution.py:114
  43.8 6.5 %collective-permute-start.15 = (f32[48,1024]{1,0:T(8,128)S(1)}, f32[48,1024]{1,0:T(8,128)S(1)}, u32[]{:S(2)}, u32[]{:S(2)}) collective-permute-start(f32[48,1024]{1,0:T(8,128)S(1)} %finish.3.refs_0_.own_ref), channel_id=1, source_target_pairs={{0,1},{1,0},{2,3},{3,2},{4,5},{5,4},{6,7},{7,6},{8,9},{9,8},{10,11... | collective-permute-start | bytes 589832 | tf_op jit(solution)/shard_map/ppermute | solution.py:321
  47.4 5.0 %collective-permute-start.14 = (f32[32,1024]{1,0:T(8,128)S(1)}, f32[32,1024]{1,0:T(8,128)S(1)}, u32[]{:S(2)}, u32[]{:S(2)}) collective-permute-start(f32[32,1024]{1,0:T(8,128)S(1)} %finish.4.refs_0_.own_ref), channel_id=1, source_target_pairs={{0,1},{1,0},{2,3},{3,2},{4,5},{5,4},{6,7},{7,6},{8,9},{9,8},{10,11... | collective-permute-start | bytes 393224 | tf_op jit(solution)/shard_map/ppermute | solution.py:321
  49.0 4.3 %collective-permute-start.13 = (f32[16,1024]{1,0:T(8,128)S(1)}, f32[16,1024]{1,0:T(8,128)S(1)}, u32[]{:S(2)}, u32[]{:S(2)}) collective-permute-start(f32[16,1024]{1,0:T(8,128)S(1)} %finish.5.own_ref), channel_id=1, source_target_pairs={{0,1},{1,0},{2,3},{3,2},{4,5},{5,4},{6,7},{7,6},{8,9},{9,8},{10,11... | collective-permute-start | bytes 196616 | tf_op jit(solution)/shard_map/ppermute | solution.py:321
  53.4 1.2 %collective-permute-start.16 = (f32[8,128]{1,0:T(8,128)S(1)}, f32[8,128]{1,0:T(8,128)S(1)}, u32[]{:S(2)}, u32[]{:S(2)}) collective-permute-start(f32[8,128]{1,0:T(8,128)S(1)} %table.5), channel_id=1, source_target_pairs={{0,2},{2,0},{4,6},{6,4},{8,10},{10,8},{12,14},{14,12},{16,18},{18,... | collective-permute-start | bytes 12296 | tf_op jit(solution)/shard_map/ppermute | solution.py:114
  54.6 3.6 %collective-permute-start.17 = (f32[8,128]{1,0:T(8,128)S(1)}, f32[8,128]{1,0:T(8,128)S(1)}, u32[]{:S(2)}, u32[]{:S(2)}) collective-permute-start(f32[8,128]{1,0:T(8,128)S(1)} %add.183), channel_id=1, source_target_pairs={{0,8},{2,10},{4,12},{6,14},{8,0},{10,2},{12,4},{14,6},{16,24},{18,... | collective-permute-start | bytes 12296 | tf_op jit(solution)/shard_map/ppermute | solution.py:114
  58.2 3.6 %collective-permute-start.18 = (f32[8,128]{1,0:T(8,128)S(1)}, f32[8,128]{1,0:T(8,128)S(1)}, u32[]{:S(2)}, u32[]{:S(2)}) collective-permute-start(f32[8,128]{1,0:T(8,128)S(1)} %add.184), channel_id=1, source_target_pairs={{0,4},{2,6},{4,0},{6,2},{8,12},{10,14},{12,8},{14,10},{16,20},{18,... | collective-permute-start | bytes 12296 | tf_op jit(solution)/shard_map/ppermute | solution.py:114
  61.8 4.5 %collective-permute-start.19 = (f32[8,128]{1,0:T(8,128)S(1)}, f32[8,128]{1,0:T(8,128)S(1)}, u32[]{:S(2)}, u32[]{:S(2)}) collective-permute-start(f32[8,128]{1,0:T(8,128)S(1)} %add.185), channel_id=1, source_target_pairs={{0,16},{2,18},{4,20},{6,22},{8,24},{10,26},{12,28},{14,30},{16,0},... | collective-permute-start | bytes 12296 | tf_op jit(solution)/shard_map/ppermute | solution.py:114

commit v5 on v4

--- a/solution.py
+++ b/solution.py
@@ -289,11 +289,19 @@
         )
 
     theirs = other, *kernel_call(split_kernel, "split", [other], halves)
+    tile, one, two, phase = (diagrams[:, i] for i in range(4))
+    column = 4 * (tile % tiles_per)
+    same = one == two
+    where = jnp.stack([phase * tiles_per + tile // tiles_per, column + jnp.where(same, one, 2), column + 3])
+    sign = jnp.where(same, 0.0, jnp.where(one == 0, 1.0, -1.0))
+    scale = jnp.stack([jnp.ones_like(sign), sign]) / TILE
     keeps, flights, groups, tokens = {}, {}, {}, {}
     table = jnp.zeros((8, 128), jnp.float32)
     for event in PLAN:
         kind, which = event[:2]
         after = [tokens[e] for e in AFTER.get(event, ())]
+        if event == ("add", 1, 0):
+            after += [where, scale]
         if kind == "rows":
             send, keep = products(which, (mine, theirs), after)
             tokens[event] = keep
@@ -330,12 +338,6 @@
             )
     for bit in (CORE, Z_NEAR, Y, Z_FAR):
         table = table + swap(table, (bit, bit))
-    tile, one, two, phase = (diagrams[:, i] for i in range(4))
-    column = 4 * (tile % tiles_per)
-    same = one == two
-    where = jnp.stack([phase * tiles_per + tile // tiles_per, column + jnp.where(same, one, 2), column + 3])
-    sign = jnp.where(same, 0.0, jnp.where(one == 0, 1.0, -1.0))
-    scale = jnp.stack([jnp.ones_like(sign), sign]) / TILE
     (values,) = kernel_call(look_up_kernel, "look_up", [table, where, scale], [floats(2, diagrams.shape[0])])
     return (jnp.concatenate([groups[g] for g in GROUPS], axis=0)[None], values.T)
 

time: 67.2 us -> 67.9 us (1.010)
  waiting for transfers between devices: 27.3 us -> 28.7 us
  starting transfers between devices: 27.1 us -> 26.3 us
    ppermute x17, waiting for transfers between devices: 24.7 us -> 25.8 us  [swap(): lax.ppermute(array, 'space', [(i, i ^ masks[i % 2]) for i in range(count)])]
where the time goes in v5:
time: 67.9 us; the launch traced here: 67.7 us
  waiting for transfers between devices  28.7 us (42%)
  starting transfers between devices  26.3 us (39%)
  Pallas kernels  7.89 us (12%)
  local copies, waits for them, and re-layouts  2.79 us (4%)
  other arithmetic  1.14 us (2%)
  between operations  0.85 us (1%)
    ppermute x17, waiting for transfers between devices, swap(): lax.ppermute(array, 'space', [(i, i ^ masks[i % 2]) for i in range(count)])  25.8 us
    ppermute x17, starting transfers between devices, swap(): lax.ppermute(array, 'space', [(i, i ^ masks[i % 2]) for i in range(count)])  22.2 us
    pallas_call x19, Pallas kernels, kernel_call(): pl.pallas_call(body, out_shape=outs, in_specs=[VMEM_SPEC] * len(ins) + [A...  7.89 us
    ppermute x3, starting transfers between devices, halving(): flights[group] = lax.ppermute(done, 'cuts', [(0, 1), (1, 0)])  4.16 us
    ppermute x3, waiting for transfers between devices, halving(): flights[group] = lax.ppermute(done, 'cuts', [(0, 1), (1, 0)])  2.86 us
    unnamed x8, local copies, waits for them, and re-layouts  2.53 us
  transfers between devices with their start and end apart: 20, of which 14 were waited for; matrix products, arithmetic and copies ran while one was open for 2% of the time, Pallas kernels for 9%

profile of v5, /device:TPU:0, one launch (start us, length us, event | category | flops | bytes accessed | tf_op | source)
XLA Modules:
  0.0 67.7 jit_solution(4677737899588110615)
XLA Ops:
  0.6 0.5 collective-permute-start
  1.1 0.0 copy-start
  1.1 1.2 %copy-done = f32[1,2,512,256]{3,2,1,0:T(8,128)S(1)} copy-done((f32[1,2,512,256]{3,2,1,0:T(8,128)S(1)}, f32[1,2,512,256]{3,2,1,0:T(8,128)}, u32[]{:S(2)}) %copy-start) | copy-done | bytes 1048600
  2.4 0.0 copy-start.1
  2.4 0.2 split.2
  2.7 0.0 copy-start.3
  2.7 0.6 copy-done.3
  3.4 0.0 copy-start.2
  3.4 0.7 copy-done.2
  4.1 0.2 slice_reduce_fusion.2
  4.3 0.2 fusion.3
  4.5 0.0 collective-permute-done.value_ref.refs_3_
  4.5 0.2 split.3
  4.7 0.0 copy-done.1
  4.7 1.1 %rows.4 = (f32[64,1024]{1,0:T(8,128)S(1)}, f32[64,1024]{1,0:T(8,128)S(1)}) custom-call(f32[2,512,256]{2,1,0:T(8,128)S(1)} %bitcast.28, bf16[512,512]{1,0:T(8,128)(2,1)S(1)} %get-tuple-element.26.refs_1_, bf16[512,512]{1,0:T(8,128)(2,1)S(1)} %get-tuple-element.27.refs_2_, f32[2,512,256]{2,1,0:T(8,128)S(1)} %collective-permute-done.value_ref.refs_3_, ...), custom_call_target="tpu_custom_call" | custom-call | flops 805306368 | bytes 1048576 | tf_op jit(solution)/shard_map/rows/pallas_call | solution.py:248
  5.8 2.6 %collective-permute-start.2 = (f32[64,1024]{1,0:T(8,128)S(1)}, f32[64,1024]{1,0:T(8,128)S(1)}, u32[]{:S(2)}, u32[]{:S(2)}) collective-permute-start(f32[64,1024]{1,0:T(8,128)S(1)} %get-tuple-element.33), channel_id=1, source_target_pairs={{0,4},{2,10},{4,0},{6,14},{8,12},{10,2},{12,8},{14,6},{16,20},{18,... | collective-permute-start | bytes 786440 | tf_op jit(solution)/shard_map/ppermute | solution.py:114
  8.4 2.0 %rows.5 = (f32[128,1024]{1,0:T(8,128)S(1)}, f32[128,1024]{1,0:T(8,128)S(1)}) custom-call(f32[2,512,256]{2,1,0:T(8,128)S(1)} %bitcast.29, bf16[512,512]{1,0:T(8,128)(2,1)S(1)} %get-tuple-element.26.refs_1_, bf16[512,512]{1,0:T(8,128)(2,1)S(1)} %get-tuple-element.27.refs_2_, f32[2,512,256]{2,1,0:T(8,128)S(1)} %collective-permute-done.value_ref.refs_3_, ...), custom_call_target="tpu_custom_call" | custom-call | flops 1610612736 | bytes 1048576 | tf_op jit(solution)/shard_map/rows/pallas_call | solution.py:248
  10.4 0.1 collective-permute-start.1
  10.5 2.3 %collective-permute-done.2 = f32[64,1024]{1,0:T(8,128)S(1)} collective-permute-done((f32[64,1024]{1,0:T(8,128)S(1)}, f32[64,1024]{1,0:T(8,128)S(1)}, u32[]{:S(2)}, u32[]{:S(2)}) %collective-permute-start.2) | collective-permute-done | bytes 262176 | tf_op jit(solution)/shard_map/ppermute | solution.py:114
  12.8 2.1 %collective-permute-start.4 = (f32[32,1024]{1,0:T(8,128)S(1)}, f32[32,1024]{1,0:T(8,128)S(1)}, u32[]{:S(2)}, u32[]{:S(2)}) collective-permute-start(f32[32,1024]{1,0:T(8,128)S(1)} %get-tuple-element.64), channel_id=1, source_target_pairs={{0,8},{2,6},{4,12},{6,2},{8,0},{10,14},{12,4},{14,10},{16,24},{18,... | collective-permute-start | bytes 393224 | tf_op jit(solution)/shard_map/ppermute | solution.py:114
  14.9 2.0 %rows.7 = (f32[128,1024]{1,0:T(8,128)S(1)}, f32[128,1024]{1,0:T(8,128)S(1)}) custom-call(f32[2,512,256]{2,1,0:T(8,128)S(1)} %bitcast.30, bf16[512,512]{1,0:T(8,128)(2,1)S(1)} %get-tuple-element.26.refs_1_, bf16[512,512]{1,0:T(8,128)(2,1)S(1)} %get-tuple-element.27.refs_2_, f32[2,512,256]{2,1,0:T(8,128)S(1)} %collective-permute-done.value_ref.refs_3_, ...), custom_call_target="tpu_custom_call" | custom-call | flops 1610612736 | bytes 1048576 | tf_op jit(solution)/shard_map/rows/pallas_call | solution.py:248
  16.9 1.6 %collective-permute-start.8 = (f32[128,1024]{1,0:T(8,128)S(1)}, f32[128,1024]{1,0:T(8,128)S(1)}, u32[]{:S(2)}, u32[]{:S(2)}) collective-permute-start(f32[128,1024]{1,0:T(8,128)S(1)} %get-tuple-element.41), channel_id=1, source_target_pairs={{0,4},{2,10},{4,0},{6,14},{8,12},{10,2},{12,8},{14,6},{16,20},{18,... | collective-permute-start | bytes 1572872 | tf_op jit(solution)/shard_map/ppermute | solution.py:114
  18.5 0.8 %collective-permute-done.4 = f32[32,1024]{1,0:T(8,128)S(1)} collective-permute-done((f32[32,1024]{1,0:T(8,128)S(1)}, f32[32,1024]{1,0:T(8,128)S(1)}, u32[]{:S(2)}, u32[]{:S(2)}) %collective-permute-start.4) | collective-permute-done | bytes 131104 | tf_op jit(solution)/shard_map/ppermute | solution.py:114
  19.3 4.1 %collective-permute-start.6 = (f32[16,1024]{1,0:T(8,128)S(1)}, f32[16,1024]{1,0:T(8,128)S(1)}, u32[]{:S(2)}, u32[]{:S(2)}) collective-permute-start(f32[16,1024]{1,0:T(8,128)S(1)} %slice_add_fusion.2), channel_id=1, source_target_pairs={{0,24},{2,18},{4,28},{6,22},{8,16},{10,26},{12,20},{14,30},{16,8},... | collective-permute-start | bytes 196616 | tf_op jit(solution)/shard_map/ppermute | solution.py:114
  23.4 1.1 %rows.6 = (f32[64,1024]{1,0:T(8,128)S(1)}, f32[64,1024]{1,0:T(8,128)S(1)}) custom-call(f32[2,512,256]{2,1,0:T(8,128)S(1)} %bitcast.31, bf16[512,512]{1,0:T(8,128)(2,1)S(1)} %get-tuple-element.26.refs_1_, bf16[512,512]{1,0:T(8,128)(2,1)S(1)} %get-tuple-element.27.refs_2_, f32[2,512,256]{2,1,0:T(8,128)S(1)} %collective-permute-done.value_ref.refs_3_, ...), custom_call_target="tpu_custom_call" | custom-call | flops 805306368 | bytes 1048576 | tf_op jit(solution)/shard_map/rows/pallas_call | solution.py:248
  24.5 1.6 %collective-permute-start.7 = (f32[64,1024]{1,0:T(8,128)S(1)}, f32[64,1024]{1,0:T(8,128)S(1)}, u32[]{:S(2)}, u32[]{:S(2)}) collective-permute-start(f32[64,1024]{1,0:T(8,128)S(1)} %get-tuple-element.39), channel_id=1, source_target_pairs={{0,4},{2,10},{4,0},{6,14},{8,12},{10,2},{12,8},{14,6},{16,20},{18,... | collective-permute-start | bytes 786440 | tf_op jit(solution)/shard_map/ppermute | solution.py:114
  26.1 0.0 collective-permute-done.1.came_ref
  26.1 0.1 halve.6
  26.2 0.1 collective-permute-start.3
  26.2 0.2 collective-permute-done.6
  26.5 0.7 %collective-permute-done.8.came_ref = f32[128,1024]{1,0:T(8,128)S(1)} collective-permute-done((f32[128,1024]{1,0:T(8,128)S(1)}, f32[128,1024]{1,0:T(8,128)S(1)}, u32[]{:S(2)}, u32[]{:S(2)}) %collective-permute-start.8) | collective-permute-done | bytes 524320 | tf_op jit(solution)/shard_map/ppermute | solution.py:114
  27.1 0.1 halve.8
  27.2 2.8 %collective-permute-start.9 = (f32[64,1024]{1,0:T(8,128)S(1)}, f32[64,1024]{1,0:T(8,128)S(1)}, u32[]{:S(2)}, u32[]{:S(2)}) collective-permute-start(f32[64,1024]{1,0:T(8,128)S(1)} %get-tuple-element.44), channel_id=1, source_target_pairs={{0,8},{2,6},{4,12},{6,2},{8,0},{10,14},{12,4},{14,10},{16,24},{18,... | collective-permute-start | bytes 786440 | tf_op jit(solution)/shard_map/ppermute | solution.py:114
  30.0 3.0 %collective-permute-done.3.came_ref = f32[64,1024]{1,0:T(8,128)S(1)} collective-permute-done((f32[64,1024]{1,0:T(8,128)S(1)}, f32[64,1024]{1,0:T(8,128)S(1)}, u32[]{:S(2)}, u32[]{:S(2)}) %collective-permute-start.3) | collective-permute-done | bytes 262176 | tf_op jit(solution)/shard_map/ppermute | solution.py:114
  33.0 2.9 %collective-permute-start.5 = (f32[32,1024]{1,0:T(8,128)S(1)}, f32[32,1024]{1,0:T(8,128)S(1)}, u32[]{:S(2)}, u32[]{:S(2)}) collective-permute-start(f32[32,1024]{1,0:T(8,128)S(1)} %get-tuple-element.37), channel_id=1, source_target_pairs={{0,24},{2,18},{4,28},{6,22},{8,16},{10,26},{12,20},{14,30},{16,8},... | collective-permute-start | bytes 393224 | tf_op jit(solution)/shard_map/ppermute | solution.py:114
  35.9 0.0 collective-permute-done.7.came_ref
  36.0 0.1 collective-permute-start.11
  36.0 4.9 %collective-permute-done.5.came_ref = f32[32,1024]{1,0:T(8,128)S(1)} collective-permute-done((f32[32,1024]{1,0:T(8,128)S(1)}, f32[32,1024]{1,0:T(8,128)S(1)}, u32[]{:S(2)}, u32[]{:S(2)}) %collective-permute-start.5) | collective-permute-done | bytes 131104 | tf_op jit(solution)/shard_map/ppermute | solution.py:114
  41.0 0.0 collective-permute-done.9.came_ref
  41.0 1.9 %collective-permute-start.10 = (f32[32,1024]{1,0:T(8,128)S(1)}, f32[32,1024]{1,0:T(8,128)S(1)}, u32[]{:S(2)}, u32[]{:S(2)}) collective-permute-start(f32[32,1024]{1,0:T(8,128)S(1)} %get-tuple-element.46), channel_id=1, source_target_pairs={{0,24},{2,18},{4,28},{6,22},{8,16},{10,26},{12,20},{14,30},{16,8},... | collective-permute-start | bytes 393224 | tf_op jit(solution)/shard_map/ppermute | solution.py:114
  42.9 1.5 %collective-permute-start.15 = (f32[48,1024]{1,0:T(8,128)S(1)}, f32[48,1024]{1,0:T(8,128)S(1)}, u32[]{:S(2)}, u32[]{:S(2)}) collective-permute-start(f32[48,1024]{1,0:T(8,128)S(1)} %finish.3.refs_0_.own_ref), channel_id=1, source_target_pairs={{0,1},{1,0},{2,3},{3,2},{4,5},{5,4},{6,7},{7,6},{8,9},{9,8},{10,11... | collective-permute-start | bytes 589832 | tf_op jit(solution)/shard_map/ppermute | solution.py:329
  44.4 0.0 collective-permute-done.11.came_ref
  44.4 0.1 collective-permute-start.12
  44.5 3.3 %collective-permute-done.10.came_ref = f32[32,1024]{1,0:T(8,128)S(1)} collective-permute-done((f32[32,1024]{1,0:T(8,128)S(1)}, f32[32,1024]{1,0:T(8,128)S(1)}, u32[]{:S(2)}, u32[]{:S(2)}) %collective-permute-start.10) | collective-permute-done | bytes 131104 | tf_op jit(solution)/shard_map/ppermute | solution.py:114
  47.9 1.6 %collective-permute-start.14 = (f32[32,1024]{1,0:T(8,128)S(1)}, f32[32,1024]{1,0:T(8,128)S(1)}, u32[]{:S(2)}, u32[]{:S(2)}) collective-permute-start(f32[32,1024]{1,0:T(8,128)S(1)} %finish.4.refs_0_.own_ref), channel_id=1, source_target_pairs={{0,1},{1,0},{2,3},{3,2},{4,5},{5,4},{6,7},{7,6},{8,9},{9,8},{10,11... | collective-permute-start | bytes 393224 | tf_op jit(solution)/shard_map/ppermute | solution.py:329
  49.4 0.3 collective-permute-done.12.came_ref
  49.7 1.1 %collective-permute-start.13 = (f32[16,1024]{1,0:T(8,128)S(1)}, f32[16,1024]{1,0:T(8,128)S(1)}, u32[]{:S(2)}, u32[]{:S(2)}) collective-permute-start(f32[16,1024]{1,0:T(8,128)S(1)} %finish.5.own_ref), channel_id=1, source_target_pairs={{0,1},{1,0},{2,3},{3,2},{4,5},{5,4},{6,7},{7,6},{8,9},{9,8},{10,11... | collective-permute-start | bytes 196616 | tf_op jit(solution)/shard_map/ppermute | solution.py:329
  50.8 0.0 collective-permute-done.15.other_ref
  50.8 0.2 table.3.before_ref
  51.0 1.9 %collective-permute-done.14.other_ref = f32[32,1024]{1,0:T(8,128)S(1)} collective-permute-done((f32[32,1024]{1,0:T(8,128)S(1)}, f32[32,1024]{1,0:T(8,128)S(1)}, u32[]{:S(2)}, u32[]{:S(2)}) %collective-permute-start.14) | collective-permute-done | bytes 131104 | tf_op jit(solution)/shard_map/ppermute | solution.py:329
  52.9 0.2 table.4.before_ref
  53.0 1.0 %collective-permute-done.13.other_ref = f32[16,1024]{1,0:T(8,128)S(1)} collective-permute-done((f32[16,1024]{1,0:T(8,128)S(1)}, f32[16,1024]{1,0:T(8,128)S(1)}, u32[]{:S(2)}, u32[]{:S(2)}) %collective-permute-start.13) | collective-permute-done | bytes 65568 | tf_op jit(solution)/shard_map/ppermute | solution.py:329
  54.0 0.1 table.5
  54.1 0.0 collective-permute-start.16
  54.1 1.2 %collective-permute-done.16 = f32[8,128]{1,0:T(8,128)S(1)} collective-permute-done((f32[8,128]{1,0:T(8,128)S(1)}, f32[8,128]{1,0:T(8,128)S(1)}, u32[]{:S(2)}, u32[]{:S(2)}) %collective-permute-start.16) | collective-permute-done | bytes 4128 | tf_op jit(solution)/shard_map/ppermute | solution.py:114
  55.3 0.0 collective-permute-start.17
  55.3 3.6 %collective-permute-done.17 = f32[8,128]{1,0:T(8,128)S(1)} collective-permute-done((f32[8,128]{1,0:T(8,128)S(1)}, f32[8,128]{1,0:T(8,128)S(1)}, u32[]{:S(2)}, u32[]{:S(2)}) %collective-permute-start.17) | collective-permute-done | bytes 4128 | tf_op jit(solution)/shard_map/ppermute | solution.py:114
  58.9 1.1 %collective-permute-start.18 = (f32[8,128]{1,0:T(8,128)S(1)}, f32[8,128]{1,0:T(8,128)S(1)}, u32[]{:S(2)}, u32[]{:S(2)}) collective-permute-start(f32[8,128]{1,0:T(8,128)S(1)} %add.189), channel_id=1, source_target_pairs={{0,4},{2,6},{4,0},{6,2},{8,12},{10,14},{12,8},{14,10},{16,20},{18,... | collective-permute-start | bytes 12296 | tf_op jit(solution)/shard_map/ppermute | solution.py:114
  60.0 2.5 %collective-permute-done.18 = f32[8,128]{1,0:T(8,128)S(1)} collective-permute-done((f32[8,128]{1,0:T(8,128)S(1)}, f32[8,128]{1,0:T(8,128)S(1)}, u32[]{:S(2)}, u32[]{:S(2)}) %collective-permute-start.18) | collective-permute-done | bytes 4128 | tf_op jit(solution)/shard_map/ppermute | solution.py:114
  62.5 0.6 collective-permute-start.19
  63.1 0.8 %maximum_bitcast_fusion = f32[1,96,1024]{2,1,0:T(8,128)} fusion(f32[16,1024]{1,0:T(8,128)S(1)} %finish.5.own_ref, f32[32,1024]{1,0:T(8,128)S(1)} %finish.4.refs_0_.own_ref, f32[48,1024]{1,0:T(8,128)S(1)} %finish.3.refs_0_.own_ref), kind=kLoop, calls=%fused_computation | loop fusion | flops 196608 | bytes 786432 | tf_op jit(solution)/shard_map/broadcast_in_dim | solution.py:342
  63.9 3.1 %collective-permute-done.19 = f32[8,128]{1,0:T(8,128)S(1)} collective-permute-done((f32[8,128]{1,0:T(8,128)S(1)}, f32[8,128]{1,0:T(8,128)S(1)}, u32[]{:S(2)}, u32[]{:S(2)}) %collective-permute-start.19) | collective-permute-done | bytes 4128 | tf_op jit(solution)/shard_map/ppermute | solution.py:114
  67.0 0.7 look_up.1
  (29 shorter events, 0.4 us)
Async XLA Ops:
  0.6 3.9 %collective-permute-start = (f32[2,512,256]{2,1,0:T(8,128)}, f32[2,512,256]{2,1,0:T(8,128)S(1)}, u32[]{:S(2)}, u32[]{:S(2)}) collective-permute-start(f32[2,512,256]{2,1,0:T(8,128)} %bitcast.26), channel_id=1, source_target_pairs={{0,2},{2,0},{4,6},{6,4},{8,10},{10,8},{12,14},{14,12},{16,18},{18,... | collective-permute-start | bytes 3145736 | tf_op jit(solution)/shard_map/ppermute | solution.py:114
  1.1 1.2 %copy-start = (f32[1,2,512,256]{3,2,1,0:T(8,128)S(1)}, f32[1,2,512,256]{3,2,1,0:T(8,128)}, u32[]{:S(2)}) copy-start(f32[1,2,512,256]{3,2,1,0:T(8,128)} %param.3) | copy-start | bytes 3145732
  2.4 2.3 %copy-start.1 = (f32[1,2,512,256]{3,2,1,0:T(8,128)S(1)}, f32[1,2,512,256]{3,2,1,0:T(8,128)}, u32[]{:S(2)}) copy-start(f32[1,2,512,256]{3,2,1,0:T(8,128)} %param.3) | copy-start | bytes 3145732
  2.7 0.7 %copy-start.3 = (s32[64,5]{0,1:T(8,128)S(1)}, s32[64,5]{0,1:T(8,128)}, u32[]{:S(2)}) copy-start(s32[64,5]{0,1:T(8,128)} %param.5) | copy-start | bytes 3844
  3.4 0.7 %copy-start.2 = (s32[3,3]{1,0:T(4,128)S(1)}, s32[3,3]{1,0:T(4,128)}, u32[]{:S(2)}) copy-start(s32[3,3]{1,0:T(4,128)} %param.4) | copy-start | bytes 112
  5.8 6.9 %collective-permute-start.2 = (f32[64,1024]{1,0:T(8,128)S(1)}, f32[64,1024]{1,0:T(8,128)S(1)}, u32[]{:S(2)}, u32[]{:S(2)}) collective-permute-start(f32[64,1024]{1,0:T(8,128)S(1)} %get-tuple-element.33), channel_id=1, source_target_pairs={{0,4},{2,10},{4,0},{6,14},{8,12},{10,2},{12,8},{14,6},{16,20},{18,... | collective-permute-start | bytes 786440 | tf_op jit(solution)/shard_map/ppermute | solution.py:114
  10.4 15.7 %collective-permute-start.1 = (f32[128,1024]{1,0:T(8,128)S(1)}, f32[128,1024]{1,0:T(8,128)S(1)}, u32[]{:S(2)}, u32[]{:S(2)}) collective-permute-start(f32[128,1024]{1,0:T(8,128)S(1)} %get-tuple-element.32), channel_id=1, source_target_pairs={{0,4},{2,10},{4,0},{6,14},{8,12},{10,2},{12,8},{14,6},{16,20},{18,... | collective-permute-start | bytes 1572872 | tf_op jit(solution)/shard_map/ppermute | solution.py:114
  12.8 6.6 %collective-permute-start.4 = (f32[32,1024]{1,0:T(8,128)S(1)}, f32[32,1024]{1,0:T(8,128)S(1)}, u32[]{:S(2)}, u32[]{:S(2)}) collective-permute-start(f32[32,1024]{1,0:T(8,128)S(1)} %get-tuple-element.64), channel_id=1, source_target_pairs={{0,8},{2,6},{4,12},{6,2},{8,0},{10,14},{12,4},{14,10},{16,24},{18,... | collective-permute-start | bytes 393224 | tf_op jit(solution)/shard_map/ppermute | solution.py:114
  16.9 10.2 %collective-permute-start.8 = (f32[128,1024]{1,0:T(8,128)S(1)}, f32[128,1024]{1,0:T(8,128)S(1)}, u32[]{:S(2)}, u32[]{:S(2)}) collective-permute-start(f32[128,1024]{1,0:T(8,128)S(1)} %get-tuple-element.41), channel_id=1, source_target_pairs={{0,4},{2,10},{4,0},{6,14},{8,12},{10,2},{12,8},{14,6},{16,20},{18,... | collective-permute-start | bytes 1572872 | tf_op jit(solution)/shard_map/ppermute | solution.py:114
  19.3 7.1 %collective-permute-start.6 = (f32[16,1024]{1,0:T(8,128)S(1)}, f32[16,1024]{1,0:T(8,128)S(1)}, u32[]{:S(2)}, u32[]{:S(2)}) collective-permute-start(f32[16,1024]{1,0:T(8,128)S(1)} %slice_add_fusion.2), channel_id=1, source_target_pairs={{0,24},{2,18},{4,28},{6,22},{8,16},{10,26},{12,20},{14,30},{16,8},... | collective-permute-start | bytes 196616 | tf_op jit(solution)/shard_map/ppermute | solution.py:114
  24.5 11.4 %collective-permute-start.7 = (f32[64,1024]{1,0:T(8,128)S(1)}, f32[64,1024]{1,0:T(8,128)S(1)}, u32[]{:S(2)}, u32[]{:S(2)}) collective-permute-start(f32[64,1024]{1,0:T(8,128)S(1)} %get-tuple-element.39), channel_id=1, source_target_pairs={{0,4},{2,10},{4,0},{6,14},{8,12},{10,2},{12,8},{14,6},{16,20},{18,... | collective-permute-start | bytes 786440 | tf_op jit(solution)/shard_map/ppermute | solution.py:114
  26.2 6.8 %collective-permute-start.3 = (f32[64,1024]{1,0:T(8,128)S(1)}, f32[64,1024]{1,0:T(8,128)S(1)}, u32[]{:S(2)}, u32[]{:S(2)}) collective-permute-start(f32[64,1024]{1,0:T(8,128)S(1)} %get-tuple-element.35), channel_id=1, source_target_pairs={{0,8},{2,6},{4,12},{6,2},{8,0},{10,14},{12,4},{14,10},{16,24},{18,... | collective-permute-start | bytes 786440 | tf_op jit(solution)/shard_map/ppermute | solution.py:114
  27.2 13.7 %collective-permute-start.9 = (f32[64,1024]{1,0:T(8,128)S(1)}, f32[64,1024]{1,0:T(8,128)S(1)}, u32[]{:S(2)}, u32[]{:S(2)}) collective-permute-start(f32[64,1024]{1,0:T(8,128)S(1)} %get-tuple-element.44), channel_id=1, source_target_pairs={{0,8},{2,6},{4,12},{6,2},{8,0},{10,14},{12,4},{14,10},{16,24},{18,... | collective-permute-start | bytes 786440 | tf_op jit(solution)/shard_map/ppermute | solution.py:114
  33.0 7.9 %collective-permute-start.5 = (f32[32,1024]{1,0:T(8,128)S(1)}, f32[32,1024]{1,0:T(8,128)S(1)}, u32[]{:S(2)}, u32[]{:S(2)}) collective-permute-start(f32[32,1024]{1,0:T(8,128)S(1)} %get-tuple-element.37), channel_id=1, source_target_pairs={{0,24},{2,18},{4,28},{6,22},{8,16},{10,26},{12,20},{14,30},{16,8},... | collective-permute-start | bytes 393224 | tf_op jit(solution)/shard_map/ppermute | solution.py:114
  36.0 8.5 %collective-permute-start.11 = (f32[32,1024]{1,0:T(8,128)S(1)}, f32[32,1024]{1,0:T(8,128)S(1)}, u32[]{:S(2)}, u32[]{:S(2)}) collective-permute-start(f32[32,1024]{1,0:T(8,128)S(1)} %get-tuple-element.47), channel_id=1, source_target_pairs={{0,8},{2,6},{4,12},{6,2},{8,0},{10,14},{12,4},{14,10},{16,24},{18,... | collective-permute-start | bytes 393224 | tf_op jit(solution)/shard_map/ppermute | solution.py:114
  41.0 6.8 %collective-permute-start.10 = (f32[32,1024]{1,0:T(8,128)S(1)}, f32[32,1024]{1,0:T(8,128)S(1)}, u32[]{:S(2)}, u32[]{:S(2)}) collective-permute-start(f32[32,1024]{1,0:T(8,128)S(1)} %get-tuple-element.46), channel_id=1, source_target_pairs={{0,24},{2,18},{4,28},{6,22},{8,16},{10,26},{12,20},{14,30},{16,8},... | collective-permute-start | bytes 393224 | tf_op jit(solution)/shard_map/ppermute | solution.py:114
  42.9 7.9 %collective-permute-start.15 = (f32[48,1024]{1,0:T(8,128)S(1)}, f32[48,1024]{1,0:T(8,128)S(1)}, u32[]{:S(2)}, u32[]{:S(2)}) collective-permute-start(f32[48,1024]{1,0:T(8,128)S(1)} %finish.3.refs_0_.own_ref), channel_id=1, source_target_pairs={{0,1},{1,0},{2,3},{3,2},{4,5},{5,4},{6,7},{7,6},{8,9},{9,8},{10,11... | collective-permute-start | bytes 589832 | tf_op jit(solution)/shard_map/ppermute | solution.py:329
  44.4 5.2 %collective-permute-start.12 = (f32[16,1024]{1,0:T(8,128)S(1)}, f32[16,1024]{1,0:T(8,128)S(1)}, u32[]{:S(2)}, u32[]{:S(2)}) collective-permute-start(f32[16,1024]{1,0:T(8,128)S(1)} %get-tuple-element.49), channel_id=1, source_target_pairs={{0,16},{2,18},{4,20},{6,22},{8,24},{10,26},{12,28},{14,30},{16,0},... | collective-permute-start | bytes 196616 | tf_op jit(solution)/shard_map/ppermute | solution.py:114
  47.9 5.0 %collective-permute-start.14 = (f32[32,1024]{1,0:T(8,128)S(1)}, f32[32,1024]{1,0:T(8,128)S(1)}, u32[]{:S(2)}, u32[]{:S(2)}) collective-permute-start(f32[32,1024]{1,0:T(8,128)S(1)} %finish.4.refs_0_.own_ref), channel_id=1, source_target_pairs={{0,1},{1,0},{2,3},{3,2},{4,5},{5,4},{6,7},{7,6},{8,9},{9,8},{10,11... | collective-permute-start | bytes 393224 | tf_op jit(solution)/shard_map/ppermute | solution.py:329
  49.7 4.3 %collective-permute-start.13 = (f32[16,1024]{1,0:T(8,128)S(1)}, f32[16,1024]{1,0:T(8,128)S(1)}, u32[]{:S(2)}, u32[]{:S(2)}) collective-permute-start(f32[16,1024]{1,0:T(8,128)S(1)} %finish.5.own_ref), channel_id=1, source_target_pairs={{0,1},{1,0},{2,3},{3,2},{4,5},{5,4},{6,7},{7,6},{8,9},{9,8},{10,11... | collective-permute-start | bytes 196616 | tf_op jit(solution)/shard_map/ppermute | solution.py:329
  54.1 1.2 %collective-permute-start.16 = (f32[8,128]{1,0:T(8,128)S(1)}, f32[8,128]{1,0:T(8,128)S(1)}, u32[]{:S(2)}, u32[]{:S(2)}) collective-permute-start(f32[8,128]{1,0:T(8,128)S(1)} %table.5), channel_id=1, source_target_pairs={{0,2},{2,0},{4,6},{6,4},{8,10},{10,8},{12,14},{14,12},{16,18},{18,... | collective-permute-start | bytes 12296 | tf_op jit(solution)/shard_map/ppermute | solution.py:114
  55.3 3.6 %collective-permute-start.17 = (f32[8,128]{1,0:T(8,128)S(1)}, f32[8,128]{1,0:T(8,128)S(1)}, u32[]{:S(2)}, u32[]{:S(2)}) collective-permute-start(f32[8,128]{1,0:T(8,128)S(1)} %add.188), channel_id=1, source_target_pairs={{0,8},{2,10},{4,12},{6,14},{8,0},{10,2},{12,4},{14,6},{16,24},{18,... | collective-permute-start | bytes 12296 | tf_op jit(solution)/shard_map/ppermute | solution.py:114
  58.9 3.6 %collective-permute-start.18 = (f32[8,128]{1,0:T(8,128)S(1)}, f32[8,128]{1,0:T(8,128)S(1)}, u32[]{:S(2)}, u32[]{:S(2)}) collective-permute-start(f32[8,128]{1,0:T(8,128)S(1)} %add.189), channel_id=1, source_target_pairs={{0,4},{2,6},{4,0},{6,2},{8,12},{10,14},{12,8},{14,10},{16,20},{18,... | collective-permute-start | bytes 12296 | tf_op jit(solution)/shard_map/ppermute | solution.py:114
  62.5 4.5 %collective-permute-start.19 = (f32[8,128]{1,0:T(8,128)S(1)}, f32[8,128]{1,0:T(8,128)S(1)}, u32[]{:S(2)}, u32[]{:S(2)}) collective-permute-start(f32[8,128]{1,0:T(8,128)S(1)} %add.190), channel_id=1, source_target_pairs={{0,16},{2,18},{4,20},{6,22},{8,24},{10,26},{12,28},{14,30},{16,0},... | collective-permute-start | bytes 12296 | tf_op jit(solution)/shard_map/ppermute | solution.py:114
